TPU v7x, 32 devices: a whole 2x2x4 slice. The times are simulated.
32 devices in a mesh: groups: 2 (over y), domain: 4 (over z), shot: 4 (over x, core).
Axes of the slice: x: 2, y: 2, z: 4, core: 2. Of those that a mesh axis runs over, the one named last changes fastest.
Arguments:
- velocity: float32 [16, 384, 128], P(('groups', 'domain'), 'shot'), parts along dimension 0, may hold values from 0.04 to 0.12
- thomsen_eps: float32 [16, 384, 128], P(('groups', 'domain'), 'shot'), parts along dimension 0, may hold values from 0.1 to 0.4
- thomsen_delta: float32 [16, 384, 128], P(('groups', 'domain'), 'shot'), parts along dimension 0, may hold values from 0 to 0.2
- tilt_angle: float32 [16, 384, 128], P(('groups', 'domain'), 'shot'), parts along dimension 0, may hold values from -1.2 to 1.2
- azimuth: float32 [16, 384, 128], P(('groups', 'domain'), 'shot'), parts along dimension 0, may hold values from -3.140625 to 3.140625
- shot_anchor: int32 [8], P(('groups', 'shot')), parts along dimension 0, may hold values from 0 to 192
- source_x: int32 [8], P(('groups', 'shot')), parts along dimension 0, may hold values from 0 to 7
- source_y: int32 [8], P(('groups', 'shot')), parts along dimension 0, may hold values from 0 to 191
- wavelet: float32 [8, 8], P(('groups', 'shot')), parts along dimension 0, may hold values from -64 to 64
- receiver_x: int32 [8, 256], P(('groups', 'shot')), parts along dimension 0, may hold values from 0 to 7
- receiver_y: int32 [8, 256], P(('groups', 'shot')), parts along dimension 0, may hold values from 0 to 191
- traces: float32 [8, 8, 256], P(('groups', 'shot')), parts along dimension 0, may hold values from -48 to 48
- source_now: float32 [8, 2, 8, 192, 128], P(('groups', 'shot'), None, 'domain'), parts along dimension 0, may hold values from -6 to 6
- source_before: float32 [8, 2, 8, 192, 128], P(('groups', 'shot'), None, 'domain'), parts along dimension 0, may hold values from -6 to 6
- receiver_now: float32 [8, 2, 8, 192, 128], P(('groups', 'shot'), None, 'domain'), parts along dimension 0, may hold values from -6 to 6
- receiver_before: float32 [8, 2, 8, 192, 128], P(('groups', 'shot'), None, 'domain'), parts along dimension 0, may hold values from -6 to 6
- slab_owner: int32 [8], P('groups'), parts along dimension 0, may hold values from 0 to 3, each once
Outputs:
- image: float32 [16, 384, 128], P(('groups', 'domain'), 'shot'), parts along dimension 0
There are 2 independent parts, one for each index of `groups`. A program takes and returns all parts, laid end to end along the dimension named above; each array names one. Nothing has to cross between parts.
Inputs may be any that keep to these rules, and one draw needn't show every extreme that they name: `receiver_y`: receivers may share a cell. `slab_owner`: each slab index appears once.
All inputs are finite; a program needn't handle non-finite values.
Results may differ from a plain program's by a relative error of at most 0.0003.
Values sent between devices are 32-bit elements; how exact they have to be, the bound alone decides.
No kernel may reach another device: no remote copies, remote signals or barrier semaphores. Data moves between devices by JAX's collectives and lax.ppermute only.
A program may use at most 64 MiB of HBM per device.

v0:
```python
import jax
import jax.numpy as jnp
from jax import lax
from jax.sharding import PartitionSpec as P

SRC_Z = 3
REC_Z = 1


def padded_2(block, sides, width):
    for axis, dim in sides:
        count = lax.axis_size(axis)
        forward = [(i, i + 1) for i in range(count - 1)]
        backward = [(target, source) for source, target in forward]
        low = lax.ppermute(
            lax.slice_in_dim(block, block.shape[dim] - width, None, axis=dim), axis, forward
        )
        high = lax.ppermute(lax.slice_in_dim(block, 0, width, axis=dim), axis, backward)
        block = jnp.concatenate([low, block, high], axis=dim)
    return block


def coefficients(velocity, thomsen_eps, thomsen_delta, tilt_angle, azimuth):
    gain_eps = 1.0 + 2.0 * thomsen_eps
    gain_delta = jnp.sqrt(1.0 + 2.0 * thomsen_delta)
    axis_x = jnp.sin(tilt_angle) * jnp.cos(azimuth)
    axis_y = jnp.sin(tilt_angle) * jnp.sin(azimuth)
    axis_z = jnp.cos(tilt_angle)
    return (velocity, gain_eps, gain_delta, axis_x, axis_y, axis_z)


def second_derivs(padded):
    middle = padded[1:-1, 1:-1, 1:-1]
    second_xx = padded[2:, 1:-1, 1:-1] - 2.0 * middle + padded[:-2, 1:-1, 1:-1]
    second_yy = padded[1:-1, 2:, 1:-1] - 2.0 * middle + padded[1:-1, :-2, 1:-1]
    second_zz = padded[1:-1, 1:-1, 2:] - 2.0 * middle + padded[1:-1, 1:-1, :-2]
    mixed_xy = 0.25 * (
        padded[2:, 2:, 1:-1]
        - padded[2:, :-2, 1:-1]
        - padded[:-2, 2:, 1:-1]
        + padded[:-2, :-2, 1:-1]
    )
    mixed_xz = 0.25 * (
        padded[2:, 1:-1, 2:]
        - padded[2:, 1:-1, :-2]
        - padded[:-2, 1:-1, 2:]
        + padded[:-2, 1:-1, :-2]
    )
    mixed_yz = 0.25 * (
        padded[1:-1, 2:, 2:]
        - padded[1:-1, 2:, :-2]
        - padded[1:-1, :-2, 2:]
        + padded[1:-1, :-2, :-2]
    )
    return (second_xx, second_yy, second_zz, mixed_xy, mixed_xz, mixed_yz)


def along_axis(derivs, axis_x, axis_y, axis_z):
    second_xx, second_yy, second_zz, mixed_xy, mixed_xz, mixed_yz = derivs
    pure = axis_x * axis_x * second_xx + axis_y * axis_y * second_yy + axis_z * axis_z * second_zz
    return pure + 2.0 * (
        axis_x * axis_y * mixed_xy + axis_x * axis_z * mixed_xz + axis_y * axis_z * mixed_yz
    )


def wave_update(padded, previous, local_coefs):
    courant, gain_eps, gain_delta, axis_x, axis_y, axis_z = local_coefs
    results = []
    for field in (0, 2):
        derivs_p = second_derivs(padded[field])
        derivs_q = second_derivs(padded[field + 1])
        axial_p = along_axis(derivs_p, axis_x, axis_y, axis_z)
        across_p = derivs_p[0] + derivs_p[1] + derivs_p[2] - axial_p
        axial_q = along_axis(derivs_q, axis_x, axis_y, axis_z)
        cur_p = padded[field][1:-1, 1:-1, 1:-1]
        cur_q = padded[field + 1][1:-1, 1:-1, 1:-1]
        new_p = (
            2.0 * cur_p - previous[field] + courant * (gain_eps * across_p + gain_delta * axial_q)
        )
        new_q = 2.0 * cur_q - previous[field + 1] + courant * (gain_delta * across_p + axial_q)
        results.append(new_p)
        results.append(new_q)
    return jnp.stack(results)


def inject(updated, courant, source_plane, receiver_plane):
    updated = updated.at[0:2, :, :, SRC_Z].add(courant[None, :, :, SRC_Z] * source_plane[None])
    updated = updated.at[2:4, :, :, REC_Z].add(courant[None, :, :, REC_Z] * receiver_plane[None])
    return updated


def per_device(
    velocity,
    thomsen_eps,
    thomsen_delta,
    tilt_angle,
    azimuth,
    shot_anchor,
    source_x,
    source_y,
    wavelet,
    receiver_x,
    receiver_y,
    traces,
    source_now,
    source_before,
    receiver_now,
    receiver_before,
    slab_owner,
):
    row_count = source_now.shape[2]
    y_count = source_now.shape[3]
    z_count = source_now.shape[4]
    step_count = wavelet.shape[1]
    shot_count = slab_owner.shape[0]
    anchor = shot_anchor[0]
    model_share = jnp.stack([velocity, thomsen_eps, thomsen_delta, tilt_angle, azimuth])
    whole_model = lax.all_gather(model_share, "shot", axis=2, tiled=True)
    window = lax.dynamic_slice_in_dim(whole_model, anchor, y_count, 2)
    all_coefs = coefficients(window[0], window[1], window[2], window[3], window[4])
    first_row = lax.axis_index("domain") * row_count
    lane_ids = jnp.arange(y_count)
    wave_row = wavelet[0]
    src_x = source_x[0]
    src_y = source_y[0]
    rec_x = receiver_x[0]
    trace_rows = traces[0]
    right_table = (receiver_y[0][:, None] == lane_ids[None, :]).astype(jnp.float32)

    def advance(extended, previous, x_start, step_id):
        out_rows = extended.shape[1] - 2
        local_coefs = tuple((table for table in all_coefs))
        padded = jnp.pad(extended, ((0, 0), (0, 0), (1, 1), (1, 1)))
        updated = wave_update(padded, previous, local_coefs)
        x_ids = x_start + jnp.arange(out_rows)
        source_plane = ((x_ids[:, None] == src_x) & (lane_ids[None, :] == src_y)).astype(
            jnp.float32
        )
        left_table = (x_ids[:, None] == rec_x[None, :]).astype(jnp.float32) * trace_rows[step_id][
            None, :
        ]
        receiver_plane = jnp.dot(
            left_table,
            right_table,
            precision=lax.Precision.HIGHEST,
            preferred_element_type=jnp.float32,
        )
        return inject(updated, local_coefs[0], source_plane * wave_row[step_id], receiver_plane)

    current = jnp.concatenate([source_now[0], receiver_now[0]], axis=0)
    previous = jnp.concatenate([source_before[0], receiver_before[0]], axis=0)
    start_image = jnp.zeros((row_count, y_count, z_count), jnp.float32)

    def one_step(step_id, states):
        now_fields, old_fields, image_sum = states
        extended = padded_2(now_fields, (("domain", 1),), 1)
        updated = advance(extended, old_fields, first_row, step_id)
        return (updated, now_fields, image_sum + updated[0] * updated[2])

    final = lax.fori_loop(0, step_count, one_step, (current, previous, start_image))
    placed = lax.dynamic_update_slice(
        jnp.zeros((row_count, 2 * y_count, z_count), jnp.float32),
        final[2],
        (jnp.int32(0), anchor, jnp.int32(0)),
    )
    blocks = placed.reshape(row_count, shot_count, 2 * y_count // shot_count, z_count)
    ordered = jnp.take(blocks, slab_owner, axis=1).reshape(row_count, 2 * y_count, z_count)
    summed = lax.psum_scatter(ordered, "shot", scatter_dimension=1, tiled=True)
    return summed / step_count


def solution(mesh):
    in_specs = (
        P(("groups", "domain"), "shot", None),
        P(("groups", "domain"), "shot", None),
        P(("groups", "domain"), "shot", None),
        P(("groups", "domain"), "shot", None),
        P(("groups", "domain"), "shot", None),
        P(("groups", "shot")),
        P(("groups", "shot")),
        P(("groups", "shot")),
        P(("groups", "shot"), None),
        P(("groups", "shot"), None),
        P(("groups", "shot"), None),
        P(("groups", "shot"), None, None),
        P(("groups", "shot"), None, "domain", None, None),
        P(("groups", "shot"), None, "domain", None, None),
        P(("groups", "shot"), None, "domain", None, None),
        P(("groups", "shot"), None, "domain", None, None),
        P("groups"),
    )
    out_specs = P(("groups", "domain"), "shot", None)
    return jax.shard_map(
        per_device, mesh=mesh, in_specs=in_specs, out_specs=out_specs, check_vma=False
    )
```

profile of v0, /device:TPU:0, one launch (start us, length us, event | category | flops | bytes accessed | tf_op | source)
XLA Modules:
  0.0 438.8 jit_solution(5975361505276457501)
XLA Ops:
  19.1 18.1 %all-gather.2.cloned.1.call-done = f32[5,2,384,128]{3,1,0,2:T(2,128)} async-done(((f32[5,2,96,128]{3,1,0,2:T(2,128)}), f32[5,2,384,128]{3,1,0,2:T(2,128)}) %all-gather.2.cloned.1.call-update) | async-done | bytes 1966096 | tf_op jit(solution)/shard_map/all_gather | solution.py:118
  37.2 7.6 %multiply_bitcast_fusion = (f32[2,192,128]{2,0,1:T(2,128)S(1)}, f32[1,2,192,128]{3,1,0,2:T(2,128)S(1)}, f32[2,192,128]{2,0,1:T(2,128)}, f32[2,192,128]{2,0,1:T(2...) fusion(f32[5,2,384,128]{3,1,0,2:T(2,128)} %all-gather.2.cloned., ...), kind=kLoop, calls=%fused_computation.175 | loop fusion | flops 442368 | bytes 2555924 | tf_op jit(solution)/shard_map/while/body/eval_jaxpr/mul | solution.py:62
  54.6 349.4 %while.22 = (s32[]{:T(128)}, f32[4,2,192,128]{2,1,3,0:T(2,128)S(1)}, f32[4,2,192,128]{2,1,3,0:T(2,128)S(1)}, f32[2,192,128]{1,0,2:T(2,128)}, f32[2,192,128]{1,0,...) while((s32[]{:T(128)}, ...), condition=%wide.region_2.0_spmd.clone, body=%wide.region_0.2_spmd.clone.sunk | while | flops 15642534 | bytes 42234596 | solution.py:160
  57.9 5.4 %collective-permute-start.1 = (f32[4,1,192,128]{2,1,3,0:T(1,128)}, f32[4,1,192,128]{2,1,3,0:T(1,128)}, u32[]{:S(2)}, u32[]{:S(2)}) collective-permute-start(f32[4,1,192,128]{2,1,3,0:T(1,128)} %get-tuple-element.792), channel_id=1, source_target_pairs={{0,4},{4,8},{8,12},{1,5},{5,9},{9,13},{2,6},{6,10},{10,14},{3,7},{... | collective-permute-start | bytes 1179656 | tf_op jit(solution)/shard_map/while/body/eval_jaxpr/ppermute | solution.py:15
  79.7 8.1 %fusion.93 = (f32[1,2,192,128]{2,1,3,0:T(2,128)S(1)}, f32[2,192,128]{1,0,2:T(2,128)S(1)}, f32[2,192,128]{1,0,2:T(2,128)S(1)}) fusion(f32[2,192,128]{1,0,2:T(2,128)S(1)} %get-tuple-element.867, f32[2,192,128]{1,0,2:T(2,128)S(1)} %get-tuple-element.866, f32[2,192,128]{1,0,2:T(2,128)S(1)} %copy-done.3, f32[4,2,192,128]{2,1,3,0:T(2,128)S(1)} %get-tuple-element.833, ...), kind=kLoop, calls=%fused_computation.134.clone.1 | loop fusion | flops 3489792 | bytes 10027008 | tf_op jit(solution)/shard_map/while/body/eval_jaxpr/stack | solution.py:83
  87.8 8.1 %fusion.92 = (f32[1,2,192,128]{2,1,3,0:T(2,128)S(1)}, f32[2,192,128]{1,0,2:T(2,128)S(1)}, f32[2,192,128]{1,0,2:T(2,128)S(1)}) fusion(f32[2,192,128]{1,0,2:T(2,128)S(1)} %get-tuple-element.867, f32[2,192,128]{1,0,2:T(2,128)S(1)} %get-tuple-element.866, f32[2,192,128]{1,0,2:T(2,128)S(1)} %copy-done.3, f32[4,2,192,128]{2,1,3,0:T(2,128)S(1)} %get-tuple-element.833, ...), kind=kLoop, calls=%fused_computation.140.clone.1 | loop fusion | flops 3489792 | bytes 10027008 | tf_op jit(solution)/shard_map/while/body/eval_jaxpr/stack | solution.py:83
  103.8 5.8 %collective-permute-start.1 = (f32[4,1,192,128]{2,1,3,0:T(1,128)}, f32[4,1,192,128]{2,1,3,0:T(1,128)}, u32[]{:S(2)}, u32[]{:S(2)}) collective-permute-start(f32[4,1,192,128]{2,1,3,0:T(1,128)} %get-tuple-element.792), channel_id=1, source_target_pairs={{0,4},{4,8},{8,12},{1,5},{5,9},{9,13},{2,6},{6,10},{10,14},{3,7},{... | collective-permute-start | bytes 1179656 | tf_op jit(solution)/shard_map/while/body/eval_jaxpr/ppermute | solution.py:15
  125.3 8.1 %fusion.93 = (f32[1,2,192,128]{2,1,3,0:T(2,128)S(1)}, f32[2,192,128]{1,0,2:T(2,128)S(1)}, f32[2,192,128]{1,0,2:T(2,128)S(1)}) fusion(f32[2,192,128]{1,0,2:T(2,128)S(1)} %get-tuple-element.867, f32[2,192,128]{1,0,2:T(2,128)S(1)} %get-tuple-element.866, f32[2,192,128]{1,0,2:T(2,128)S(1)} %copy-done.3, f32[4,2,192,128]{2,1,3,0:T(2,128)S(1)} %get-tuple-element.833, ...), kind=kLoop, calls=%fused_computation.134.clone.1 | loop fusion | flops 3489792 | bytes 10027008 | tf_op jit(solution)/shard_map/while/body/eval_jaxpr/stack | solution.py:83
  133.3 8.1 %fusion.92 = (f32[1,2,192,128]{2,1,3,0:T(2,128)S(1)}, f32[2,192,128]{1,0,2:T(2,128)S(1)}, f32[2,192,128]{1,0,2:T(2,128)S(1)}) fusion(f32[2,192,128]{1,0,2:T(2,128)S(1)} %get-tuple-element.867, f32[2,192,128]{1,0,2:T(2,128)S(1)} %get-tuple-element.866, f32[2,192,128]{1,0,2:T(2,128)S(1)} %copy-done.3, f32[4,2,192,128]{2,1,3,0:T(2,128)S(1)} %get-tuple-element.833, ...), kind=kLoop, calls=%fused_computation.140.clone.1 | loop fusion | flops 3489792 | bytes 10027008 | tf_op jit(solution)/shard_map/while/body/eval_jaxpr/stack | solution.py:83
  149.4 5.8 %collective-permute-start.1 = (f32[4,1,192,128]{2,1,3,0:T(1,128)}, f32[4,1,192,128]{2,1,3,0:T(1,128)}, u32[]{:S(2)}, u32[]{:S(2)}) collective-permute-start(f32[4,1,192,128]{2,1,3,0:T(1,128)} %get-tuple-element.792), channel_id=1, source_target_pairs={{0,4},{4,8},{8,12},{1,5},{5,9},{9,13},{2,6},{6,10},{10,14},{3,7},{... | collective-permute-start | bytes 1179656 | tf_op jit(solution)/shard_map/while/body/eval_jaxpr/ppermute | solution.py:15
  169.9 8.1 %fusion.93 = (f32[1,2,192,128]{2,1,3,0:T(2,128)S(1)}, f32[2,192,128]{1,0,2:T(2,128)S(1)}, f32[2,192,128]{1,0,2:T(2,128)S(1)}) fusion(f32[2,192,128]{1,0,2:T(2,128)S(1)} %get-tuple-element.867, f32[2,192,128]{1,0,2:T(2,128)S(1)} %get-tuple-element.866, f32[2,192,128]{1,0,2:T(2,128)S(1)} %copy-done.3, f32[4,2,192,128]{2,1,3,0:T(2,128)S(1)} %get-tuple-element.833, ...), kind=kLoop, calls=%fused_computation.134.clone.1 | loop fusion | flops 3489792 | bytes 10027008 | tf_op jit(solution)/shard_map/while/body/eval_jaxpr/stack | solution.py:83
  178.0 8.1 %fusion.92 = (f32[1,2,192,128]{2,1,3,0:T(2,128)S(1)}, f32[2,192,128]{1,0,2:T(2,128)S(1)}, f32[2,192,128]{1,0,2:T(2,128)S(1)}) fusion(f32[2,192,128]{1,0,2:T(2,128)S(1)} %get-tuple-element.867, f32[2,192,128]{1,0,2:T(2,128)S(1)} %get-tuple-element.866, f32[2,192,128]{1,0,2:T(2,128)S(1)} %copy-done.3, f32[4,2,192,128]{2,1,3,0:T(2,128)S(1)} %get-tuple-element.833, ...), kind=kLoop, calls=%fused_computation.140.clone.1 | loop fusion | flops 3489792 | bytes 10027008 | tf_op jit(solution)/shard_map/while/body/eval_jaxpr/stack | solution.py:83
  194.0 5.8 %collective-permute-start.1 = (f32[4,1,192,128]{2,1,3,0:T(1,128)}, f32[4,1,192,128]{2,1,3,0:T(1,128)}, u32[]{:S(2)}, u32[]{:S(2)}) collective-permute-start(f32[4,1,192,128]{2,1,3,0:T(1,128)} %get-tuple-element.792), channel_id=1, source_target_pairs={{0,4},{4,8},{8,12},{1,5},{5,9},{9,13},{2,6},{6,10},{10,14},{3,7},{... | collective-permute-start | bytes 1179656 | tf_op jit(solution)/shard_map/while/body/eval_jaxpr/ppermute | solution.py:15
  208.0 4.5 %select_maximum_fusion.3 = f32[4,4,194,130]{2,1,3,0:T(4,128)S(1)} fusion(f32[4,1,192,128]{2,1,3,0:T(1,128)} %collective-permute-done, f32[4,2,192,128]{2,1,3,0:T(2,128)S(1)} %get-tuple-element.832, f32[4,1,192,128]{2,1,3,0:T(1,128)} %collective-permute-done.1), kind=kLoop, calls=%fused_computation.7.clone.1 | loop fusion | flops 6052800 | bytes 3186944 | tf_op jit(solution)/shard_map/while/body/eval_jaxpr/concatenate | solution.py:19
  213.6 8.1 %fusion.93 = (f32[1,2,192,128]{2,1,3,0:T(2,128)S(1)}, f32[2,192,128]{1,0,2:T(2,128)S(1)}, f32[2,192,128]{1,0,2:T(2,128)S(1)}) fusion(f32[2,192,128]{1,0,2:T(2,128)S(1)} %get-tuple-element.867, f32[2,192,128]{1,0,2:T(2,128)S(1)} %get-tuple-element.866, f32[2,192,128]{1,0,2:T(2,128)S(1)} %copy-done.3, f32[4,2,192,128]{2,1,3,0:T(2,128)S(1)} %get-tuple-element.833, ...), kind=kLoop, calls=%fused_computation.134.clone.1 | loop fusion | flops 3489792 | bytes 10027008 | tf_op jit(solution)/shard_map/while/body/eval_jaxpr/stack | solution.py:83
  221.7 8.1 %fusion.92 = (f32[1,2,192,128]{2,1,3,0:T(2,128)S(1)}, f32[2,192,128]{1,0,2:T(2,128)S(1)}, f32[2,192,128]{1,0,2:T(2,128)S(1)}) fusion(f32[2,192,128]{1,0,2:T(2,128)S(1)} %get-tuple-element.867, f32[2,192,128]{1,0,2:T(2,128)S(1)} %get-tuple-element.866, f32[2,192,128]{1,0,2:T(2,128)S(1)} %copy-done.3, f32[4,2,192,128]{2,1,3,0:T(2,128)S(1)} %get-tuple-element.833, ...), kind=kLoop, calls=%fused_computation.140.clone.1 | loop fusion | flops 3489792 | bytes 10027008 | tf_op jit(solution)/shard_map/while/body/eval_jaxpr/stack | solution.py:83
  237.7 5.8 %collective-permute-start.1 = (f32[4,1,192,128]{2,1,3,0:T(1,128)}, f32[4,1,192,128]{2,1,3,0:T(1,128)}, u32[]{:S(2)}, u32[]{:S(2)}) collective-permute-start(f32[4,1,192,128]{2,1,3,0:T(1,128)} %get-tuple-element.792), channel_id=1, source_target_pairs={{0,4},{4,8},{8,12},{1,5},{5,9},{9,13},{2,6},{6,10},{10,14},{3,7},{... | collective-permute-start | bytes 1179656 | tf_op jit(solution)/shard_map/while/body/eval_jaxpr/ppermute | solution.py:15
  256.4 8.1 %fusion.93 = (f32[1,2,192,128]{2,1,3,0:T(2,128)S(1)}, f32[2,192,128]{1,0,2:T(2,128)S(1)}, f32[2,192,128]{1,0,2:T(2,128)S(1)}) fusion(f32[2,192,128]{1,0,2:T(2,128)S(1)} %get-tuple-element.867, f32[2,192,128]{1,0,2:T(2,128)S(1)} %get-tuple-element.866, f32[2,192,128]{1,0,2:T(2,128)S(1)} %copy-done.3, f32[4,2,192,128]{2,1,3,0:T(2,128)S(1)} %get-tuple-element.833, ...), kind=kLoop, calls=%fused_computation.134.clone.1 | loop fusion | flops 3489792 | bytes 10027008 | tf_op jit(solution)/shard_map/while/body/eval_jaxpr/stack | solution.py:83
  264.5 8.1 %fusion.92 = (f32[1,2,192,128]{2,1,3,0:T(2,128)S(1)}, f32[2,192,128]{1,0,2:T(2,128)S(1)}, f32[2,192,128]{1,0,2:T(2,128)S(1)}) fusion(f32[2,192,128]{1,0,2:T(2,128)S(1)} %get-tuple-element.867, f32[2,192,128]{1,0,2:T(2,128)S(1)} %get-tuple-element.866, f32[2,192,128]{1,0,2:T(2,128)S(1)} %copy-done.3, f32[4,2,192,128]{2,1,3,0:T(2,128)S(1)} %get-tuple-element.833, ...), kind=kLoop, calls=%fused_computation.140.clone.1 | loop fusion | flops 3489792 | bytes 10027008 | tf_op jit(solution)/shard_map/while/body/eval_jaxpr/stack | solution.py:83
  280.5 5.8 %collective-permute-start.1 = (f32[4,1,192,128]{2,1,3,0:T(1,128)}, f32[4,1,192,128]{2,1,3,0:T(1,128)}, u32[]{:S(2)}, u32[]{:S(2)}) collective-permute-start(f32[4,1,192,128]{2,1,3,0:T(1,128)} %get-tuple-element.792), channel_id=1, source_target_pairs={{0,4},{4,8},{8,12},{1,5},{5,9},{9,13},{2,6},{6,10},{10,14},{3,7},{... | collective-permute-start | bytes 1179656 | tf_op jit(solution)/shard_map/while/body/eval_jaxpr/ppermute | solution.py:15
  293.2 4.5 %select_maximum_fusion.3 = f32[4,4,194,130]{2,1,3,0:T(4,128)S(1)} fusion(f32[4,1,192,128]{2,1,3,0:T(1,128)} %collective-permute-done, f32[4,2,192,128]{2,1,3,0:T(2,128)S(1)} %get-tuple-element.832, f32[4,1,192,128]{2,1,3,0:T(1,128)} %collective-permute-done.1), kind=kLoop, calls=%fused_computation.7.clone.1 | loop fusion | flops 6052800 | bytes 3186944 | tf_op jit(solution)/shard_map/while/body/eval_jaxpr/concatenate | solution.py:19
  298.9 8.1 %fusion.93 = (f32[1,2,192,128]{2,1,3,0:T(2,128)S(1)}, f32[2,192,128]{1,0,2:T(2,128)S(1)}, f32[2,192,128]{1,0,2:T(2,128)S(1)}) fusion(f32[2,192,128]{1,0,2:T(2,128)S(1)} %get-tuple-element.867, f32[2,192,128]{1,0,2:T(2,128)S(1)} %get-tuple-element.866, f32[2,192,128]{1,0,2:T(2,128)S(1)} %copy-done.3, f32[4,2,192,128]{2,1,3,0:T(2,128)S(1)} %get-tuple-element.833, ...), kind=kLoop, calls=%fused_computation.134.clone.1 | loop fusion | flops 3489792 | bytes 10027008 | tf_op jit(solution)/shard_map/while/body/eval_jaxpr/stack | solution.py:83
  307.0 8.1 %fusion.92 = (f32[1,2,192,128]{2,1,3,0:T(2,128)S(1)}, f32[2,192,128]{1,0,2:T(2,128)S(1)}, f32[2,192,128]{1,0,2:T(2,128)S(1)}) fusion(f32[2,192,128]{1,0,2:T(2,128)S(1)} %get-tuple-element.867, f32[2,192,128]{1,0,2:T(2,128)S(1)} %get-tuple-element.866, f32[2,192,128]{1,0,2:T(2,128)S(1)} %copy-done.3, f32[4,2,192,128]{2,1,3,0:T(2,128)S(1)} %get-tuple-element.833, ...), kind=kLoop, calls=%fused_computation.140.clone.1 | loop fusion | flops 3489792 | bytes 10027008 | tf_op jit(solution)/shard_map/while/body/eval_jaxpr/stack | solution.py:83
  323.0 5.4 %collective-permute-start.1 = (f32[4,1,192,128]{2,1,3,0:T(1,128)}, f32[4,1,192,128]{2,1,3,0:T(1,128)}, u32[]{:S(2)}, u32[]{:S(2)}) collective-permute-start(f32[4,1,192,128]{2,1,3,0:T(1,128)} %get-tuple-element.792), channel_id=1, source_target_pairs={{0,4},{4,8},{8,12},{1,5},{5,9},{9,13},{2,6},{6,10},{10,14},{3,7},{... | collective-permute-start | bytes 1179656 | tf_op jit(solution)/shard_map/while/body/eval_jaxpr/ppermute | solution.py:15
  335.2 4.5 %select_maximum_fusion.3 = f32[4,4,194,130]{2,1,3,0:T(4,128)S(1)} fusion(f32[4,1,192,128]{2,1,3,0:T(1,128)} %collective-permute-done, f32[4,2,192,128]{2,1,3,0:T(2,128)S(1)} %get-tuple-element.832, f32[4,1,192,128]{2,1,3,0:T(1,128)} %collective-permute-done.1), kind=kLoop, calls=%fused_computation.7.clone.1 | loop fusion | flops 6052800 | bytes 3186944 | tf_op jit(solution)/shard_map/while/body/eval_jaxpr/concatenate | solution.py:19
  340.9 8.1 %fusion.93 = (f32[1,2,192,128]{2,1,3,0:T(2,128)S(1)}, f32[2,192,128]{1,0,2:T(2,128)S(1)}, f32[2,192,128]{1,0,2:T(2,128)S(1)}) fusion(f32[2,192,128]{1,0,2:T(2,128)S(1)} %get-tuple-element.867, f32[2,192,128]{1,0,2:T(2,128)S(1)} %get-tuple-element.866, f32[2,192,128]{1,0,2:T(2,128)S(1)} %copy-done.3, f32[4,2,192,128]{2,1,3,0:T(2,128)S(1)} %get-tuple-element.833, ...), kind=kLoop, calls=%fused_computation.134.clone.1 | loop fusion | flops 3489792 | bytes 10027008 | tf_op jit(solution)/shard_map/while/body/eval_jaxpr/stack | solution.py:83
  349.0 8.1 %fusion.92 = (f32[1,2,192,128]{2,1,3,0:T(2,128)S(1)}, f32[2,192,128]{1,0,2:T(2,128)S(1)}, f32[2,192,128]{1,0,2:T(2,128)S(1)}) fusion(f32[2,192,128]{1,0,2:T(2,128)S(1)} %get-tuple-element.867, f32[2,192,128]{1,0,2:T(2,128)S(1)} %get-tuple-element.866, f32[2,192,128]{1,0,2:T(2,128)S(1)} %copy-done.3, f32[4,2,192,128]{2,1,3,0:T(2,128)S(1)} %get-tuple-element.833, ...), kind=kLoop, calls=%fused_computation.140.clone.1 | loop fusion | flops 3489792 | bytes 10027008 | tf_op jit(solution)/shard_map/while/body/eval_jaxpr/stack | solution.py:83
  365.0 5.4 %collective-permute-start.1 = (f32[4,1,192,128]{2,1,3,0:T(1,128)}, f32[4,1,192,128]{2,1,3,0:T(1,128)}, u32[]{:S(2)}, u32[]{:S(2)}) collective-permute-start(f32[4,1,192,128]{2,1,3,0:T(1,128)} %get-tuple-element.792), channel_id=1, source_target_pairs={{0,4},{4,8},{8,12},{1,5},{5,9},{9,13},{2,6},{6,10},{10,14},{3,7},{... | collective-permute-start | bytes 1179656 | tf_op jit(solution)/shard_map/while/body/eval_jaxpr/ppermute | solution.py:15
  377.2 4.5 %select_maximum_fusion.3 = f32[4,4,194,130]{2,1,3,0:T(4,128)S(1)} fusion(f32[4,1,192,128]{2,1,3,0:T(1,128)} %collective-permute-done, f32[4,2,192,128]{2,1,3,0:T(2,128)S(1)} %get-tuple-element.832, f32[4,1,192,128]{2,1,3,0:T(1,128)} %collective-permute-done.1), kind=kLoop, calls=%fused_computation.7.clone.1 | loop fusion | flops 6052800 | bytes 3186944 | tf_op jit(solution)/shard_map/while/body/eval_jaxpr/concatenate | solution.py:19
  382.9 8.1 %fusion.93 = (f32[1,2,192,128]{2,1,3,0:T(2,128)S(1)}, f32[2,192,128]{1,0,2:T(2,128)S(1)}, f32[2,192,128]{1,0,2:T(2,128)S(1)}) fusion(f32[2,192,128]{1,0,2:T(2,128)S(1)} %get-tuple-element.867, f32[2,192,128]{1,0,2:T(2,128)S(1)} %get-tuple-element.866, f32[2,192,128]{1,0,2:T(2,128)S(1)} %copy-done.3, f32[4,2,192,128]{2,1,3,0:T(2,128)S(1)} %get-tuple-element.833, ...), kind=kLoop, calls=%fused_computation.134.clone.1 | loop fusion | flops 3489792 | bytes 10027008 | tf_op jit(solution)/shard_map/while/body/eval_jaxpr/stack | solution.py:83
  391.0 8.1 %fusion.92 = (f32[1,2,192,128]{2,1,3,0:T(2,128)S(1)}, f32[2,192,128]{1,0,2:T(2,128)S(1)}, f32[2,192,128]{1,0,2:T(2,128)S(1)}) fusion(f32[2,192,128]{1,0,2:T(2,128)S(1)} %get-tuple-element.867, f32[2,192,128]{1,0,2:T(2,128)S(1)} %get-tuple-element.866, f32[2,192,128]{1,0,2:T(2,128)S(1)} %copy-done.3, f32[4,2,192,128]{2,1,3,0:T(2,128)S(1)} %get-tuple-element.833, ...), kind=kLoop, calls=%fused_computation.140.clone.1 | loop fusion | flops 3489792 | bytes 10027008 | tf_op jit(solution)/shard_map/while/body/eval_jaxpr/stack | solution.py:83
  407.4 23.0 %reduce-scatter.2.cloned.1.call-done = f32[2,96,128]{2,1,0:T(8,128)} async-done(((f32[2,384,128]{2,1,0:T(8,128)}), f32[2,96,128]{2,1,0:T(8,128)}) %reduce-scatter.2.cloned.1.call-update) | async-done | bytes 98320 | tf_op jit(solution)/shard_map/reduce_scatter | solution.py:168
  (335 shorter events, 181.9 us)
Async XLA Ops:
  6.5 7.9 %copy-start.7 = (f32[1,2,2,192,128]{4,3,2,1,0:T(8,128)S(1)}, f32[1,2,2,192,128]{4,3,2,1,0:T(8,128)}, u32[]{:S(2)}) copy-start(f32[1,2,2,192,128]{4,3,2,1,0:T(8,128)} %param.37) | copy-start | bytes 1179652
  6.5 8.1 %copy-start.8 = (f32[1,2,2,192,128]{4,3,2,1,0:T(8,128)S(1)}, f32[1,2,2,192,128]{4,3,2,1,0:T(8,128)}, u32[]{:S(2)}) copy-start(f32[1,2,2,192,128]{4,3,2,1,0:T(8,128)} %param.36) | copy-start | bytes 1179652
  6.5 9.1 %copy-start.9 = (f32[1,2,2,192,128]{4,3,2,1,0:T(8,128)S(1)}, f32[1,2,2,192,128]{4,3,2,1,0:T(8,128)}, u32[]{:S(2)}) copy-start(f32[1,2,2,192,128]{4,3,2,1,0:T(8,128)} %param.38) | copy-start | bytes 1179652
  6.5 30.6 %all-gather.2.cloned.1.call-start = ((), (), s32[]{:S(2)}) async-start(), calls=%async_computation.1 | async-start | bytes 2457600 | tf_op jit(solution)/shard_map/all_gather | solution.py:118
  11.7 5.0 %copy-start.13 = (s32[4]{0:T(128)S(1)}, s32[4]{0:T(128)}, u32[]{:S(2)}) copy-start(s32[4]{0:T(128)} %param.39) | copy-start | bytes 52
  12.5 417.9 %reduce-scatter.2.cloned.1.call-start = ((), (), s32[]{:S(2)}) async-start(), calls=%async_computation.2 | async-start | bytes 491520 | tf_op jit(solution)/shard_map/reduce_scatter | solution.py:168
  45.7 8.8 %copy-start.10 = (s32[4]{0:T(128)S(1)}, s32[4]{0:T(128)}, u32[]{:S(2)}) copy-start(s32[4]{0:T(128)} %constant.211.clone.2) | copy-start | bytes 52
  45.7 8.8 %copy-start.11 = (s32[1,256]{1,0:T(1,128)S(1)}, s32[1,256]{1,0:T(1,128)}, u32[]{:S(2)}) copy-start(s32[1,256]{1,0:T(1,128)} %param.32) | copy-start | bytes 3076
  54.8 15.0 %copy-start.12 = (s32[256]{0:T(256)S(1)}, s32[256]{0:T(256)}, u32[]{:S(2)}) copy-start(s32[256]{0:T(256)} %get-tuple-element.874) | copy-start | bytes 3076 | tf_op jit(solution)/shard_map/while
  56.6 16.3 %collective-permute-start = (f32[4,1,192,128]{2,1,3,0:T(1,128)}, f32[4,1,192,128]{2,1,3,0:T(1,128)}, u32[]{:S(2)}, u32[]{:S(2)}) collective-permute-start(f32[4,1,192,128]{2,1,3,0:T(1,128)} %get-tuple-element.791), channel_id=1, source_target_pairs={{4,0},{8,4},{12,8},{5,1},{9,5},{13,9},{6,2},{10,6},{14,10},{7,3},{... | collective-permute-start | bytes 1179656 | tf_op jit(solution)/shard_map/while/body/eval_jaxpr/ppermute | solution.py:18
  57.9 16.2 %collective-permute-start.1 = (f32[4,1,192,128]{2,1,3,0:T(1,128)}, f32[4,1,192,128]{2,1,3,0:T(1,128)}, u32[]{:S(2)}, u32[]{:S(2)}) collective-permute-start(f32[4,1,192,128]{2,1,3,0:T(1,128)} %get-tuple-element.792), channel_id=1, source_target_pairs={{0,4},{4,8},{8,12},{1,5},{5,9},{9,13},{2,6},{6,10},{10,14},{3,7},{... | collective-permute-start | bytes 1179656 | tf_op jit(solution)/shard_map/while/body/eval_jaxpr/ppermute | solution.py:15
  100.7 15.5 %copy-start.12 = (s32[256]{0:T(256)S(1)}, s32[256]{0:T(256)}, u32[]{:S(2)}) copy-start(s32[256]{0:T(256)} %get-tuple-element.874) | copy-start | bytes 3076 | tf_op jit(solution)/shard_map/while
  102.5 15.9 %collective-permute-start = (f32[4,1,192,128]{2,1,3,0:T(1,128)}, f32[4,1,192,128]{2,1,3,0:T(1,128)}, u32[]{:S(2)}, u32[]{:S(2)}) collective-permute-start(f32[4,1,192,128]{2,1,3,0:T(1,128)} %get-tuple-element.791), channel_id=1, source_target_pairs={{4,0},{8,4},{12,8},{5,1},{9,5},{13,9},{6,2},{10,6},{14,10},{7,3},{... | collective-permute-start | bytes 1179656 | tf_op jit(solution)/shard_map/while/body/eval_jaxpr/ppermute | solution.py:18
  103.8 15.8 %collective-permute-start.1 = (f32[4,1,192,128]{2,1,3,0:T(1,128)}, f32[4,1,192,128]{2,1,3,0:T(1,128)}, u32[]{:S(2)}, u32[]{:S(2)}) collective-permute-start(f32[4,1,192,128]{2,1,3,0:T(1,128)} %get-tuple-element.792), channel_id=1, source_target_pairs={{0,4},{4,8},{8,12},{1,5},{5,9},{9,13},{2,6},{6,10},{10,14},{3,7},{... | collective-permute-start | bytes 1179656 | tf_op jit(solution)/shard_map/while/body/eval_jaxpr/ppermute | solution.py:15
  146.3 15.5 %copy-start.12 = (s32[256]{0:T(256)S(1)}, s32[256]{0:T(256)}, u32[]{:S(2)}) copy-start(s32[256]{0:T(256)} %get-tuple-element.874) | copy-start | bytes 3076 | tf_op jit(solution)/shard_map/while
  148.1 15.0 %collective-permute-start = (f32[4,1,192,128]{2,1,3,0:T(1,128)}, f32[4,1,192,128]{2,1,3,0:T(1,128)}, u32[]{:S(2)}, u32[]{:S(2)}) collective-permute-start(f32[4,1,192,128]{2,1,3,0:T(1,128)} %get-tuple-element.791), channel_id=1, source_target_pairs={{4,0},{8,4},{12,8},{5,1},{9,5},{13,9},{6,2},{10,6},{14,10},{7,3},{... | collective-permute-start | bytes 1179656 | tf_op jit(solution)/shard_map/while/body/eval_jaxpr/ppermute | solution.py:18
  149.4 14.8 %collective-permute-start.1 = (f32[4,1,192,128]{2,1,3,0:T(1,128)}, f32[4,1,192,128]{2,1,3,0:T(1,128)}, u32[]{:S(2)}, u32[]{:S(2)}) collective-permute-start(f32[4,1,192,128]{2,1,3,0:T(1,128)} %get-tuple-element.792), channel_id=1, source_target_pairs={{0,4},{4,8},{8,12},{1,5},{5,9},{9,13},{2,6},{6,10},{10,14},{3,7},{... | collective-permute-start | bytes 1179656 | tf_op jit(solution)/shard_map/while/body/eval_jaxpr/ppermute | solution.py:15
  190.9 15.5 %copy-start.12 = (s32[256]{0:T(256)S(1)}, s32[256]{0:T(256)}, u32[]{:S(2)}) copy-start(s32[256]{0:T(256)} %get-tuple-element.874) | copy-start | bytes 3076 | tf_op jit(solution)/shard_map/while
  192.7 14.0 %collective-permute-start = (f32[4,1,192,128]{2,1,3,0:T(1,128)}, f32[4,1,192,128]{2,1,3,0:T(1,128)}, u32[]{:S(2)}, u32[]{:S(2)}) collective-permute-start(f32[4,1,192,128]{2,1,3,0:T(1,128)} %get-tuple-element.791), channel_id=1, source_target_pairs={{4,0},{8,4},{12,8},{5,1},{9,5},{13,9},{6,2},{10,6},{14,10},{7,3},{... | collective-permute-start | bytes 1179656 | tf_op jit(solution)/shard_map/while/body/eval_jaxpr/ppermute | solution.py:18
  194.0 13.9 %collective-permute-start.1 = (f32[4,1,192,128]{2,1,3,0:T(1,128)}, f32[4,1,192,128]{2,1,3,0:T(1,128)}, u32[]{:S(2)}, u32[]{:S(2)}) collective-permute-start(f32[4,1,192,128]{2,1,3,0:T(1,128)} %get-tuple-element.792), channel_id=1, source_target_pairs={{0,4},{4,8},{8,12},{1,5},{5,9},{9,13},{2,6},{6,10},{10,14},{3,7},{... | collective-permute-start | bytes 1179656 | tf_op jit(solution)/shard_map/while/body/eval_jaxpr/ppermute | solution.py:15
  234.6 15.5 %copy-start.12 = (s32[256]{0:T(256)S(1)}, s32[256]{0:T(256)}, u32[]{:S(2)}) copy-start(s32[256]{0:T(256)} %get-tuple-element.874) | copy-start | bytes 3076 | tf_op jit(solution)/shard_map/while
  236.5 13.9 %collective-permute-start = (f32[4,1,192,128]{2,1,3,0:T(1,128)}, f32[4,1,192,128]{2,1,3,0:T(1,128)}, u32[]{:S(2)}, u32[]{:S(2)}) collective-permute-start(f32[4,1,192,128]{2,1,3,0:T(1,128)} %get-tuple-element.791), channel_id=1, source_target_pairs={{4,0},{8,4},{12,8},{5,1},{9,5},{13,9},{6,2},{10,6},{14,10},{7,3},{... | collective-permute-start | bytes 1179656 | tf_op jit(solution)/shard_map/while/body/eval_jaxpr/ppermute | solution.py:18
  237.7 13.0 %collective-permute-start.1 = (f32[4,1,192,128]{2,1,3,0:T(1,128)}, f32[4,1,192,128]{2,1,3,0:T(1,128)}, u32[]{:S(2)}, u32[]{:S(2)}) collective-permute-start(f32[4,1,192,128]{2,1,3,0:T(1,128)} %get-tuple-element.792), channel_id=1, source_target_pairs={{0,4},{4,8},{8,12},{1,5},{5,9},{9,13},{2,6},{6,10},{10,14},{3,7},{... | collective-permute-start | bytes 1179656 | tf_op jit(solution)/shard_map/while/body/eval_jaxpr/ppermute | solution.py:15
  277.4 15.5 %copy-start.12 = (s32[256]{0:T(256)S(1)}, s32[256]{0:T(256)}, u32[]{:S(2)}) copy-start(s32[256]{0:T(256)} %get-tuple-element.874) | copy-start | bytes 3076 | tf_op jit(solution)/shard_map/while
  279.2 13.9 %collective-permute-start = (f32[4,1,192,128]{2,1,3,0:T(1,128)}, f32[4,1,192,128]{2,1,3,0:T(1,128)}, u32[]{:S(2)}, u32[]{:S(2)}) collective-permute-start(f32[4,1,192,128]{2,1,3,0:T(1,128)} %get-tuple-element.791), channel_id=1, source_target_pairs={{4,0},{8,4},{12,8},{5,1},{9,5},{13,9},{6,2},{10,6},{14,10},{7,3},{... | collective-permute-start | bytes 1179656 | tf_op jit(solution)/shard_map/while/body/eval_jaxpr/ppermute | solution.py:18
  280.5 12.7 %collective-permute-start.1 = (f32[4,1,192,128]{2,1,3,0:T(1,128)}, f32[4,1,192,128]{2,1,3,0:T(1,128)}, u32[]{:S(2)}, u32[]{:S(2)}) collective-permute-start(f32[4,1,192,128]{2,1,3,0:T(1,128)} %get-tuple-element.792), channel_id=1, source_target_pairs={{0,4},{4,8},{8,12},{1,5},{5,9},{9,13},{2,6},{6,10},{10,14},{3,7},{... | collective-permute-start | bytes 1179656 | tf_op jit(solution)/shard_map/while/body/eval_jaxpr/ppermute | solution.py:15
  319.9 15.0 %copy-start.12 = (s32[256]{0:T(256)S(1)}, s32[256]{0:T(256)}, u32[]{:S(2)}) copy-start(s32[256]{0:T(256)} %get-tuple-element.874) | copy-start | bytes 3076 | tf_op jit(solution)/shard_map/while
  321.7 13.5 %collective-permute-start = (f32[4,1,192,128]{2,1,3,0:T(1,128)}, f32[4,1,192,128]{2,1,3,0:T(1,128)}, u32[]{:S(2)}, u32[]{:S(2)}) collective-permute-start(f32[4,1,192,128]{2,1,3,0:T(1,128)} %get-tuple-element.791), channel_id=1, source_target_pairs={{4,0},{8,4},{12,8},{5,1},{9,5},{13,9},{6,2},{10,6},{14,10},{7,3},{... | collective-permute-start | bytes 1179656 | tf_op jit(solution)/shard_map/while/body/eval_jaxpr/ppermute | solution.py:18
  323.0 12.2 %collective-permute-start.1 = (f32[4,1,192,128]{2,1,3,0:T(1,128)}, f32[4,1,192,128]{2,1,3,0:T(1,128)}, u32[]{:S(2)}, u32[]{:S(2)}) collective-permute-start(f32[4,1,192,128]{2,1,3,0:T(1,128)} %get-tuple-element.792), channel_id=1, source_target_pairs={{0,4},{4,8},{8,12},{1,5},{5,9},{9,13},{2,6},{6,10},{10,14},{3,7},{... | collective-permute-start | bytes 1179656 | tf_op jit(solution)/shard_map/while/body/eval_jaxpr/ppermute | solution.py:15
  361.9 15.0 %copy-start.12 = (s32[256]{0:T(256)S(1)}, s32[256]{0:T(256)}, u32[]{:S(2)}) copy-start(s32[256]{0:T(256)} %get-tuple-element.874) | copy-start | bytes 3076 | tf_op jit(solution)/shard_map/while
  363.7 13.5 %collective-permute-start = (f32[4,1,192,128]{2,1,3,0:T(1,128)}, f32[4,1,192,128]{2,1,3,0:T(1,128)}, u32[]{:S(2)}, u32[]{:S(2)}) collective-permute-start(f32[4,1,192,128]{2,1,3,0:T(1,128)} %get-tuple-element.791), channel_id=1, source_target_pairs={{4,0},{8,4},{12,8},{5,1},{9,5},{13,9},{6,2},{10,6},{14,10},{7,3},{... | collective-permute-start | bytes 1179656 | tf_op jit(solution)/shard_map/while/body/eval_jaxpr/ppermute | solution.py:18
  365.0 12.2 %collective-permute-start.1 = (f32[4,1,192,128]{2,1,3,0:T(1,128)}, f32[4,1,192,128]{2,1,3,0:T(1,128)}, u32[]{:S(2)}, u32[]{:S(2)}) collective-permute-start(f32[4,1,192,128]{2,1,3,0:T(1,128)} %get-tuple-element.792), channel_id=1, source_target_pairs={{0,4},{4,8},{8,12},{1,5},{5,9},{9,13},{2,6},{6,10},{10,14},{3,7},{... | collective-permute-start | bytes 1179656 | tf_op jit(solution)/shard_map/while/body/eval_jaxpr/ppermute | solution.py:15
  (49 other events, 62.7 us)
Sparse Core Ops, SparseCore 0:
  12.6 24.5 all-gather.1
  407.5 22.8 reduce-scatter.1
where the time goes:
time: 442 us; the launch traced here: 439 us
  other arithmetic  240 us (54%)
  local copies, waits for them, and re-layouts  73.6 us (17%)
  starting transfers between devices  55.4 us (13%)
  waiting for transfers between devices  52.2 us (12%)
  between operations  14.2 us (3%)
    another operation x32, other arithmetic, wave_update(): return jnp.stack(results)  141 us
    ppermute x8, starting transfers between devices, padded_2(): lax.ppermute(lax.slice_in_dim(block, block.shape[dim] - width, None, axis...  45.1 us
    concatenate x8, other arithmetic, padded_2(): block = jnp.concatenate([low, block, high], axis=dim)  35.7 us
    reduce_scatter x1, waiting for transfers between devices, per_device(): summed = lax.psum_scatter(ordered, 'shot', scatter_dimension=1, tiled=True)  23 us
    all_gather x1, waiting for transfers between devices, per_device(): whole_model = lax.all_gather(model_share, 'shot', axis=2, tiled=True)  18.1 us
    unnamed x31, local copies, waits for them, and re-layouts  17.1 us
    another operation x16, other arithmetic  16.2 us
    scatter-add x8, other arithmetic, inject(): updated.at[0:2, :, :, SRC_Z]  15.1 us
  transfers between devices with their start and end apart: 18, of which 11 were waited for; matrix products, arithmetic and copies ran while one was open for 14% of the time, Pallas kernels for 0%

commit v1 on v0

v1 whole, which is shorter than its diff:
```python
import functools

import jax
import jax.numpy as jnp
from jax import lax
from jax.experimental import pallas as pl
from jax.experimental.pallas import tpu as pltpu
from jax.sharding import PartitionSpec as P

SRC_Z = 3
REC_Z = 1
TILE = 8
COEFS = 16
LIMIT = 40 * 1024 * 1024


class Layout:
    def __init__(self, domain, shots, rows, lines, steps):
        self.domain, self.shots, self.rows, self.lines, self.steps = domain, shots, rows, lines, steps
        self.half = domain // 2
        self.part = rows // 2
        self.width = rows * domain
        self.own = lines // domain
        halo = -(-steps // TILE) * TILE
        if self.half == 2 and self.own % TILE == 0:
            self.pad = (0, 0)
            self.chip = 2 * self.own + halo
            self.stride = lines - self.chip
            self.span = self.own + 2 * halo
        else:
            self.chip = -(-(2 * self.own + 2 * halo) // TILE) * TILE
            self.pad = (halo, max(0, (self.half - 1) * 2 * self.own + self.chip - halo - lines))
            self.stride = 2 * self.own
            self.span = self.chip

    def start(self, kc):
        return kc * self.stride

    def shift(self, c):
        return c * (self.chip - self.span)

    def rounds(self):
        count = self.domain * self.shots
        for r in range(self.domain):
            pairs = []
            for d in range(self.domain):
                for s in range(self.shots):
                    k = (d + r) % self.domain
                    to_d = self.half * (s & 1) + (k >> 1)
                    to_s = (s & ~1) | (k & 1)
                    pairs.append((d * self.shots + s, to_d * self.shots + to_s))
            assert len({pair[1] for pair in pairs}) == count
            yield r, pairs


def swapped(value, axis, bit):
    count = lax.axis_size(axis)
    return lax.ppermute(value, axis, [(i, i ^ bit) for i in range(count)])


def gather_rows(info_ref, lay, own_refs, other_refs, store):
    kc, c = info_ref[0], info_ref[1]
    shift = pl.multiple_of(info_ref[2], TILE)
    for core, refs in ((c, own_refs), (1 - c, other_refs)):
        k = 2 * kc + core
        for r, ref in enumerate(refs):
            source = lax.rem(k - r + lay.domain, lay.domain)
            for part in range(lay.part):
                store(source * lay.rows + core * lay.part + part, part, ref, shift)


def make_coefs(raw_ref, coef_ref, lay):
    lane = lax.broadcasted_iota(jnp.int32, (lay.span, raw_ref.shape[-1]), 1)
    last = raw_ref.shape[-1] - 1

    def from_below(value):
        return jnp.where(lane == 0, 0.0, pltpu.roll(value, 1, 1))

    def from_above(value):
        return jnp.where(lane == last, 0.0, pltpu.roll(value, last, 1))

    def one_row(row, unused):
        velocity, eps, delta, tilt, azimuth = (raw_ref[i, row] for i in range(5))
        gain_eps = 1.0 + 2.0 * eps
        gain_delta = jnp.sqrt(1.0 + 2.0 * delta)
        sin_tilt = jnp.sin(tilt)
        n_x = sin_tilt * jnp.cos(azimuth)
        n_y = sin_tilt * jnp.sin(azimuth)
        n_z = jnp.cos(tilt)
        xx, yy, zz = n_x * n_x, n_y * n_y, n_z * n_z
        xz, yz = 0.5 * n_x * n_z, 0.5 * n_y * n_z
        values = (
            xx, 1.0 - xx, yy, 1.0 - yy, 0.5 * n_x * n_y,
            from_below(zz), from_below(1.0 - zz), from_below(xz), from_below(yz),
            from_above(zz), from_above(1.0 - zz), from_above(xz), from_above(yz),
            velocity * gain_eps, velocity * gain_delta, velocity,
        )
        for i, value in enumerate(values):
            coef_ref[i, row] = value
        return unused

    lax.fori_loop(0, lay.width, one_row, 0)


def run_steps(state, coef_ref, inject_ref, depth, lay, after):
    z_count = state.shape[-1]
    last = z_count - 1
    lane = lax.broadcasted_iota(jnp.int32, (TILE, z_count), 1)
    chunk = next(size for size in (8, 4, 2, 1) if lay.width % size == 0)

    def row_of(now, field, row, tile):
        base = TILE + TILE * tile
        middle = state[now, field, row, base : base + TILE, :]
        low = state[now, field, row, base - 1 : base - 1 + TILE, :]
        high = state[now, field, row, base + 1 : base + 1 + TILE, :]
        return middle, high - low, high + low

    def one_step(step, unused):
        now = lax.rem(step, 2)
        new = 1 - now
        turn = lax.rem(depth - step + z_count, z_count)

        def one_chunk(first):
            for tile in range(lay.span // TILE):
                lines = slice(TILE * tile, TILE * tile + TILE)
                inner = slice(TILE + TILE * tile, 2 * TILE + TILE * tile)
                before = [row_of(now, field, first, tile) for field in (0, 1)]
                here = [row_of(now, field, first + 1, tile) for field in (0, 1)]
                for i in range(chunk):
                    row = first + i
                    beyond = [row_of(now, field, row + 2, tile) for field in (0, 1)]
                    coef = [coef_ref[n, row, lines, :] for n in range(COEFS)]
                    xx, xx0, yy, yy0, xy = coef[:5]
                    zz_b, zz0_b, xz_b, yz_b, zz_a, zz0_a, xz_a, yz_a = coef[5:13]
                    axial_gain, cross_gain, velocity = coef[13:]

                    def terms(field):
                        f, diff_y, sum_y = here[field]
                        sum_x = beyond[field][0] + before[field][0]
                        diff_x = beyond[field][0] - before[field][0]
                        mixed = beyond[field][1] - before[field][1]
                        below = xz_b * diff_x + yz_b * diff_y
                        above = xz_a * diff_x + yz_a * diff_y
                        return f, sum_x, sum_y, xy * mixed, below, above

                    p, sum_x, sum_y, mixed, below, above = terms(0)
                    across = xx0 * sum_x + yy0 * sum_y - mixed
                    across += pltpu.roll(zz0_b * p - below, last, 1) + pltpu.roll(zz0_a * p + above, 1, 1)
                    across -= 4.0 * p
                    q, sum_x, sum_y, mixed, below, above = terms(1)
                    axial = xx * sum_x + yy * sum_y + mixed
                    axial += pltpu.roll(zz_b * q + below, last, 1) + pltpu.roll(zz_a * q - above, 1, 1)
                    axial -= 2.0 * q
                    pulse = pltpu.roll(inject_ref[row, lines, :], turn, 1)
                    pulse = velocity * jnp.where(lane == depth, pulse, 0.0)
                    old_p = state[new, 0, row + 1, inner, :]
                    old_q = state[new, 1, row + 1, inner, :]
                    new_p = (p + p - old_p) + (axial_gain * across + cross_gain * axial) + pulse
                    new_q = (q + q - old_q) + (cross_gain * across + velocity * axial) + pulse
                    state[new, 0, row + 1, inner, :] = new_p
                    state[new, 1, row + 1, inner, :] = new_q
                    after(step, row, lines, new_p)
                    before, here = here, beyond

        if chunk == lay.width:
            one_chunk(0)
        else:
            lax.fori_loop(0, lay.width // chunk, lambda n, u: (one_chunk(n * chunk), u)[1], 0)
        return unused

    lax.fori_loop(0, lay.steps, one_step, 0)


def clear_edges(state, lay):
    rows, lines = state.shape[2], state.shape[3]
    edge = jnp.zeros((lines,) + state.shape[4:], jnp.float32)
    strip = jnp.zeros((rows, TILE) + state.shape[4:], jnp.float32)
    for time in (0, 1):
        for field in (0, 1):
            state[time, field, 0] = edge
            state[time, field, rows - 1] = edge
            state[time, field, :, :TILE] = strip
            state[time, field, :, lines - TILE :] = strip


def source_kernel(lay, info_ref, inject_ref, *refs):
    count = lay.domain
    waves_own, waves_other, model_own, model_other = (refs[i * count : (i + 1) * count] for i in range(4))
    coef_ref, history_ref, raw, state = refs[4 * count :]
    clear_edges(state, lay)

    def store_wave(row, part, ref, shift):
        for time in (0, 1):
            for field in (0, 1):
                state[time, field, row + 1, TILE : TILE + lay.span, :] = ref[
                    2 * time + field, part, pl.ds(shift, lay.span), :
                ]

    def store_model(row, part, ref, shift):
        for i in range(5):
            raw[i, row] = ref[i, part, pl.ds(shift, lay.span), :]

    gather_rows(info_ref, lay, waves_own, waves_other, store_wave)
    gather_rows(info_ref, lay, model_own, model_other, store_model)
    make_coefs(raw, coef_ref, lay)

    def after(step, row, lines, new_p):
        history_ref[step, row, lines, :] = new_p

    run_steps(state, coef_ref, inject_ref, SRC_Z, lay, after)


def receiver_kernel(lay, info_ref, inject_ref, coef_ref, history_ref, *refs):
    count = lay.domain
    waves_own, waves_other, old_own, old_other = (refs[i * count : (i + 1) * count] for i in range(4))
    image_ref, state = refs[4 * count :]
    clear_edges(state, lay)

    def store_now(row, part, ref, shift):
        for field in (0, 1):
            state[0, field, row + 1, TILE : TILE + lay.span, :] = ref[4 + field, part, pl.ds(shift, lay.span), :]

    def store_old(row, part, ref, shift):
        for field in (0, 1):
            state[1, field, row + 1, TILE : TILE + lay.span, :] = ref[field, part, pl.ds(shift, lay.span), :]

    gather_rows(info_ref, lay, waves_own, waves_other, store_now)
    gather_rows(info_ref, lay, old_own, old_other, store_old)
    image_ref[...] = jnp.zeros_like(image_ref)

    def after(step, row, lines, new_p):
        image_ref[row, lines, :] += history_ref[step, row, lines, :] * new_p

    run_steps(state, coef_ref, inject_ref, REC_Z, lay, after)


def call(kernel, lay, outs, scratch, info, *operands):
    vmem = pl.BlockSpec(memory_space=pltpu.VMEM)
    return pl.pallas_call(
        functools.partial(kernel, lay),
        out_shape=outs,
        in_specs=[pl.BlockSpec(memory_space=pltpu.SMEM)] + [vmem] * len(operands),
        out_specs=jax.tree.map(lambda unused: vmem, outs),
        scratch_shapes=scratch,
        compiler_params=pltpu.CompilerParams(vmem_limit_bytes=LIMIT),
    )(info, *operands)


def per_device(
    velocity,
    thomsen_eps,
    thomsen_delta,
    tilt_angle,
    azimuth,
    shot_anchor,
    source_x,
    source_y,
    wavelet,
    receiver_x,
    receiver_y,
    traces,
    source_now,
    source_before,
    receiver_now,
    receiver_before,
    slab_owner,
):
    rows, lines, z_count = source_now.shape[2:]
    steps = wavelet.shape[1]
    domain, shots = lax.axis_size("domain"), lax.axis_size("shot")
    lay = Layout(domain, shots, rows, lines, steps)
    d, s = lax.axis_index("domain"), lax.axis_index("shot")
    core = s & 1
    chip_id = lax.rem(d, lay.half)
    works_on = d // lay.half
    zero = jnp.int32(0)

    def send(pick):
        own, other = [], []
        for r, pairs in lay.rounds():
            k = lax.rem(d + r, domain)
            message = lax.ppermute(pick(k & 1, k >> 1), ("domain", "shot"), pairs)
            own.append(message)
            other.append(swapped(message, "shot", 1))
        return own + other

    def wave_pick(*fields):
        fields = [jnp.pad(field[0], ((0, 0), (0, 0), lay.pad, (0, 0))) for field in fields]

        def pick(c, kc):
            return jnp.concatenate(
                [
                    lax.dynamic_slice(
                        field,
                        (zero, c * lay.part, lay.start(kc), zero),
                        (2, lay.part, lay.chip, z_count),
                    )
                    for field in fields
                ]
            )

        return pick

    waves = send(wave_pick(source_now, source_before, receiver_now))

    model = jnp.stack([velocity, thomsen_eps, thomsen_delta, tilt_angle, azimuth])
    slab = model.shape[2]
    model = model[:, :, None]
    bit = shots // 2
    while bit:
        twin = swapped(model, "shot", bit)
        upper = (s & bit) != 0
        model = jnp.stack([jnp.where(upper, twin, model), jnp.where(upper, model, twin)], axis=3)
        model = model.reshape(model.shape[:2] + (-1,) + model.shape[4:])
        bit //= 2
    model = model.reshape(model.shape[:2] + (shots * slab, z_count))
    anchor = shot_anchor[0]
    if lay.pad != (0, 0):
        model = lax.dynamic_slice_in_dim(model, anchor, lines, 2)
        model = jnp.pad(model, ((0, 0), (0, 0), lay.pad, (0, 0)))
        first_line = zero
    else:
        first_line = anchor

    def model_pick(c, kc):
        return lax.dynamic_slice(
            model,
            (zero, c * lay.part, first_line + lay.start(kc), zero),
            (5, lay.part, lay.chip, z_count),
        )

    models = send(model_pick)
    olds = send(wave_pick(receiver_before))

    receivers = receiver_x.shape[1]
    mine = jnp.concatenate(
        [
            traces[0].reshape(-1),
            wavelet[0],
            receiver_x[0].astype(jnp.float32),
            receiver_y[0].astype(jnp.float32),
            source_x.astype(jnp.float32),
            source_y.astype(jnp.float32),
            shot_anchor.astype(jnp.float32),
        ]
    )
    twin = swapped(mine, "shot", 1)
    table = jnp.where(works_on == core, mine, twin)
    trace_rows = table[: steps * receivers].reshape(steps, receivers)
    at = steps * receivers
    wave_row = table[at : at + steps]
    at += steps
    rec_x = table[at : at + receivers].astype(jnp.int32)
    rec_y = table[at + receivers : at + 2 * receivers].astype(jnp.int32)
    at += 2 * receivers
    src_x, src_y = table[at].astype(jnp.int32), table[at + 1].astype(jnp.int32)
    twin_anchor = twin[at + 2].astype(jnp.int32)
    anchors = (jnp.where(core == 0, anchor, twin_anchor), jnp.where(core == 0, twin_anchor, anchor))

    window = lay.start(chip_id) + lay.shift(core) - lay.pad[0]
    row_ids = jnp.arange(lay.width)
    line_ids = window + jnp.arange(lay.span)
    spread = ((0, 0), (0, 0), (0, z_count - steps))
    spot = (row_ids[:, None] == src_x) & (line_ids[None, :] == src_y)
    source_pulse = jnp.where(spot[:, :, None], wave_row[None, None, :], 0.0)
    receiver_pulse = jnp.einsum(
        "yr,xtr->xyt",
        (line_ids[:, None] == rec_y[None, :]).astype(jnp.float32),
        jnp.where((row_ids[:, None] == rec_x[None, :])[:, None, :], trace_rows[None], 0.0),
        precision=lax.Precision.HIGHEST,
        preferred_element_type=jnp.float32,
    )
    source_pulse = jnp.pad(source_pulse, spread)
    receiver_pulse = jnp.pad(receiver_pulse, spread)

    info = jnp.stack([chip_id, core, lay.shift(core)]).astype(jnp.int32)
    block = (lay.width, lay.span, z_count)
    state = pltpu.VMEM((2, 2, lay.width + 2, lay.span + 2 * TILE, z_count), jnp.float32)
    coefs, history = call(
        source_kernel,
        lay,
        [jax.ShapeDtypeStruct((COEFS,) + block, jnp.float32), jax.ShapeDtypeStruct((steps,) + block, jnp.float32)],
        [pltpu.VMEM((5,) + block, jnp.float32), state],
        info,
        source_pulse,
        *waves,
        *models,
    )
    image = call(
        receiver_kernel,
        lay,
        jax.ShapeDtypeStruct(block, jnp.float32),
        [state],
        info,
        receiver_pulse,
        coefs,
        history,
        *waves,
        *olds,
    )

    skip = (2 * chip_id + core) * lay.own - window
    frame = jnp.zeros((rows, shots * slab, z_count), jnp.float32)
    for r in range(domain):
        piece = lax.dynamic_slice(
            image, (lax.rem(d + r, domain) * rows, skip, zero), (rows, lay.own, z_count)
        )
        if r:
            piece = lax.ppermute(piece, "domain", [(i, (i + r) % domain) for i in range(domain)])
        source = lax.rem(d - r + domain, domain)
        place = jnp.where(source < lay.half, anchors[0], anchors[1])
        place = place + (2 * lax.rem(source, lay.half) + core) * lay.own
        spot = (zero, place, zero)
        frame = lax.dynamic_update_slice(
            frame, piece + lax.dynamic_slice(frame, spot, piece.shape), spot
        )
    total = 0.0
    for r in range(shots):
        part = lax.dynamic_slice_in_dim(frame, slab_owner[s ^ r] * slab, slab, 1)
        total = total + (swapped(part, "shot", r) if r else part)
    return total / steps


def solution(mesh):
    in_specs = (
        P(("groups", "domain"), "shot", None),
        P(("groups", "domain"), "shot", None),
        P(("groups", "domain"), "shot", None),
        P(("groups", "domain"), "shot", None),
        P(("groups", "domain"), "shot", None),
        P(("groups", "shot")),
        P(("groups", "shot")),
        P(("groups", "shot")),
        P(("groups", "shot"), None),
        P(("groups", "shot"), None),
        P(("groups", "shot"), None),
        P(("groups", "shot"), None, None),
        P(("groups", "shot"), None, "domain", None, None),
        P(("groups", "shot"), None, "domain", None, None),
        P(("groups", "shot"), None, "domain", None, None),
        P(("groups", "shot"), None, "domain", None, None),
        P("groups"),
    )
    out_specs = P(("groups", "domain"), "shot", None)
    return jax.shard_map(
        per_device, mesh=mesh, in_specs=in_specs, out_specs=out_specs, check_vma=False
    )
```

time: 442 us -> 130 us (0.29)
  other arithmetic: 240 us -> 5.02 us
  local copies, waits for them, and re-layouts: 73.6 us -> 10.6 us
  waiting for transfers between devices: 52.2 us -> 28.7 us
  Pallas kernels: 0 us -> 20.6 us
  between operations: 14.2 us -> 7.19 us
    another operation x48 -> x4, other arithmetic: 157 us -> 1.68 us  [the longest x3 1.6 us: per_device(): jnp.stack([jnp.where(upper, twin, model), jnp.where(upper, model, twin)],...]
    concatenate x9 -> x4, other arithmetic: 37.9 us -> 2.25 us  [pick(): jnp.concatenate([lax.dynamic_slice(field, (zero, c * lay.part, lay.start(...]
    reduce_scatter x1 -> x0, waiting for transfers between devices: 23 us -> none  [per_device(): summed = lax.psum_scatter(ordered, 'shot', scatter_dimension=1, tiled=True)]
    pallas_call x0 -> x2, Pallas kernels: none -> 20.6 us  [call(): pl.pallas_call(functools.partial(kernel, lay), out_shape=outs, in_specs=[...]
    all_gather x1 -> x0, waiting for transfers between devices: 18.1 us -> none  [per_device(): whole_model = lax.all_gather(model_share, 'shot', axis=2, tiled=True)]
    ppermute x16 -> x33, waiting for transfers between devices: 11.1 us -> 28.7 us  [the longest x12 22.7 us: send(): message = lax.ppermute(pick(k & 1, k >> 1), ('domain', 'shot'), pairs)]
    while x121 -> x0, local copies, waits for them, and re-layouts: 16 us -> none
    scatter-add x16 -> x0, other arithmetic: 15.2 us -> none  [the longest x8 15.1 us: inject(): updated.at[0:2, :, :, SRC_Z]]
  transfers between devices with their start and end apart: 18 -> 33, of which waited for: 11 -> 8; matrix products, arithmetic and copies ran while one was open for 14% -> 8% of each run, Pallas kernels for 0% -> 9%
where the time goes in v1:
time: 130 us
  starting transfers between devices  57.1 us (44%)
  waiting for transfers between devices  28.7 us (22%)
  Pallas kernels  20.6 us (16%)
  local copies, waits for them, and re-layouts  10.6 us (8%)
  between operations  7.19 us (6%)
  other arithmetic  5.02 us (4%)
    ppermute x12, starting transfers between devices, send(): message = lax.ppermute(pick(k & 1, k >> 1), ('domain', 'shot'), pairs)  39.9 us
    ppermute x12, waiting for transfers between devices, send(): message = lax.ppermute(pick(k & 1, k >> 1), ('domain', 'shot'), pairs)  22.7 us
    pallas_call x2, Pallas kernels, call(): pl.pallas_call(functools.partial(kernel, lay), out_shape=outs, in_specs=[...  20.6 us
    ppermute x18, starting transfers between devices, swapped(): return lax.ppermute(value, axis, [(i, i ^ bit) for i in range(count)])  13.2 us
    ppermute x18, waiting for transfers between devices, swapped(): return lax.ppermute(value, axis, [(i, i ^ bit) for i in range(count)])  4.4 us
    unnamed x21, local copies, waits for them, and re-layouts  3.98 us
    ppermute x3, starting transfers between devices, per_device(): lax.ppermute(piece, 'domain', [(i, (i + r) % domain) for i in range(domai...  3.93 us
  transfers between devices with their start and end apart: 33, of which 8 were waited for; matrix products, arithmetic and copies ran while one was open for 8% of the time, Pallas kernels for 9%

profile of v1, /device:TPU:0, one launch (start us, length us, event | category | flops | bytes accessed | tf_op | source)
XLA Modules:
  0.0 129.7 jit_solution(17555133319248550286)
XLA Ops:
  0.0 1.0 bitcast_dynamic-update-slice_fusion.4
  1.0 0.9 bitcast_dynamic-update-slice_fusion.3
  1.9 0.9 bitcast_dynamic-update-slice_fusion.2
  2.8 0.9 bitcast_dynamic-update-slice_fusion.1
  3.7 0.9 bitcast_dynamic-update-slice_fusion
  4.6 2.9 %collective-permute-start.9 = (f32[5,2,1,96,128]{4,3,1,0,2:T(8,128)S(1)}, f32[5,2,1,96,128]{4,3,1,0,2:T(8,128)S(1)}, u32[]{:S(2)}, u32[]{:S(2)}) collective-permute-start(f32[5,2,1,96,128]{4,3,1,0,2:T(8,128)S(1)} %bitcast.88), channel_id=1, source_target_pairs={{0,2},{1,3},{2,0},{3,1},{4,6},{5,7},{6,4},{7,5},{8,10},{9,11},{10,... | collective-permute-start | bytes 1474568 | tf_op jit(solution)/shard_map/ppermute | solution.py:58
  7.5 1.3 %dynamic-slice_bitcast_fusion.4 = (f32[2,1,104,128]{3,2,1,0:T(8,128)S(1)}, f32[2,1,104,128]{3,2,1,0:T(8,128)S(1)}, f32[2,1,104,128]{3,2,1,0:T(8,128)S(1)}, f32[2...) fusion(f32[1,2,2,192,128]{4,3,2,1,0:T(8,128)} %param.31, ...), kind=kLoop, calls=%fused_computation.16 | loop fusion | bytes 1703968 | tf_op jit(solution)/shard_map/dynamic_slice | solution.py:293
  9.6 1.6 %collective-permute-start.3 = (f32[6,1,104,128]{3,2,1,0:T(8,128)}, f32[6,1,104,128]{3,2,1,0:T(8,128)S(1)}, u32[]{:S(2)}, u32[]{:S(2)}) collective-permute-start(f32[6,1,104,128]{3,2,1,0:T(8,128)} %pad_maximum_fusion.3), channel_id=1, source_target_pairs={{0,4},{1,12},{2,6},{3,14},{4,5},{5,13},{6,7},{7,15},{8,0},{9,8},{1... | collective-permute-start | bytes 958472 | tf_op jit(solution)/shard_map/ppermute | solution.py:282
  12.0 3.4 %collective-permute-start.4 = (f32[6,1,104,128]{3,2,1,0:T(8,128)}, f32[6,1,104,128]{3,2,1,0:T(8,128)S(1)}, u32[]{:S(2)}, u32[]{:S(2)}) collective-permute-start(f32[6,1,104,128]{3,2,1,0:T(8,128)} %pad_maximum_fusion.4), channel_id=1, source_target_pairs={{0,5},{1,13},{2,7},{3,15},{4,0},{5,8},{6,2},{7,10},{8,1},{9,9},{10... | collective-permute-start | bytes 958472 | tf_op jit(solution)/shard_map/ppermute | solution.py:282
  15.4 2.6 %collective-permute-start.2 = (f32[6,1,104,128]{3,2,1,0:T(8,128)S(1)}, f32[6,1,104,128]{3,2,1,0:T(8,128)S(1)}, u32[]{:S(2)}, u32[]{:S(2)}) collective-permute-start(f32[6,1,104,128]{3,2,1,0:T(8,128)S(1)} %pad_maximum_fusion.2), channel_id=1, source_target_pairs={{0,1},{1,9},{2,3},{3,11},{4,4},{5,12},{6,6},{7,14},{8,5},{9,13},{1... | collective-permute-start | bytes 958472 | tf_op jit(solution)/shard_map/ppermute | solution.py:282
  21.8 0.7 dynamic-slice_bitcast_fusion
  22.7 1.6 %collective-permute-start.19 = (f32[2,1,104,128]{3,2,1,0:T(8,128)}, f32[2,1,104,128]{3,2,1,0:T(8,128)S(1)}, u32[]{:S(2)}, u32[]{:S(2)}) collective-permute-start(f32[2,1,104,128]{3,2,1,0:T(8,128)} %get-tuple-element.22), channel_id=1, source_target_pairs={{0,0},{1,8},{2,2},{3,10},{4,1},{5,9},{6,3},{7,11},{8,4},{9,12},{10... | collective-permute-start | bytes 319496 | tf_op jit(solution)/shard_map/ppermute | solution.py:282
  24.4 1.6 %collective-permute-start.1 = (f32[6,1,104,128]{3,2,1,0:T(8,128)}, f32[6,1,104,128]{3,2,1,0:T(8,128)S(1)}, u32[]{:S(2)}, u32[]{:S(2)}) collective-permute-start(f32[6,1,104,128]{3,2,1,0:T(8,128)} %pad_maximum_fusion.1), channel_id=1, source_target_pairs={{0,0},{1,8},{2,2},{3,10},{4,1},{5,9},{6,3},{7,11},{8,4},{9,12},{10... | collective-permute-start | bytes 958472 | tf_op jit(solution)/shard_map/ppermute | solution.py:282
  26.0 14.9 %collective-permute-start.20 = (f32[2,1,104,128]{3,2,1,0:T(8,128)}, f32[2,1,104,128]{3,2,1,0:T(8,128)S(1)}, u32[]{:S(2)}, u32[]{:S(2)}) collective-permute-start(f32[2,1,104,128]{3,2,1,0:T(8,128)} %get-tuple-element.21), channel_id=1, source_target_pairs={{0,1},{1,9},{2,3},{3,11},{4,4},{5,12},{6,6},{7,14},{8,5},{9,13},{1... | collective-permute-start | bytes 319496 | tf_op jit(solution)/shard_map/ppermute | solution.py:282
  41.0 1.1 collective-permute-start.7
  42.0 1.4 %select_bitcast_fusion.1 = (f32[5,2,2,1,96,128]{5,4,1,0,2,3:T(8,128)S(1)}, f32[5,2,2,1,96,128]{5,4,1,0,2,3:T(8,128)S(1)}) fusion(f32[5,2,2,96,128]{4,3,1,0,2:T(8,128)} %collective-permute-done.10, pred[]{:T(512)S(6)} %ne.16, f32[5,2,1,1,96,128]{5,4,1,0,3,2:T(8,128)S(1)} %get-tuple-element.16, f32[5,2,1,1,96,128]{5,4,1,0,3,2:T(8,128)S(1)} %get-tuple-element.15), kind=kLoop, calls=%fused_computation.4 | loop fusion | flops 737280 | bytes 3932161 | tf_op jit(solution)/shard_map/stack | solution.py:313
  43.4 4.6 %collective-permute-done.20.refs_9_ = f32[2,1,104,128]{3,2,1,0:T(8,128)S(1)} collective-permute-done((f32[2,1,104,128]{3,2,1,0:T(8,128)}, f32[2,1,104,128]{3,2,1,0:T(8,128)S(1)}, u32[]{:S(2)}, u32[]{:S(2)}) %collective-permute-start.20) | collective-permute-done | bytes 106528 | tf_op jit(solution)/shard_map/ppermute | solution.py:282
  48.3 5.5 %collective-permute-done.21.refs_10_ = f32[2,1,104,128]{3,2,1,0:T(8,128)S(1)} collective-permute-done((f32[2,1,104,128]{3,2,1,0:T(8,128)S(1)}, f32[2,1,104,128]{3,2,1,0:T(8,128)S(1)}, u32[]{:S(2)}, u32[]{:S(2)}) %collective-permute-start.21) | collective-permute-done | bytes 106528 | tf_op jit(solution)/shard_map/ppermute | solution.py:282
  53.8 1.9 %collective-permute-start.22 = (f32[2,1,104,128]{3,2,1,0:T(8,128)S(1)}, f32[2,1,104,128]{3,2,1,0:T(8,128)S(1)}, u32[]{:S(2)}, u32[]{:S(2)}) collective-permute-start(f32[2,1,104,128]{3,2,1,0:T(8,128)S(1)} %get-tuple-element.20), channel_id=1, source_target_pairs={{0,5},{1,13},{2,7},{3,15},{4,0},{5,8},{6,2},{7,10},{8,1},{9,9},{10... | collective-permute-start | bytes 319496 | tf_op jit(solution)/shard_map/ppermute | solution.py:282
  55.7 2.3 %collective-permute-start.8 = (f32[6,1,104,128]{3,2,1,0:T(8,128)S(1)}, f32[6,1,104,128]{3,2,1,0:T(8,128)S(1)}, u32[]{:S(2)}, u32[]{:S(2)}) collective-permute-start(f32[6,1,104,128]{3,2,1,0:T(8,128)S(1)} %collective-permute-done.4.refs_3_), channel_id=1, source_target_pairs={{0,1},{1,0},{2,3},{3,2},{4,5},{5,4},{6,7},{7,6},{8,9},{9,8},{10,11... | collective-permute-start | bytes 958472 | tf_op jit(solution)/shard_map/ppermute | solution.py:58
  58.2 2.2 %collective-permute-done.22.refs_11_ = f32[2,1,104,128]{3,2,1,0:T(8,128)S(1)} collective-permute-done((f32[2,1,104,128]{3,2,1,0:T(8,128)S(1)}, f32[2,1,104,128]{3,2,1,0:T(8,128)S(1)}, u32[]{:S(2)}, u32[]{:S(2)}) %collective-permute-start.22) | collective-permute-done | bytes 106528 | tf_op jit(solution)/shard_map/ppermute | solution.py:282
  61.1 6.2 %collective-permute-start.12 = (f32[5,1,104,128]{3,2,1,0:T(8,128)S(1)}, f32[5,1,104,128]{3,2,1,0:T(8,128)S(1)}, u32[]{:S(2)}, u32[]{:S(2)}) collective-permute-start(f32[5,1,104,128]{3,2,1,0:T(8,128)S(1)} %get-tuple-element.11), channel_id=1, source_target_pairs={{0,1},{1,9},{2,3},{3,11},{4,4},{5,12},{6,6},{7,14},{8,5},{9,13},{1... | collective-permute-start | bytes 798728 | tf_op jit(solution)/shard_map/ppermute | solution.py:282
  68.2 5.0 %collective-permute-start.14 = (f32[5,1,104,128]{3,2,1,0:T(8,128)S(1)}, f32[5,1,104,128]{3,2,1,0:T(8,128)S(1)}, u32[]{:S(2)}, u32[]{:S(2)}) collective-permute-start(f32[5,1,104,128]{3,2,1,0:T(8,128)S(1)} %get-tuple-element.9), channel_id=1, source_target_pairs={{0,5},{1,13},{2,7},{3,15},{4,0},{5,8},{6,2},{7,10},{8,1},{9,9},{10... | collective-permute-start | bytes 798728 | tf_op jit(solution)/shard_map/ppermute | solution.py:282
  75.9 10.5 %collective-permute-done.13.refs_10_ = f32[5,1,104,128]{3,2,1,0:T(8,128)S(1)} collective-permute-done((f32[5,1,104,128]{3,2,1,0:T(8,128)S(1)}, f32[5,1,104,128]{3,2,1,0:T(8,128)S(1)}, u32[]{:S(2)}, u32[]{:S(2)}) %collective-permute-start.13) | collective-permute-done | bytes 266272 | tf_op jit(solution)/shard_map/ppermute | solution.py:282
  86.4 2.7 %collective-permute-start.18 = (f32[5,1,104,128]{3,2,1,0:T(8,128)S(1)}, f32[5,1,104,128]{3,2,1,0:T(8,128)S(1)}, u32[]{:S(2)}, u32[]{:S(2)}) collective-permute-start(f32[5,1,104,128]{3,2,1,0:T(8,128)S(1)} %collective-permute-done.14.refs_11_), channel_id=1, source_target_pairs={{0,1},{1,0},{2,3},{3,2},{4,5},{5,4},{6,7},{7,6},{8,9},{9,8},{10,11... | collective-permute-start | bytes 798728 | tf_op jit(solution)/shard_map/ppermute | solution.py:58
  90.4 11.8 %shard_map.163 = (f32[16,8,64,128]{3,2,1,0:T(8,128)S(1)}, f32[8,8,64,128]{3,2,1,0:T(8,128)S(1)}) custom-call(s32[3]{0:T(128)S(1)} %pad_add_fusion.info_ref, f32[8,64,128]{2,1,0:T(8,128)S(1)} %pad.8.inject_ref, f32[6,1,104,128]{3,2,1,0:T(8,128)S(1)} %collective-permute-done.1.refs_0_, f32[6,1,104,128]{3,2,1,0:T(8,128)S(1)} %collective-permute-done.2.refs_1_, ...), custom_call_target="tpu_custom_call" | custom-call | tf_op jit(solution)/shard_map/pallas_call | solution.py:239
  102.3 8.9 %shard_map.164 = f32[8,64,128]{2,1,0:T(8,128)S(1)} custom-call(s32[3]{0:T(128)S(1)} %pad_add_fusion.info_ref, f32[8,64,128]{2,1,0:T(8,128)S(1)} %pad.7.inject_ref, f32[16,8,64,128]{3,2,1,0:T(8,128)S(1)} %get-tuple-element.7.coef_ref, f32[8,8,64,128]{3,2,1,0:T(8,128)S(1)} %get-tuple-element.8.history_ref, ...), custom_call_target="tpu_custom_call" | custom-call | tf_op jit(solution)/shard_map/pallas_call | solution.py:239
  115.5 3.6 %collective-permute-start.29 = (f32[2,48,128]{2,1,0:T(8,128)S(1)}, f32[2,48,128]{2,1,0:T(8,128)S(1)}, u32[]{:S(2)}, u32[]{:S(2)}) collective-permute-start(f32[2,48,128]{2,1,0:T(8,128)S(1)} %get-tuple-element.36), channel_id=1, source_target_pairs={{0,12},{4,0},{8,4},{12,8},{1,13},{5,1},{9,5},{13,9},{2,14},{6,2},{... | collective-permute-start | bytes 147464 | tf_op jit(solution)/shard_map/ppermute | solution.py:409
  119.8 1.3 collective-permute-done.28
  122.3 1.6 %collective-permute-start.32 = (f32[2,96,128]{2,1,0:T(8,128)S(1)}, f32[2,96,128]{2,1,0:T(8,128)S(1)}, u32[]{:S(2)}, u32[]{:S(2)}) collective-permute-start(f32[2,96,128]{2,1,0:T(8,128)S(1)} %get-tuple-element.18), channel_id=1, source_target_pairs={{0,3},{1,2},{2,1},{3,0},{4,7},{5,6},{6,5},{7,4},{8,11},{9,10},{10,... | collective-permute-start | bytes 294920 | tf_op jit(solution)/shard_map/ppermute | solution.py:58
  124.6 3.2 %collective-permute-done.31 = f32[2,96,128]{2,1,0:T(8,128)S(1)} collective-permute-done((f32[2,96,128]{2,1,0:T(8,128)S(1)}, f32[2,96,128]{2,1,0:T(8,128)S(1)}, u32[]{:S(2)}, u32[]{:S(2)}) %collective-permute-start.31) | collective-permute-done | bytes 98336 | tf_op jit(solution)/shard_map/ppermute | solution.py:58
  127.8 1.2 collective-permute-done.32
  (103 shorter events, 12.5 us)
Async XLA Ops:
  4.6 16.3 %collective-permute-start.9 = (f32[5,2,1,96,128]{4,3,1,0,2:T(8,128)S(1)}, f32[5,2,1,96,128]{4,3,1,0,2:T(8,128)S(1)}, u32[]{:S(2)}, u32[]{:S(2)}) collective-permute-start(f32[5,2,1,96,128]{4,3,1,0,2:T(8,128)S(1)} %bitcast.88), channel_id=1, source_target_pairs={{0,2},{1,3},{2,0},{3,1},{4,6},{5,7},{6,4},{7,5},{8,10},{9,11},{10,... | collective-permute-start | bytes 1474568 | tf_op jit(solution)/shard_map/ppermute | solution.py:58
  9.6 16.4 %collective-permute-start.3 = (f32[6,1,104,128]{3,2,1,0:T(8,128)}, f32[6,1,104,128]{3,2,1,0:T(8,128)S(1)}, u32[]{:S(2)}, u32[]{:S(2)}) collective-permute-start(f32[6,1,104,128]{3,2,1,0:T(8,128)} %pad_maximum_fusion.3), channel_id=1, source_target_pairs={{0,4},{1,12},{2,6},{3,14},{4,5},{5,13},{6,7},{7,15},{8,0},{9,8},{1... | collective-permute-start | bytes 958472 | tf_op jit(solution)/shard_map/ppermute | solution.py:282
  12.0 43.7 %collective-permute-start.4 = (f32[6,1,104,128]{3,2,1,0:T(8,128)}, f32[6,1,104,128]{3,2,1,0:T(8,128)S(1)}, u32[]{:S(2)}, u32[]{:S(2)}) collective-permute-start(f32[6,1,104,128]{3,2,1,0:T(8,128)} %pad_maximum_fusion.4), channel_id=1, source_target_pairs={{0,5},{1,13},{2,7},{3,15},{4,0},{5,8},{6,2},{7,10},{8,1},{9,9},{10... | collective-permute-start | bytes 958472 | tf_op jit(solution)/shard_map/ppermute | solution.py:282
  15.4 42.8 %collective-permute-start.2 = (f32[6,1,104,128]{3,2,1,0:T(8,128)S(1)}, f32[6,1,104,128]{3,2,1,0:T(8,128)S(1)}, u32[]{:S(2)}, u32[]{:S(2)}) collective-permute-start(f32[6,1,104,128]{3,2,1,0:T(8,128)S(1)} %pad_maximum_fusion.2), channel_id=1, source_target_pairs={{0,1},{1,9},{2,3},{3,11},{4,4},{5,12},{6,6},{7,14},{8,5},{9,13},{1... | collective-permute-start | bytes 958472 | tf_op jit(solution)/shard_map/ppermute | solution.py:282
  20.1 2.6 %collective-permute-start = (f32[2571]{0:T(1024)S(1)}, f32[2571]{0:T(1024)S(1)}, u32[]{:S(2)}, u32[]{:S(2)}) collective-permute-start(f32[2571]{0:T(1024)S(1)} %concatenate.15), channel_id=1, source_target_pairs={{0,1},{1,0},{2,3},{3,2},{4,5},{5,4},{6,7},{7,6},{8,9},{9,8},{10,11... | collective-permute-start | bytes 30860 | tf_op jit(solution)/shard_map/ppermute | solution.py:58
  21.0 20.0 %collective-permute-start.10 = (f32[5,2,2,96,128]{4,3,1,0,2:T(8,128)S(1)}, f32[5,2,2,96,128]{4,3,1,0,2:T(8,128)}, u32[]{:S(2)}, u32[]{:S(2)}) collective-permute-start(f32[5,2,2,96,128]{4,3,1,0,2:T(8,128)S(1)} %maximum_bitcast_fusion), channel_id=1, source_target_pairs={{0,1},{1,0},{2,3},{3,2},{4,5},{5,4},{6,7},{7,6},{8,9},{9,8},{10,11... | collective-permute-start | bytes 2949128 | tf_op jit(solution)/shard_map/ppermute | solution.py:58
  24.4 36.7 %collective-permute-start.1 = (f32[6,1,104,128]{3,2,1,0:T(8,128)}, f32[6,1,104,128]{3,2,1,0:T(8,128)S(1)}, u32[]{:S(2)}, u32[]{:S(2)}) collective-permute-start(f32[6,1,104,128]{3,2,1,0:T(8,128)} %pad_maximum_fusion.1), channel_id=1, source_target_pairs={{0,0},{1,8},{2,2},{3,10},{4,1},{5,9},{6,3},{7,11},{8,4},{9,12},{10... | collective-permute-start | bytes 958472 | tf_op jit(solution)/shard_map/ppermute | solution.py:282
  26.0 22.0 %collective-permute-start.20 = (f32[2,1,104,128]{3,2,1,0:T(8,128)}, f32[2,1,104,128]{3,2,1,0:T(8,128)S(1)}, u32[]{:S(2)}, u32[]{:S(2)}) collective-permute-start(f32[2,1,104,128]{3,2,1,0:T(8,128)} %get-tuple-element.21), channel_id=1, source_target_pairs={{0,1},{1,9},{2,3},{3,11},{4,4},{5,12},{6,6},{7,14},{8,5},{9,13},{1... | collective-permute-start | bytes 319496 | tf_op jit(solution)/shard_map/ppermute | solution.py:282
  41.0 26.3 %collective-permute-start.7 = (f32[6,1,104,128]{3,2,1,0:T(8,128)S(1)}, f32[6,1,104,128]{3,2,1,0:T(8,128)S(1)}, u32[]{:S(2)}, u32[]{:S(2)}) collective-permute-start(f32[6,1,104,128]{3,2,1,0:T(8,128)S(1)} %collective-permute-done.3.refs_2_), channel_id=1, source_target_pairs={{0,1},{1,0},{2,3},{3,2},{4,5},{5,4},{6,7},{7,6},{8,9},{9,8},{10,11... | collective-permute-start | bytes 958472 | tf_op jit(solution)/shard_map/ppermute | solution.py:58
  48.0 5.8 %collective-permute-start.21 = (f32[2,1,104,128]{3,2,1,0:T(8,128)S(1)}, f32[2,1,104,128]{3,2,1,0:T(8,128)S(1)}, u32[]{:S(2)}, u32[]{:S(2)}) collective-permute-start(f32[2,1,104,128]{3,2,1,0:T(8,128)S(1)} %copy-done.2), channel_id=1, source_target_pairs={{0,4},{1,12},{2,6},{3,14},{4,5},{5,13},{6,7},{7,15},{8,0},{9,8},{1... | collective-permute-start | bytes 319496 | tf_op jit(solution)/shard_map/ppermute | solution.py:282
  53.8 6.6 %collective-permute-start.22 = (f32[2,1,104,128]{3,2,1,0:T(8,128)S(1)}, f32[2,1,104,128]{3,2,1,0:T(8,128)S(1)}, u32[]{:S(2)}, u32[]{:S(2)}) collective-permute-start(f32[2,1,104,128]{3,2,1,0:T(8,128)S(1)} %get-tuple-element.20), channel_id=1, source_target_pairs={{0,5},{1,13},{2,7},{3,15},{4,0},{5,8},{6,2},{7,10},{8,1},{9,9},{10... | collective-permute-start | bytes 319496 | tf_op jit(solution)/shard_map/ppermute | solution.py:282
  55.7 12.5 %collective-permute-start.8 = (f32[6,1,104,128]{3,2,1,0:T(8,128)S(1)}, f32[6,1,104,128]{3,2,1,0:T(8,128)S(1)}, u32[]{:S(2)}, u32[]{:S(2)}) collective-permute-start(f32[6,1,104,128]{3,2,1,0:T(8,128)S(1)} %collective-permute-done.4.refs_3_), channel_id=1, source_target_pairs={{0,1},{1,0},{2,3},{3,2},{4,5},{5,4},{6,7},{7,6},{8,9},{9,8},{10,11... | collective-permute-start | bytes 958472 | tf_op jit(solution)/shard_map/ppermute | solution.py:58
  58.1 17.1 %collective-permute-start.6 = (f32[6,1,104,128]{3,2,1,0:T(8,128)S(1)}, f32[6,1,104,128]{3,2,1,0:T(8,128)S(1)}, u32[]{:S(2)}, u32[]{:S(2)}) collective-permute-start(f32[6,1,104,128]{3,2,1,0:T(8,128)S(1)} %collective-permute-done.2.refs_1_), channel_id=1, source_target_pairs={{0,1},{1,0},{2,3},{3,2},{4,5},{5,4},{6,7},{7,6},{8,9},{9,8},{10,11... | collective-permute-start | bytes 958472 | tf_op jit(solution)/shard_map/ppermute | solution.py:58
  60.4 14.9 %collective-permute-start.11 = (f32[5,1,104,128]{3,2,1,0:T(8,128)S(1)}, f32[5,1,104,128]{3,2,1,0:T(8,128)S(1)}, u32[]{:S(2)}, u32[]{:S(2)}) collective-permute-start(f32[5,1,104,128]{3,2,1,0:T(8,128)S(1)} %get-tuple-element.12), channel_id=1, source_target_pairs={{0,0},{1,8},{2,2},{3,10},{4,1},{5,9},{6,3},{7,11},{8,4},{9,12},{10... | collective-permute-start | bytes 798728 | tf_op jit(solution)/shard_map/ppermute | solution.py:282
  61.1 14.7 %collective-permute-start.12 = (f32[5,1,104,128]{3,2,1,0:T(8,128)S(1)}, f32[5,1,104,128]{3,2,1,0:T(8,128)S(1)}, u32[]{:S(2)}, u32[]{:S(2)}) collective-permute-start(f32[5,1,104,128]{3,2,1,0:T(8,128)S(1)} %get-tuple-element.11), channel_id=1, source_target_pairs={{0,1},{1,9},{2,3},{3,11},{4,4},{5,12},{6,6},{7,14},{8,5},{9,13},{1... | collective-permute-start | bytes 798728 | tf_op jit(solution)/shard_map/ppermute | solution.py:282
  67.3 19.1 %collective-permute-start.13 = (f32[5,1,104,128]{3,2,1,0:T(8,128)S(1)}, f32[5,1,104,128]{3,2,1,0:T(8,128)S(1)}, u32[]{:S(2)}, u32[]{:S(2)}) collective-permute-start(f32[5,1,104,128]{3,2,1,0:T(8,128)S(1)} %get-tuple-element.10), channel_id=1, source_target_pairs={{0,4},{1,12},{2,6},{3,14},{4,5},{5,13},{6,7},{7,15},{8,0},{9,8},{1... | collective-permute-start | bytes 798728 | tf_op jit(solution)/shard_map/ppermute | solution.py:282
  68.2 18.2 %collective-permute-start.14 = (f32[5,1,104,128]{3,2,1,0:T(8,128)S(1)}, f32[5,1,104,128]{3,2,1,0:T(8,128)S(1)}, u32[]{:S(2)}, u32[]{:S(2)}) collective-permute-start(f32[5,1,104,128]{3,2,1,0:T(8,128)S(1)} %get-tuple-element.9), channel_id=1, source_target_pairs={{0,5},{1,13},{2,7},{3,15},{4,0},{5,8},{6,2},{7,10},{8,1},{9,9},{10... | collective-permute-start | bytes 798728 | tf_op jit(solution)/shard_map/ppermute | solution.py:282
  75.2 13.9 %collective-permute-start.5 = (f32[6,1,104,128]{3,2,1,0:T(8,128)S(1)}, f32[6,1,104,128]{3,2,1,0:T(8,128)S(1)}, u32[]{:S(2)}, u32[]{:S(2)}) collective-permute-start(f32[6,1,104,128]{3,2,1,0:T(8,128)S(1)} %collective-permute-done.1.refs_0_), channel_id=1, source_target_pairs={{0,1},{1,0},{2,3},{3,2},{4,5},{5,4},{6,7},{7,6},{8,9},{9,8},{10,11... | collective-permute-start | bytes 958472 | tf_op jit(solution)/shard_map/ppermute | solution.py:58
  75.3 13.9 %collective-permute-start.15 = (f32[5,1,104,128]{3,2,1,0:T(8,128)S(1)}, f32[5,1,104,128]{3,2,1,0:T(8,128)S(1)}, u32[]{:S(2)}, u32[]{:S(2)}) collective-permute-start(f32[5,1,104,128]{3,2,1,0:T(8,128)S(1)} %collective-permute-done.11.refs_8_), channel_id=1, source_target_pairs={{0,1},{1,0},{2,3},{3,2},{4,5},{5,4},{6,7},{7,6},{8,9},{9,8},{10,11... | collective-permute-start | bytes 798728 | tf_op jit(solution)/shard_map/ppermute | solution.py:58
  75.8 13.9 %collective-permute-start.16 = (f32[5,1,104,128]{3,2,1,0:T(8,128)S(1)}, f32[5,1,104,128]{3,2,1,0:T(8,128)S(1)}, u32[]{:S(2)}, u32[]{:S(2)}) collective-permute-start(f32[5,1,104,128]{3,2,1,0:T(8,128)S(1)} %collective-permute-done.12.refs_9_), channel_id=1, source_target_pairs={{0,1},{1,0},{2,3},{3,2},{4,5},{5,4},{6,7},{7,6},{8,9},{9,8},{10,11... | collective-permute-start | bytes 798728 | tf_op jit(solution)/shard_map/ppermute | solution.py:58
  86.4 3.4 %collective-permute-start.17 = (f32[5,1,104,128]{3,2,1,0:T(8,128)S(1)}, f32[5,1,104,128]{3,2,1,0:T(8,128)S(1)}, u32[]{:S(2)}, u32[]{:S(2)}) collective-permute-start(f32[5,1,104,128]{3,2,1,0:T(8,128)S(1)} %collective-permute-done.13.refs_10_), channel_id=1, source_target_pairs={{0,1},{1,0},{2,3},{3,2},{4,5},{5,4},{6,7},{7,6},{8,9},{9,8},{10,11... | collective-permute-start | bytes 798728 | tf_op jit(solution)/shard_map/ppermute | solution.py:58
  86.4 4.0 %collective-permute-start.18 = (f32[5,1,104,128]{3,2,1,0:T(8,128)S(1)}, f32[5,1,104,128]{3,2,1,0:T(8,128)S(1)}, u32[]{:S(2)}, u32[]{:S(2)}) collective-permute-start(f32[5,1,104,128]{3,2,1,0:T(8,128)S(1)} %collective-permute-done.14.refs_11_), channel_id=1, source_target_pairs={{0,1},{1,0},{2,3},{3,2},{4,5},{5,4},{6,7},{7,6},{8,9},{9,8},{10,11... | collective-permute-start | bytes 798728 | tf_op jit(solution)/shard_map/ppermute | solution.py:58
  89.2 13.1 %collective-permute-start.23 = (f32[2,1,104,128]{3,2,1,0:T(8,128)S(1)}, f32[2,1,104,128]{3,2,1,0:T(8,128)S(1)}, u32[]{:S(2)}, u32[]{:S(2)}) collective-permute-start(f32[2,1,104,128]{3,2,1,0:T(8,128)S(1)} %collective-permute-done.19.refs_8_), channel_id=1, source_target_pairs={{0,1},{1,0},{2,3},{3,2},{4,5},{5,4},{6,7},{7,6},{8,9},{9,8},{10,11... | collective-permute-start | bytes 319496 | tf_op jit(solution)/shard_map/ppermute | solution.py:58
  89.2 13.0 %collective-permute-start.24 = (f32[2,1,104,128]{3,2,1,0:T(8,128)S(1)}, f32[2,1,104,128]{3,2,1,0:T(8,128)S(1)}, u32[]{:S(2)}, u32[]{:S(2)}) collective-permute-start(f32[2,1,104,128]{3,2,1,0:T(8,128)S(1)} %collective-permute-done.20.refs_9_), channel_id=1, source_target_pairs={{0,1},{1,0},{2,3},{3,2},{4,5},{5,4},{6,7},{7,6},{8,9},{9,8},{10,11... | collective-permute-start | bytes 319496 | tf_op jit(solution)/shard_map/ppermute | solution.py:58
  89.7 12.5 %collective-permute-start.25 = (f32[2,1,104,128]{3,2,1,0:T(8,128)S(1)}, f32[2,1,104,128]{3,2,1,0:T(8,128)S(1)}, u32[]{:S(2)}, u32[]{:S(2)}) collective-permute-start(f32[2,1,104,128]{3,2,1,0:T(8,128)S(1)} %collective-permute-done.21.refs_10_), channel_id=1, source_target_pairs={{0,1},{1,0},{2,3},{3,2},{4,5},{5,4},{6,7},{7,6},{8,9},{9,8},{10,11... | collective-permute-start | bytes 319496 | tf_op jit(solution)/shard_map/ppermute | solution.py:58
  89.8 12.5 %collective-permute-start.26 = (f32[2,1,104,128]{3,2,1,0:T(8,128)S(1)}, f32[2,1,104,128]{3,2,1,0:T(8,128)S(1)}, u32[]{:S(2)}, u32[]{:S(2)}) collective-permute-start(f32[2,1,104,128]{3,2,1,0:T(8,128)S(1)} %collective-permute-done.22.refs_11_), channel_id=1, source_target_pairs={{0,1},{1,0},{2,3},{3,2},{4,5},{5,4},{6,7},{7,6},{8,9},{9,8},{10,11... | collective-permute-start | bytes 319496 | tf_op jit(solution)/shard_map/ppermute | solution.py:58
  111.2 8.3 %collective-permute-start.27 = (f32[2,48,128]{2,1,0:T(8,128)S(1)}, f32[2,48,128]{2,1,0:T(8,128)S(1)}, u32[]{:S(2)}, u32[]{:S(2)}) collective-permute-start(f32[2,48,128]{2,1,0:T(8,128)S(1)} %get-tuple-element.38), channel_id=1, source_target_pairs={{0,4},{4,8},{8,12},{12,0},{1,5},{5,9},{9,13},{13,1},{2,6},{6,10},{... | collective-permute-start | bytes 147464 | tf_op jit(solution)/shard_map/ppermute | solution.py:409
  115.2 5.8 %collective-permute-start.28 = (f32[2,48,128]{2,1,0:T(8,128)S(1)}, f32[2,48,128]{2,1,0:T(8,128)S(1)}, u32[]{:S(2)}, u32[]{:S(2)}) collective-permute-start(f32[2,48,128]{2,1,0:T(8,128)S(1)} %get-tuple-element.37), channel_id=1, source_target_pairs={{0,8},{4,12},{8,0},{12,4},{1,9},{5,13},{9,1},{13,5},{2,10},{6,14},... | collective-permute-start | bytes 147464 | tf_op jit(solution)/shard_map/ppermute | solution.py:409
  115.5 6.2 %collective-permute-start.29 = (f32[2,48,128]{2,1,0:T(8,128)S(1)}, f32[2,48,128]{2,1,0:T(8,128)S(1)}, u32[]{:S(2)}, u32[]{:S(2)}) collective-permute-start(f32[2,48,128]{2,1,0:T(8,128)S(1)} %get-tuple-element.36), channel_id=1, source_target_pairs={{0,12},{4,0},{8,4},{12,8},{1,13},{5,1},{9,5},{13,9},{2,14},{6,2},{... | collective-permute-start | bytes 147464 | tf_op jit(solution)/shard_map/ppermute | solution.py:409
  122.0 2.6 %collective-permute-start.30 = (f32[2,96,128]{2,1,0:T(8,128)S(1)}, f32[2,96,128]{2,1,0:T(8,128)S(1)}, u32[]{:S(2)}, u32[]{:S(2)}) collective-permute-start(f32[2,96,128]{2,1,0:T(8,128)S(1)} %get-tuple-element.17), channel_id=1, source_target_pairs={{0,1},{1,0},{2,3},{3,2},{4,5},{5,4},{6,7},{7,6},{8,9},{9,8},{10,11... | collective-permute-start | bytes 294920 | tf_op jit(solution)/shard_map/ppermute | solution.py:58
  122.1 5.7 %collective-permute-start.31 = (f32[2,96,128]{2,1,0:T(8,128)S(1)}, f32[2,96,128]{2,1,0:T(8,128)S(1)}, u32[]{:S(2)}, u32[]{:S(2)}) collective-permute-start(f32[2,96,128]{2,1,0:T(8,128)S(1)} %get-tuple-element.19), channel_id=1, source_target_pairs={{0,2},{1,3},{2,0},{3,1},{4,6},{5,7},{6,4},{7,5},{8,10},{9,11},{10,... | collective-permute-start | bytes 294920 | tf_op jit(solution)/shard_map/ppermute | solution.py:58
  122.3 6.6 %collective-permute-start.32 = (f32[2,96,128]{2,1,0:T(8,128)S(1)}, f32[2,96,128]{2,1,0:T(8,128)S(1)}, u32[]{:S(2)}, u32[]{:S(2)}) collective-permute-start(f32[2,96,128]{2,1,0:T(8,128)S(1)} %get-tuple-element.18), channel_id=1, source_target_pairs={{0,3},{1,2},{2,1},{3,0},{4,7},{5,6},{6,5},{7,4},{8,11},{9,10},{10,... | collective-permute-start | bytes 294920 | tf_op jit(solution)/shard_map/ppermute | solution.py:58
  (9 other events, 88.4 us)

commit v2 on v1

--- a/solution.py
+++ b/solution.py
@@ -58,15 +58,21 @@
     return lax.ppermute(value, axis, [(i, i ^ bit) for i in range(count)])
 
 
-def gather_rows(info_ref, lay, own_refs, other_refs, store):
+def swapped_round(value, axis, r):
+    count = lax.axis_size(axis)
+    return lax.ppermute(value, axis, [(i, (i + r) % count) for i in range(count)])
+
+
+def gather_rows(info_ref, lay, own_refs, other_ref, store):
     kc, c = info_ref[0], info_ref[1]
-    shift = pl.multiple_of(info_ref[2], TILE)
-    for core, refs in ((c, own_refs), (1 - c, other_refs)):
+    window = pl.ds(pl.multiple_of(info_ref[2], TILE), lay.span)
+    for core, local in ((c, True), (1 - c, False)):
         k = 2 * kc + core
-        for r, ref in enumerate(refs):
+        for r in range(lay.domain):
             source = lax.rem(k - r + lay.domain, lay.domain)
             for part in range(lay.part):
-                store(source * lay.rows + core * lay.part + part, part, ref, shift)
+                ref = own_refs[r].at[:, part, window, :] if local else other_ref.at[r, :, part]
+                store(source * lay.rows + core * lay.part + part, ref)
 
 
 def make_coefs(raw_ref, coef_ref, lay):
@@ -183,25 +189,22 @@
             state[time, field, :, lines - TILE :] = strip
 
 
-def source_kernel(lay, info_ref, inject_ref, *refs):
+def source_kernel(lay, info_ref, inject_ref, waves_other, model_other, *refs):
     count = lay.domain
-    waves_own, waves_other, model_own, model_other = (refs[i * count : (i + 1) * count] for i in range(4))
-    coef_ref, history_ref, raw, state = refs[4 * count :]
+    coef_ref, history_ref, raw, state = refs[2 * count :]
     clear_edges(state, lay)
 
-    def store_wave(row, part, ref, shift):
+    def store_wave(row, ref):
         for time in (0, 1):
             for field in (0, 1):
-                state[time, field, row + 1, TILE : TILE + lay.span, :] = ref[
-                    2 * time + field, part, pl.ds(shift, lay.span), :
-                ]
-
-    def store_model(row, part, ref, shift):
+                state[time, field, row + 1, TILE : TILE + lay.span, :] = ref[2 * time + field]
+
+    def store_model(row, ref):
         for i in range(5):
-            raw[i, row] = ref[i, part, pl.ds(shift, lay.span), :]
-
-    gather_rows(info_ref, lay, waves_own, waves_other, store_wave)
-    gather_rows(info_ref, lay, model_own, model_other, store_model)
+            raw[i, row] = ref[i]
+
+    gather_rows(info_ref, lay, refs[:count], waves_other, store_wave)
+    gather_rows(info_ref, lay, refs[count : 2 * count], model_other, store_model)
     make_coefs(raw, coef_ref, lay)
 
     def after(step, row, lines, new_p):
@@ -210,28 +213,89 @@
     run_steps(state, coef_ref, inject_ref, SRC_Z, lay, after)
 
 
-def receiver_kernel(lay, info_ref, inject_ref, coef_ref, history_ref, *refs):
+def receiver_kernel(lay, info_ref, inject_ref, coef_ref, history_ref, waves_other, old_other, *refs):
     count = lay.domain
-    waves_own, waves_other, old_own, old_other = (refs[i * count : (i + 1) * count] for i in range(4))
-    image_ref, state = refs[4 * count :]
+    pieces, (image_ref, state) = refs[2 * count : 3 * count], refs[3 * count :]
     clear_edges(state, lay)
 
-    def store_now(row, part, ref, shift):
+    def store_now(row, ref):
         for field in (0, 1):
-            state[0, field, row + 1, TILE : TILE + lay.span, :] = ref[4 + field, part, pl.ds(shift, lay.span), :]
-
-    def store_old(row, part, ref, shift):
+            state[0, field, row + 1, TILE : TILE + lay.span, :] = ref[4 + field]
+
+    def store_old(row, ref):
         for field in (0, 1):
-            state[1, field, row + 1, TILE : TILE + lay.span, :] = ref[field, part, pl.ds(shift, lay.span), :]
-
-    gather_rows(info_ref, lay, waves_own, waves_other, store_now)
-    gather_rows(info_ref, lay, old_own, old_other, store_old)
+            state[1, field, row + 1, TILE : TILE + lay.span, :] = ref[field]
+
+    gather_rows(info_ref, lay, refs[:count], waves_other, store_now)
+    gather_rows(info_ref, lay, refs[count : 2 * count], old_other, store_old)
     image_ref[...] = jnp.zeros_like(image_ref)
 
     def after(step, row, lines, new_p):
         image_ref[row, lines, :] += history_ref[step, row, lines, :] * new_p
 
     run_steps(state, coef_ref, inject_ref, REC_Z, lay, after)
+    d, skip = info_ref[3], info_ref[4]
+    if lay.own % TILE == 0:
+        skip = pl.multiple_of(skip, TILE)
+    for r, piece in enumerate(pieces):
+        first = lax.rem(d + r, lay.domain) * lay.rows
+        for row in range(lay.rows):
+            if lay.own % TILE == 0:
+                piece[row] = image_ref[first + row, pl.ds(skip, lay.own), :]
+            else:
+                piece[row] = pltpu.roll(image_ref[first + row], lay.span - skip, 0)[: lay.own]
+
+
+def pack_kernel(lay, info_ref, *refs, sources, models):
+    fields, arrays = refs[:sources], refs[sources : sources + models]
+    outs, sem = refs[len(refs) - 1 - lay.domain - (models > 0) : -1], refs[-1]
+    copies = []
+    for r in range(lay.domain):
+        k = lax.rem(info_ref[3] + r, lay.domain)
+        rows = pl.ds((k & 1) * lay.part, lay.part)
+        lines = pl.ds(pl.multiple_of((k >> 1) * lay.stride, TILE), lay.chip)
+        for i, field in enumerate(fields):
+            copies.append((field.at[:, rows, lines, :], outs[r].at[2 * i : 2 * i + 2]))
+    for i, array in enumerate(arrays):
+        copies.append((array, outs[lay.domain].at[i]))
+    copies = [pltpu.make_async_copy(source, target, sem.at[i]) for i, (source, target) in enumerate(copies)]
+    for copy in copies:
+        copy.start()
+    for copy in copies:
+        copy.wait()
+
+
+def pack(lay, info, fields, arrays, after):
+    anywhere = pl.BlockSpec(memory_space=pl.ANY)
+    z_count = fields[0].shape[-1]
+    outs = [jax.ShapeDtypeStruct((2 * len(fields), lay.part, lay.chip, z_count), jnp.float32)] * lay.domain
+    if arrays:
+        outs.append(jax.ShapeDtypeStruct((len(arrays),) + arrays[0].shape, jnp.float32))
+    operands = list(fields) + list(arrays) + list(after)
+    return pl.pallas_call(
+        functools.partial(pack_kernel, lay, sources=len(fields), models=len(arrays)),
+        out_shape=outs,
+        in_specs=[pl.BlockSpec(memory_space=pltpu.SMEM)] + [anywhere] * len(operands),
+        out_specs=[anywhere] * len(outs),
+        scratch_shapes=[pltpu.SemaphoreType.DMA((lay.domain * len(fields) + len(arrays),))],
+    )(info, *operands)
+
+
+def frame_kernel(lay, info_ref, *refs, slab):
+    pieces, outs, frame = refs[: lay.domain], refs[lay.domain : -1], refs[-1]
+    frame[...] = jnp.zeros_like(frame)
+    room = -(-lay.own // TILE) * TILE + TILE
+    filler = jnp.zeros((room - lay.own, frame.shape[-1]), jnp.float32)
+    for r, piece in enumerate(pieces):
+        place = info_ref[r]
+        first = pl.multiple_of(place & ~(TILE - 1), TILE)
+        for row in range(lay.rows):
+            moved = pltpu.roll(jnp.concatenate([piece[row], filler]), place & (TILE - 1), 0)
+            frame[row, pl.ds(first, room), :] += moved
+    for r, out in enumerate(outs):
+        first = pl.multiple_of(info_ref[lay.domain + r] * slab, TILE)
+        for row in range(lay.rows):
+            out[row] = frame[row, pl.ds(first, slab), :]
 
 
 def call(kernel, lay, outs, scratch, info, *operands):
@@ -275,35 +339,38 @@
     works_on = d // lay.half
     zero = jnp.int32(0)
 
-    def send(pick):
-        own, other = [], []
-        for r, pairs in lay.rounds():
+    window = lay.start(chip_id) + lay.shift(core) - lay.pad[0]
+    skip = (2 * chip_id + core) * lay.own - window
+    info = jnp.stack([chip_id, core, lay.shift(core), d, skip]).astype(jnp.int32)
+    tight = lay.pad == (0, 0)
+
+    def wave_messages(fields, arrays=(), after=()):
+        fields = [field[0] for field in fields]
+        if tight:
+            return pack(lay, info, fields, arrays, after)
+        fields = [jnp.pad(field, ((0, 0), (0, 0), lay.pad, (0, 0))) for field in fields]
+        messages = []
+        for r in range(domain):
             k = lax.rem(d + r, domain)
-            message = lax.ppermute(pick(k & 1, k >> 1), ("domain", "shot"), pairs)
-            own.append(message)
-            other.append(swapped(message, "shot", 1))
-        return own + other
-
-    def wave_pick(*fields):
-        fields = [jnp.pad(field[0], ((0, 0), (0, 0), lay.pad, (0, 0))) for field in fields]
-
-        def pick(c, kc):
-            return jnp.concatenate(
-                [
-                    lax.dynamic_slice(
-                        field,
-                        (zero, c * lay.part, lay.start(kc), zero),
-                        (2, lay.part, lay.chip, z_count),
-                    )
-                    for field in fields
-                ]
-            )
-
-        return pick
-
-    waves = send(wave_pick(source_now, source_before, receiver_now))
-
-    model = jnp.stack([velocity, thomsen_eps, thomsen_delta, tilt_angle, azimuth])
+            spot = (zero, (k & 1) * lay.part, lay.start(k >> 1), zero)
+            size = (2, lay.part, lay.chip, z_count)
+            messages.append(jnp.concatenate([lax.dynamic_slice(field, spot, size) for field in fields]))
+        return messages + ([jnp.stack(arrays)] if arrays else [])
+
+    def send(messages):
+        return [lax.ppermute(messages[r], ("domain", "shot"), pairs) for r, pairs in lay.rounds()]
+
+    def other_core(messages):
+        cut = lay.shift(1 - core)
+        return swapped(
+            jnp.stack([lax.dynamic_slice_in_dim(message, cut, lay.span, 2) for message in messages]), "shot", 1
+        )
+
+    *messages, model = wave_messages(
+        (source_now, source_before, receiver_now), (velocity, thomsen_eps, thomsen_delta, tilt_angle, azimuth)
+    )
+    waves = send(messages)
+
     slab = model.shape[2]
     model = model[:, :, None]
     bit = shots // 2
@@ -315,22 +382,20 @@
         bit //= 2
     model = model.reshape(model.shape[:2] + (shots * slab, z_count))
     anchor = shot_anchor[0]
-    if lay.pad != (0, 0):
+    if tight:
+        first_line = anchor
+    else:
         model = lax.dynamic_slice_in_dim(model, anchor, lines, 2)
         model = jnp.pad(model, ((0, 0), (0, 0), lay.pad, (0, 0)))
         first_line = zero
-    else:
-        first_line = anchor
-
-    def model_pick(c, kc):
-        return lax.dynamic_slice(
-            model,
-            (zero, c * lay.part, first_line + lay.start(kc), zero),
-            (5, lay.part, lay.chip, z_count),
-        )
-
-    models = send(model_pick)
-    olds = send(wave_pick(receiver_before))
+    messages = []
+    for r in range(domain):
+        k = lax.rem(d + r, domain)
+        spot = (zero, (k & 1) * lay.part, first_line + lay.start(k >> 1), zero)
+        messages.append(lax.dynamic_slice(model, spot, (5, lay.part, lay.chip, z_count)))
+    models = send(messages)
+    olds = send(wave_messages((receiver_before,), after=models[1:2]))
+    waves_other, models_other, olds_other = other_core(waves), other_core(models), other_core(olds)
 
     receivers = receiver_x.shape[1]
     mine = jnp.concatenate(
@@ -357,7 +422,6 @@
     twin_anchor = twin[at + 2].astype(jnp.int32)
     anchors = (jnp.where(core == 0, anchor, twin_anchor), jnp.where(core == 0, twin_anchor, anchor))
 
-    window = lay.start(chip_id) + lay.shift(core) - lay.pad[0]
     row_ids = jnp.arange(lay.width)
     line_ids = window + jnp.arange(lay.span)
     spread = ((0, 0), (0, 0), (0, z_count - steps))
@@ -373,7 +437,6 @@
     source_pulse = jnp.pad(source_pulse, spread)
     receiver_pulse = jnp.pad(receiver_pulse, spread)
 
-    info = jnp.stack([chip_id, core, lay.shift(core)]).astype(jnp.int32)
     block = (lay.width, lay.span, z_count)
     state = pltpu.VMEM((2, 2, lay.width + 2, lay.span + 2 * TILE, z_count), jnp.float32)
     coefs, history = call(
@@ -383,41 +446,45 @@
         [pltpu.VMEM((5,) + block, jnp.float32), state],
         info,
         source_pulse,
+        waves_other,
+        models_other,
         *waves,
         *models,
     )
-    image = call(
+    pieces = call(
         receiver_kernel,
         lay,
-        jax.ShapeDtypeStruct(block, jnp.float32),
-        [state],
+        [jax.ShapeDtypeStruct((rows, lay.own, z_count), jnp.float32)] * domain,
+        [pltpu.VMEM(block, jnp.float32), state],
         info,
         receiver_pulse,
         coefs,
         history,
+        waves_other,
+        olds_other,
         *waves,
         *olds,
     )
 
-    skip = (2 * chip_id + core) * lay.own - window
-    frame = jnp.zeros((rows, shots * slab, z_count), jnp.float32)
-    for r in range(domain):
-        piece = lax.dynamic_slice(
-            image, (lax.rem(d + r, domain) * rows, skip, zero), (rows, lay.own, z_count)
-        )
-        if r:
-            piece = lax.ppermute(piece, "domain", [(i, (i + r) % domain) for i in range(domain)])
-        source = lax.rem(d - r + domain, domain)
-        place = jnp.where(source < lay.half, anchors[0], anchors[1])
-        place = place + (2 * lax.rem(source, lay.half) + core) * lay.own
-        spot = (zero, place, zero)
-        frame = lax.dynamic_update_slice(
-            frame, piece + lax.dynamic_slice(frame, spot, piece.shape), spot
-        )
-    total = 0.0
-    for r in range(shots):
-        part = lax.dynamic_slice_in_dim(frame, slab_owner[s ^ r] * slab, slab, 1)
-        total = total + (swapped(part, "shot", r) if r else part)
+    source = lax.rem(d - jnp.arange(domain) + domain, domain)
+    places = jnp.where(source < lay.half, anchors[0], anchors[1])
+    places = places + (2 * lax.rem(source, lay.half) + core) * lay.own
+    owners = slab_owner[s ^ jnp.arange(shots)]
+    pieces = [
+        swapped_round(piece, "domain", r) if r else piece for r, piece in enumerate(pieces)
+    ]
+    room = -(-lay.own // TILE) * TILE + TILE
+    parts = call(
+        functools.partial(frame_kernel, slab=slab),
+        lay,
+        [jax.ShapeDtypeStruct((rows, slab, z_count), jnp.float32)] * shots,
+        [pltpu.VMEM((rows, shots * slab + room, z_count), jnp.float32)],
+        jnp.concatenate([places, owners]).astype(jnp.int32),
+        *pieces,
+    )
+    total = parts[0]
+    for r in range(1, shots):
+        total = total + swapped(parts[r], "shot", r)
     return total / steps
 
 

time: 130 us -> 174 us (1.34)
  Pallas kernels: 20.6 us -> 91.5 us
  starting transfers between devices: 57.1 us -> 36.8 us
  local copies, waits for them, and re-layouts: 10.6 us -> 7.06 us
  between operations: 7.19 us -> 4.37 us
    pallas_call x0 -> x2, Pallas kernels: none -> 70.2 us  [pack(): pl.pallas_call(functools.partial(pack_kernel, lay, sources=len(fields), m...]
    ppermute x15, starting transfers between devices: 43.9 us -> 29.1 us  [the longest x12 24.4 us: send(): lax.ppermute(messages[r], ('domain', 'shot'), pairs)]
    ppermute x15, waiting for transfers between devices: 24.3 us -> 12 us  [the longest x12 8.49 us: send(): lax.ppermute(messages[r], ('domain', 'shot'), pairs)]
    ppermute x18 -> x9, waiting for transfers between devices: 4.4 us -> 15.9 us  [swapped(): return lax.ppermute(value, axis, [(i, i ^ bit) for i in range(count)])]
    ppermute x18 -> x9, starting transfers between devices: 13.2 us -> 7.63 us  [swapped(): return lax.ppermute(value, axis, [(i, i ^ bit) for i in range(count)])]
    unnamed x21 -> x17, local copies, waits for them, and re-layouts: 3.98 us -> 1.45 us
    concatenate x4 -> x1, other arithmetic: 2.25 us -> 0.07 us  [per_device(): jnp.concatenate([places, owners]).astype(jnp.int32)]
    dynamic_slice x7 -> x1, local copies, waits for them, and re-layouts: 2.95 us -> 0.94 us  [per_device(): lax.dynamic_slice(model, spot, (5, lay.part, lay.chip, z_count))]
  transfers between devices with their start and end apart: 33 -> 24, of which waited for: 8 -> 10; matrix products, arithmetic and copies ran while one was open for 8% -> 5% of each run, Pallas kernels for 9% -> 47%
where the time goes in v2:
time: 174 us; the launch traced here: 173 us
  Pallas kernels  91.5 us (53%)
  starting transfers between devices  36.8 us (21%)
  waiting for transfers between devices  27.8 us (16%)
  local copies, waits for them, and re-layouts  7.06 us (4%)
  other arithmetic  5 us (3%)
  between operations  4.37 us (3%)
    pallas_call x2, Pallas kernels, pack(): pl.pallas_call(functools.partial(pack_kernel, lay, sources=len(fields), m...  70.2 us
    ppermute x12, starting transfers between devices, send(): lax.ppermute(messages[r], ('domain', 'shot'), pairs)  24.4 us
    pallas_call x3, Pallas kernels, call(): pl.pallas_call(functools.partial(kernel, lay), out_shape=outs, in_specs=[...  21.3 us
    ppermute x9, waiting for transfers between devices, swapped(): return lax.ppermute(value, axis, [(i, i ^ bit) for i in range(count)])  15.9 us
    ppermute x12, waiting for transfers between devices, send(): lax.ppermute(messages[r], ('domain', 'shot'), pairs)  8.49 us
    ppermute x9, starting transfers between devices, swapped(): return lax.ppermute(value, axis, [(i, i ^ bit) for i in range(count)])  7.63 us
    ppermute x3, starting transfers between devices, swapped_round(): lax.ppermute(value, axis, [(i, (i + r) % count) for i in range(count)])  4.76 us
  transfers between devices with their start and end apart: 24, of which 10 were waited for; matrix products, arithmetic and copies ran while one was open for 5% of the time, Pallas kernels for 47%

profile of v2, /device:TPU:0, one launch (start us, length us, event | category | flops | bytes accessed | tf_op | source)
XLA Modules:
  0.0 173.0 jit_solution(10229425541239235505)
XLA Ops:
  5.9 55.5 %shard_map.163 = (f32[6,1,104,128]{3,2,1,0:T(8,128)}, f32[6,1,104,128]{3,2,1,0:T(8,128)}, f32[6,1,104,128]{3,2,1,0:T(8,128)}, f32[6,1,104,128]{3,2,1,0:T(8,128)}, f32[5,2,96,128]{3,2,1,0:T(8,128)}) custom-call(s32[5]{0:T(128)} %stack.86.info_ref, f32[2,2,192,128]{3,2,1,0:T(8,128)} %bitcast.76, f32[2,2,192,128]{3,2,1,0:T(8,128)} %bitcast.77, ...), custom_call_target="tpu_custom_call" | custom-call | tf_op jit(solution)/shard_map/pallas_call | solution.py:275
  61.4 4.6 %collective-permute-start.4 = (f32[6,1,104,128]{3,2,1,0:T(8,128)}, f32[6,1,104,128]{3,2,1,0:T(8,128)S(1)}, u32[]{:S(2)}, u32[]{:S(2)}) collective-permute-start(f32[6,1,104,128]{3,2,1,0:T(8,128)} %get-tuple-element.27), channel_id=1, source_target_pairs={{0,5},{1,13},{2,7},{3,15},{4,0},{5,8},{6,2},{7,10},{8,1},{9,9},{10... | collective-permute-start | bytes 958472 | tf_op jit(solution)/shard_map/ppermute | solution.py:361
  66.1 4.3 %collective-permute-start.2 = (f32[6,1,104,128]{3,2,1,0:T(8,128)}, f32[6,1,104,128]{3,2,1,0:T(8,128)S(1)}, u32[]{:S(2)}, u32[]{:S(2)}) collective-permute-start(f32[6,1,104,128]{3,2,1,0:T(8,128)} %get-tuple-element.25), channel_id=1, source_target_pairs={{0,1},{1,9},{2,3},{3,11},{4,4},{5,12},{6,6},{7,14},{8,5},{9,13},{1... | collective-permute-start | bytes 958472 | tf_op jit(solution)/shard_map/ppermute | solution.py:361
  70.4 1.6 collective-permute-start.1
  72.7 1.5 collective-permute-start.6
  75.8 10.5 %collective-permute-done.6 = f32[5,2,1,96,128]{4,3,1,0,2:T(8,128)S(1)} collective-permute-done((f32[5,2,1,96,128]{4,3,1,0,2:T(8,128)}, f32[5,2,1,96,128]{4,3,1,0,2:T(8,128)S(1)}, u32[]{:S(2)}, u32[]{:S(2)}) %collective-permute-start.6) | collective-permute-done | bytes 491552 | tf_op jit(solution)/shard_map/ppermute | solution.py:58
  86.3 1.1 select_bitcast_fusion.3
  91.2 0.9 constant_dynamic-slice_fusion.3
  92.1 2.0 %collective-permute-start.9 = (f32[5,1,104,128]{3,2,1,0:T(8,128)S(1)}, f32[5,1,104,128]{3,2,1,0:T(8,128)S(1)}, u32[]{:S(2)}, u32[]{:S(2)}) collective-permute-start(f32[5,1,104,128]{3,2,1,0:T(8,128)S(1)} %get-tuple-element.46), channel_id=1, source_target_pairs={{0,1},{1,9},{2,3},{3,11},{4,4},{5,12},{6,6},{7,14},{8,5},{9,13},{1... | collective-permute-start | bytes 798728 | tf_op jit(solution)/shard_map/ppermute | solution.py:361
  94.2 3.5 %collective-permute-start.11 = (f32[5,1,104,128]{3,2,1,0:T(8,128)}, f32[5,1,104,128]{3,2,1,0:T(8,128)S(1)}, u32[]{:S(2)}, u32[]{:S(2)}) collective-permute-start(f32[5,1,104,128]{3,2,1,0:T(8,128)} %get-tuple-element.44), channel_id=1, source_target_pairs={{0,5},{1,13},{2,7},{3,15},{4,0},{5,8},{6,2},{7,10},{8,1},{9,9},{10... | collective-permute-start | bytes 798728 | tf_op jit(solution)/shard_map/ppermute | solution.py:361
  98.2 0.9 pad_maximum_fusion.1
  99.2 1.8 %collective-permute-start.5 = (f32[4,6,1,64,128]{4,3,2,1,0:T(8,128)}, f32[4,6,1,64,128]{4,3,2,1,0:T(8,128)S(1)}, u32[]{:S(2)}, u32[]{:S(2)}) collective-permute-start(f32[4,6,1,64,128]{4,3,2,1,0:T(8,128)} %pad_maximum_fusion.1), channel_id=1, source_target_pairs={{0,1},{1,0},{2,3},{3,2},{4,5},{5,4},{6,7},{7,6},{8,9},{9,8},{10,11... | collective-permute-start | bytes 2359304 | tf_op jit(solution)/shard_map/ppermute | solution.py:58
  101.0 1.6 collective-permute-start.8
  102.6 2.5 %collective-permute-done.9.refs_5_.refs_1_ = f32[5,1,104,128]{3,2,1,0:T(8,128)S(1)} collective-permute-done((f32[5,1,104,128]{3,2,1,0:T(8,128)S(1)}, f32[5,1,104,128]{3,2,1,0:T(8,128)S(1)}, u32[]{:S(2)}, u32[]{:S(2)}) %collective-permute-start.9) | collective-permute-done | bytes 266272 | tf_op jit(solution)/shard_map/ppermute | solution.py:361
  105.8 14.7 %shard_map.165 = (f32[2,1,104,128]{3,2,1,0:T(8,128)}, f32[2,1,104,128]{3,2,1,0:T(8,128)}, f32[2,1,104,128]{3,2,1,0:T(8,128)}, f32[2,1,104,128]{3,2,1,0:T(8,128)}) custom-call(s32[5]{0:T(128)} %stack.86.info_ref, f32[2,2,192,128]{3,2,1,0:T(8,128)} %bitcast.75, f32[5,1,104,128]{3,2,1,0:T(8,128)} %copy-done.1), custom_call_target="tpu_custom_call" | custom-call | tf_op jit(solution)/shard_map/pallas_call | solution.py:275
  120.6 2.1 %collective-permute-start.16 = (f32[2,1,104,128]{3,2,1,0:T(8,128)}, f32[2,1,104,128]{3,2,1,0:T(8,128)S(1)}, u32[]{:S(2)}, u32[]{:S(2)}) collective-permute-start(f32[2,1,104,128]{3,2,1,0:T(8,128)} %get-tuple-element.34), channel_id=1, source_target_pairs={{0,5},{1,13},{2,7},{3,15},{4,0},{5,8},{6,2},{7,10},{8,1},{9,9},{10... | collective-permute-start | bytes 319496 | tf_op jit(solution)/shard_map/ppermute | solution.py:361
  122.6 0.9 dynamic-slice_bitcast_fusion.6
  124.3 1.6 collective-permute-start.15
  125.9 1.9 %collective-permute-start.14 = (f32[2,1,104,128]{3,2,1,0:T(8,128)S(1)}, f32[2,1,104,128]{3,2,1,0:T(8,128)S(1)}, u32[]{:S(2)}, u32[]{:S(2)}) collective-permute-start(f32[2,1,104,128]{3,2,1,0:T(8,128)S(1)} %copy-done.6), channel_id=1, source_target_pairs={{0,1},{1,9},{2,3},{3,11},{4,4},{5,12},{6,6},{7,14},{8,5},{9,13},{1... | collective-permute-start | bytes 319496 | tf_op jit(solution)/shard_map/ppermute | solution.py:361
  128.8 2.2 %collective-permute-done.15.refs_6_ = f32[2,1,104,128]{3,2,1,0:T(8,128)S(1)} collective-permute-done((f32[2,1,104,128]{3,2,1,0:T(8,128)S(1)}, f32[2,1,104,128]{3,2,1,0:T(8,128)S(1)}, u32[]{:S(2)}, u32[]{:S(2)}) %collective-permute-start.15) | collective-permute-done | bytes 106528 | tf_op jit(solution)/shard_map/ppermute | solution.py:361
  131.1 3.4 %collective-permute-done.14.refs_5_ = f32[2,1,104,128]{3,2,1,0:T(8,128)S(1)} collective-permute-done((f32[2,1,104,128]{3,2,1,0:T(8,128)S(1)}, f32[2,1,104,128]{3,2,1,0:T(8,128)S(1)}, u32[]{:S(2)}, u32[]{:S(2)}) %collective-permute-start.14) | collective-permute-done | bytes 106528 | tf_op jit(solution)/shard_map/ppermute | solution.py:361
  135.4 11.8 %shard_map.164 = (f32[16,8,64,128]{3,2,1,0:T(8,128)S(1)}, f32[8,8,64,128]{3,2,1,0:T(8,128)S(1)}) custom-call(s32[5]{0:T(128)S(1)} %copy-done.3, f32[8,64,128]{2,1,0:T(8,128)S(1)} %pad.8.inject_ref, f32[4,6,1,64,128]{4,3,2,1,0:T(8,128)S(1)} %collective-permute-done.5.waves_other, f32[4,5,1,64,128]{4,3,2,1,0:T(8,128)S(1)} %collective-permute-done.12.model_other, ...), custom_call_target="tpu_custom_call" | custom-call | tf_op jit(solution)/shard_map/pallas_call | solution.py:303
  147.2 8.9 %shard_map.166 = (f32[2,48,128]{2,1,0:T(8,128)S(1)}, f32[2,48,128]{2,1,0:T(8,128)S(1)}, f32[2,48,128]{2,1,0:T(8,128)S(1)}, f32[2,48,128]{2,1,0:T(8,128)S(1)}) custom-call(s32[5]{0:T(128)S(1)} %copy-done.3, f32[8,64,128]{2,1,0:T(8,128)S(1)} %pad.7.inject_ref, f32[16,8,64,128]{3,2,1,0:T(8,128)S(1)} %get-tuple-element.29.coef_ref, ...), custom_call_target="tpu_custom_call" | custom-call | tf_op jit(solution)/shard_map/pallas_call | solution.py:303
  156.1 2.3 %collective-permute-start.18 = (f32[2,48,128]{2,1,0:T(8,128)S(1)}, f32[2,48,128]{2,1,0:T(8,128)S(1)}, u32[]{:S(2)}, u32[]{:S(2)}) collective-permute-start(f32[2,48,128]{2,1,0:T(8,128)S(1)} %get-tuple-element.36), channel_id=1, source_target_pairs={{0,4},{4,8},{8,12},{12,0},{1,5},{5,9},{9,13},{13,1},{2,6},{6,10},{... | collective-permute-start | bytes 147464 | tf_op jit(solution)/shard_map/ppermute | solution.py:63
  158.4 0.9 collective-permute-start.19
  159.4 1.5 collective-permute-start.20
  160.9 1.7 collective-permute-done.18.refs_1_
  162.6 1.6 collective-permute-done.19.refs_2_
  165.1 0.9 collective-permute-start.23
  165.9 0.8 collective-permute-start.22
  167.0 3.2 %collective-permute-done.23 = f32[2,96,128]{2,1,0:T(8,128)S(1)} collective-permute-done((f32[2,96,128]{2,1,0:T(8,128)S(1)}, f32[2,96,128]{2,1,0:T(8,128)S(1)}, u32[]{:S(2)}, u32[]{:S(2)}) %collective-permute-start.23) | collective-permute-done | bytes 98336 | tf_op jit(solution)/shard_map/ppermute | solution.py:58
  170.2 2.1 %collective-permute-done.22 = f32[2,96,128]{2,1,0:T(8,128)S(1)} collective-permute-done((f32[2,96,128]{2,1,0:T(8,128)S(1)}, f32[2,96,128]{2,1,0:T(8,128)S(1)}, u32[]{:S(2)}, u32[]{:S(2)}) %collective-permute-start.22) | collective-permute-done | bytes 98336 | tf_op jit(solution)/shard_map/ppermute | solution.py:58
  (86 shorter events, 13.6 us)
Async XLA Ops:
  0.0 72.1 %copy-start = (s32[4]{0:T(128)S(1)}, s32[4]{0:T(128)}, u32[]{:S(2)}) copy-start(s32[4]{0:T(128)} %param.33) | copy-start | bytes 52
  4.8 68.0 %collective-permute-start = (f32[2571]{0:T(1024)S(1)}, f32[2571]{0:T(1024)S(1)}, u32[]{:S(2)}, u32[]{:S(2)}) collective-permute-start(f32[2571]{0:T(1024)S(1)} %concatenate.6), channel_id=1, source_target_pairs={{0,1},{1,0},{2,3},{3,2},{4,5},{5,4},{6,7},{7,6},{8,9},{9,8},{10,11... | collective-permute-start | bytes 30860 | tf_op jit(solution)/shard_map/ppermute | solution.py:58
  61.4 29.1 %collective-permute-start.4 = (f32[6,1,104,128]{3,2,1,0:T(8,128)}, f32[6,1,104,128]{3,2,1,0:T(8,128)S(1)}, u32[]{:S(2)}, u32[]{:S(2)}) collective-permute-start(f32[6,1,104,128]{3,2,1,0:T(8,128)} %get-tuple-element.27), channel_id=1, source_target_pairs={{0,5},{1,13},{2,7},{3,15},{4,0},{5,8},{6,2},{7,10},{8,1},{9,9},{10... | collective-permute-start | bytes 958472 | tf_op jit(solution)/shard_map/ppermute | solution.py:361
  66.0 24.5 %collective-permute-start.3 = (f32[6,1,104,128]{3,2,1,0:T(8,128)}, f32[6,1,104,128]{3,2,1,0:T(8,128)S(1)}, u32[]{:S(2)}, u32[]{:S(2)}) collective-permute-start(f32[6,1,104,128]{3,2,1,0:T(8,128)} %get-tuple-element.26), channel_id=1, source_target_pairs={{0,4},{1,12},{2,6},{3,14},{4,5},{5,13},{6,7},{7,15},{8,0},{9,8},{1... | collective-permute-start | bytes 958472 | tf_op jit(solution)/shard_map/ppermute | solution.py:361
  66.1 28.0 %collective-permute-start.2 = (f32[6,1,104,128]{3,2,1,0:T(8,128)}, f32[6,1,104,128]{3,2,1,0:T(8,128)S(1)}, u32[]{:S(2)}, u32[]{:S(2)}) collective-permute-start(f32[6,1,104,128]{3,2,1,0:T(8,128)} %get-tuple-element.25), channel_id=1, source_target_pairs={{0,1},{1,9},{2,3},{3,11},{4,4},{5,12},{6,6},{7,14},{8,5},{9,13},{1... | collective-permute-start | bytes 958472 | tf_op jit(solution)/shard_map/ppermute | solution.py:361
  70.4 27.3 %collective-permute-start.1 = (f32[6,1,104,128]{3,2,1,0:T(8,128)}, f32[6,1,104,128]{3,2,1,0:T(8,128)S(1)}, u32[]{:S(2)}, u32[]{:S(2)}) collective-permute-start(f32[6,1,104,128]{3,2,1,0:T(8,128)} %get-tuple-element.24), channel_id=1, source_target_pairs={{0,0},{1,8},{2,2},{3,10},{4,1},{5,9},{6,3},{7,11},{8,4},{9,12},{10... | collective-permute-start | bytes 958472 | tf_op jit(solution)/shard_map/ppermute | solution.py:361
  72.7 13.5 %collective-permute-start.6 = (f32[5,2,1,96,128]{4,3,1,0,2:T(8,128)}, f32[5,2,1,96,128]{4,3,1,0,2:T(8,128)S(1)}, u32[]{:S(2)}, u32[]{:S(2)}) collective-permute-start(f32[5,2,1,96,128]{4,3,1,0,2:T(8,128)} %bitcast.74), channel_id=1, source_target_pairs={{0,2},{1,3},{2,0},{3,1},{4,6},{5,7},{6,4},{7,5},{8,10},{9,11},{10,... | collective-permute-start | bytes 1474568 | tf_op jit(solution)/shard_map/ppermute | solution.py:58
  74.3 13.9 %copy-start.4 = (f32[2571]{0:T(1024)}, f32[2571]{0:T(1024)S(1)}, u32[]{:S(2)}) copy-start(f32[2571]{0:T(1024)S(1)} %broadcast_select_fusion.1) | copy-start | bytes 30856
  87.4 3.2 %collective-permute-start.7 = (f32[5,2,2,96,128]{4,3,1,0,2:T(8,128)S(1)}, f32[5,2,2,96,128]{4,3,1,0,2:T(8,128)S(1)}, u32[]{:S(2)}, u32[]{:S(2)}) collective-permute-start(f32[5,2,2,96,128]{4,3,1,0,2:T(8,128)S(1)} %maximum_bitcast_fusion), channel_id=1, source_target_pairs={{0,1},{1,0},{2,3},{3,2},{4,5},{5,4},{6,7},{7,6},{8,9},{9,8},{10,11... | collective-permute-start | bytes 2949128 | tf_op jit(solution)/shard_map/ppermute | solution.py:58
  92.1 13.0 %collective-permute-start.9 = (f32[5,1,104,128]{3,2,1,0:T(8,128)S(1)}, f32[5,1,104,128]{3,2,1,0:T(8,128)S(1)}, u32[]{:S(2)}, u32[]{:S(2)}) collective-permute-start(f32[5,1,104,128]{3,2,1,0:T(8,128)S(1)} %get-tuple-element.46), channel_id=1, source_target_pairs={{0,1},{1,9},{2,3},{3,11},{4,4},{5,12},{6,6},{7,14},{8,5},{9,13},{1... | collective-permute-start | bytes 798728 | tf_op jit(solution)/shard_map/ppermute | solution.py:361
  94.2 29.4 %collective-permute-start.11 = (f32[5,1,104,128]{3,2,1,0:T(8,128)}, f32[5,1,104,128]{3,2,1,0:T(8,128)S(1)}, u32[]{:S(2)}, u32[]{:S(2)}) collective-permute-start(f32[5,1,104,128]{3,2,1,0:T(8,128)} %get-tuple-element.44), channel_id=1, source_target_pairs={{0,5},{1,13},{2,7},{3,15},{4,0},{5,8},{6,2},{7,10},{8,1},{9,9},{10... | collective-permute-start | bytes 798728 | tf_op jit(solution)/shard_map/ppermute | solution.py:361
  97.7 25.9 %collective-permute-start.10 = (f32[5,1,104,128]{3,2,1,0:T(8,128)}, f32[5,1,104,128]{3,2,1,0:T(8,128)S(1)}, u32[]{:S(2)}, u32[]{:S(2)}) collective-permute-start(f32[5,1,104,128]{3,2,1,0:T(8,128)} %get-tuple-element.45), channel_id=1, source_target_pairs={{0,4},{1,12},{2,6},{3,14},{4,5},{5,13},{6,7},{7,15},{8,0},{9,8},{1... | collective-permute-start | bytes 798728 | tf_op jit(solution)/shard_map/ppermute | solution.py:361
  99.2 36.2 %collective-permute-start.5 = (f32[4,6,1,64,128]{4,3,2,1,0:T(8,128)}, f32[4,6,1,64,128]{4,3,2,1,0:T(8,128)S(1)}, u32[]{:S(2)}, u32[]{:S(2)}) collective-permute-start(f32[4,6,1,64,128]{4,3,2,1,0:T(8,128)} %pad_maximum_fusion.1), channel_id=1, source_target_pairs={{0,1},{1,0},{2,3},{3,2},{4,5},{5,4},{6,7},{7,6},{8,9},{9,8},{10,11... | collective-permute-start | bytes 2359304 | tf_op jit(solution)/shard_map/ppermute | solution.py:58
  101.0 22.7 %collective-permute-start.8 = (f32[5,1,104,128]{3,2,1,0:T(8,128)}, f32[5,1,104,128]{3,2,1,0:T(8,128)S(1)}, u32[]{:S(2)}, u32[]{:S(2)}) collective-permute-start(f32[5,1,104,128]{3,2,1,0:T(8,128)} %get-tuple-element.43), channel_id=1, source_target_pairs={{0,0},{1,8},{2,2},{3,10},{4,1},{5,9},{6,3},{7,11},{8,4},{9,12},{10... | collective-permute-start | bytes 798728 | tf_op jit(solution)/shard_map/ppermute | solution.py:361
  120.5 3.8 %copy-start.7 = (f32[2,1,104,128]{3,2,1,0:T(8,128)S(1)}, f32[2,1,104,128]{3,2,1,0:T(8,128)}, u32[]{:S(2)}) copy-start(f32[2,1,104,128]{3,2,1,0:T(8,128)} %get-tuple-element.33) | copy-start | bytes 319492
  120.5 5.4 %copy-start.6 = (f32[2,1,104,128]{3,2,1,0:T(8,128)S(1)}, f32[2,1,104,128]{3,2,1,0:T(8,128)}, u32[]{:S(2)}) copy-start(f32[2,1,104,128]{3,2,1,0:T(8,128)} %get-tuple-element.32) | copy-start | bytes 319492
  120.6 7.6 %copy-start.5 = (f32[2,1,104,128]{3,2,1,0:T(8,128)S(1)}, f32[2,1,104,128]{3,2,1,0:T(8,128)}, u32[]{:S(2)}) copy-start(f32[2,1,104,128]{3,2,1,0:T(8,128)} %get-tuple-element.31) | copy-start | bytes 319492
  120.6 14.6 %slice-start = ((f32[2571]{0:T(1024)}), f32[8]{0:T(128)S(1)}, s32[]{:S(2)}) async-start(f32[2571]{0:T(1024)} %copy-done.4), calls=%async_computation | async-start | bytes 1024 | tf_op jit(solution)/shard_map/slice | solution.py:416
  120.6 7.6 %collective-permute-start.16 = (f32[2,1,104,128]{3,2,1,0:T(8,128)}, f32[2,1,104,128]{3,2,1,0:T(8,128)S(1)}, u32[]{:S(2)}, u32[]{:S(2)}) collective-permute-start(f32[2,1,104,128]{3,2,1,0:T(8,128)} %get-tuple-element.34), channel_id=1, source_target_pairs={{0,5},{1,13},{2,7},{3,15},{4,0},{5,8},{6,2},{7,10},{8,1},{9,9},{10... | collective-permute-start | bytes 319496 | tf_op jit(solution)/shard_map/ppermute | solution.py:361
  123.6 11.8 %copy-start.2 = (f32[5,1,104,128]{3,2,1,0:T(8,128)S(1)}, f32[5,1,104,128]{3,2,1,0:T(8,128)}, u32[]{:S(2)}) copy-start(f32[5,1,104,128]{3,2,1,0:T(8,128)} %copy-done.1) | copy-start | bytes 798724
  123.6 11.8 %copy-start.3 = (s32[5]{0:T(128)S(1)}, s32[5]{0:T(128)}, u32[]{:S(2)}) copy-start(s32[5]{0:T(128)} %stack.86.info_ref) | copy-start | bytes 64
  123.8 11.6 %collective-permute-start.12 = (f32[4,5,1,64,128]{4,3,2,1,0:T(8,128)S(1)}, f32[4,5,1,64,128]{4,3,2,1,0:T(8,128)S(1)}, u32[]{:S(2)}, u32[]{:S(2)}) collective-permute-start(f32[4,5,1,64,128]{4,3,2,1,0:T(8,128)S(1)} %pad_maximum_fusion.2), channel_id=1, source_target_pairs={{0,1},{1,0},{2,3},{3,2},{4,5},{5,4},{6,7},{7,6},{8,9},{9,8},{10,11... | collective-permute-start | bytes 1966088 | tf_op jit(solution)/shard_map/ppermute | solution.py:58
  124.3 6.7 %collective-permute-start.15 = (f32[2,1,104,128]{3,2,1,0:T(8,128)S(1)}, f32[2,1,104,128]{3,2,1,0:T(8,128)S(1)}, u32[]{:S(2)}, u32[]{:S(2)}) collective-permute-start(f32[2,1,104,128]{3,2,1,0:T(8,128)S(1)} %copy-done.7), channel_id=1, source_target_pairs={{0,4},{1,12},{2,6},{3,14},{4,5},{5,13},{6,7},{7,15},{8,0},{9,8},{1... | collective-permute-start | bytes 319496 | tf_op jit(solution)/shard_map/ppermute | solution.py:361
  125.9 8.5 %collective-permute-start.14 = (f32[2,1,104,128]{3,2,1,0:T(8,128)S(1)}, f32[2,1,104,128]{3,2,1,0:T(8,128)S(1)}, u32[]{:S(2)}, u32[]{:S(2)}) collective-permute-start(f32[2,1,104,128]{3,2,1,0:T(8,128)S(1)} %copy-done.6), channel_id=1, source_target_pairs={{0,1},{1,9},{2,3},{3,11},{4,4},{5,12},{6,6},{7,14},{8,5},{9,13},{1... | collective-permute-start | bytes 319496 | tf_op jit(solution)/shard_map/ppermute | solution.py:361
  128.2 6.3 %collective-permute-start.13 = (f32[2,1,104,128]{3,2,1,0:T(8,128)S(1)}, f32[2,1,104,128]{3,2,1,0:T(8,128)S(1)}, u32[]{:S(2)}, u32[]{:S(2)}) collective-permute-start(f32[2,1,104,128]{3,2,1,0:T(8,128)S(1)} %copy-done.5), channel_id=1, source_target_pairs={{0,0},{1,8},{2,2},{3,10},{4,1},{5,9},{6,3},{7,11},{8,4},{9,12},{10... | collective-permute-start | bytes 319496 | tf_op jit(solution)/shard_map/ppermute | solution.py:361
  134.5 12.7 %collective-permute-start.17 = (f32[4,2,1,64,128]{4,3,2,1,0:T(8,128)S(1)}, f32[4,2,1,64,128]{4,3,2,1,0:T(8,128)S(1)}, u32[]{:S(2)}, u32[]{:S(2)}) collective-permute-start(f32[4,2,1,64,128]{4,3,2,1,0:T(8,128)S(1)} %pad_maximum_fusion.3), channel_id=1, source_target_pairs={{0,1},{1,0},{2,3},{3,2},{4,5},{5,4},{6,7},{7,6},{8,9},{9,8},{10,11... | collective-permute-start | bytes 786440 | tf_op jit(solution)/shard_map/ppermute | solution.py:58
  156.1 6.5 %collective-permute-start.18 = (f32[2,48,128]{2,1,0:T(8,128)S(1)}, f32[2,48,128]{2,1,0:T(8,128)S(1)}, u32[]{:S(2)}, u32[]{:S(2)}) collective-permute-start(f32[2,48,128]{2,1,0:T(8,128)S(1)} %get-tuple-element.36), channel_id=1, source_target_pairs={{0,4},{4,8},{8,12},{12,0},{1,5},{5,9},{9,13},{13,1},{2,6},{6,10},{... | collective-permute-start | bytes 147464 | tf_op jit(solution)/shard_map/ppermute | solution.py:63
  158.4 5.8 %collective-permute-start.19 = (f32[2,48,128]{2,1,0:T(8,128)S(1)}, f32[2,48,128]{2,1,0:T(8,128)S(1)}, u32[]{:S(2)}, u32[]{:S(2)}) collective-permute-start(f32[2,48,128]{2,1,0:T(8,128)S(1)} %get-tuple-element.37), channel_id=1, source_target_pairs={{0,8},{4,12},{8,0},{12,4},{1,9},{5,13},{9,1},{13,5},{2,10},{6,14},... | collective-permute-start | bytes 147464 | tf_op jit(solution)/shard_map/ppermute | solution.py:63
  159.4 5.0 %collective-permute-start.20 = (f32[2,48,128]{2,1,0:T(8,128)S(1)}, f32[2,48,128]{2,1,0:T(8,128)S(1)}, u32[]{:S(2)}, u32[]{:S(2)}) collective-permute-start(f32[2,48,128]{2,1,0:T(8,128)S(1)} %get-tuple-element.38), channel_id=1, source_target_pairs={{0,12},{4,0},{8,4},{12,8},{1,13},{5,1},{9,5},{13,9},{2,14},{6,2},{... | collective-permute-start | bytes 147464 | tf_op jit(solution)/shard_map/ppermute | solution.py:63
  165.1 5.1 %collective-permute-start.23 = (f32[2,96,128]{2,1,0:T(8,128)S(1)}, f32[2,96,128]{2,1,0:T(8,128)S(1)}, u32[]{:S(2)}, u32[]{:S(2)}) collective-permute-start(f32[2,96,128]{2,1,0:T(8,128)S(1)} %get-tuple-element.42), channel_id=1, source_target_pairs={{0,3},{1,2},{2,1},{3,0},{4,7},{5,6},{6,5},{7,4},{8,11},{9,10},{10,... | collective-permute-start | bytes 294920 | tf_op jit(solution)/shard_map/ppermute | solution.py:58
  165.9 6.4 %collective-permute-start.22 = (f32[2,96,128]{2,1,0:T(8,128)S(1)}, f32[2,96,128]{2,1,0:T(8,128)S(1)}, u32[]{:S(2)}, u32[]{:S(2)}) collective-permute-start(f32[2,96,128]{2,1,0:T(8,128)S(1)} %get-tuple-element.41), channel_id=1, source_target_pairs={{0,2},{1,3},{2,0},{3,1},{4,6},{5,7},{6,4},{7,5},{8,10},{9,11},{10,... | collective-permute-start | bytes 294920 | tf_op jit(solution)/shard_map/ppermute | solution.py:58
  166.7 5.6 %collective-permute-start.21 = (f32[2,96,128]{2,1,0:T(8,128)S(1)}, f32[2,96,128]{2,1,0:T(8,128)S(1)}, u32[]{:S(2)}, u32[]{:S(2)}) collective-permute-start(f32[2,96,128]{2,1,0:T(8,128)S(1)} %get-tuple-element.40), channel_id=1, source_target_pairs={{0,1},{1,0},{2,3},{3,2},{4,5},{5,4},{6,7},{7,6},{8,9},{9,8},{10,11... | collective-permute-start | bytes 294920 | tf_op jit(solution)/shard_map/ppermute | solution.py:58
  (1 other events, 0.7 us)

commit v3 on v2

v3 whole, which is shorter than its diff:
```python
import functools
import math

import jax
import jax.numpy as jnp
from jax import lax
from jax.experimental import pallas as pl
from jax.experimental.pallas import tpu as pltpu
from jax.sharding import PartitionSpec as P

SRC_Z = 3
REC_Z = 1
TILE = 8
COEFS = 16


class Layout:
    def __init__(self, domain, shots, rows, lines, steps):
        self.domain, self.shots, self.rows, self.lines, self.steps = domain, shots, rows, lines, steps
        self.half = domain // 2
        self.part = rows // 2
        self.width = rows * domain
        self.own = lines // domain
        halo = -(-steps // TILE) * TILE
        if self.half == 2 and self.own % TILE == 0:
            self.pad = (0, 0)
            self.chip = 2 * self.own + halo
            self.stride = lines - self.chip
            self.span = self.own + 2 * halo
        else:
            self.chip = -(-(2 * self.own + 2 * halo) // TILE) * TILE
            self.pad = (halo, max(0, (self.half - 1) * 2 * self.own + self.chip - halo - lines))
            self.stride = 2 * self.own
            self.span = self.chip

    def start(self, kc):
        return kc * self.stride

    def shift(self, c):
        return c * (self.chip - self.span)

    def rounds(self):
        count = self.domain * self.shots
        for r in range(self.domain):
            pairs = []
            for d in range(self.domain):
                for s in range(self.shots):
                    k = (d + r) % self.domain
                    to_d = self.half * (s & 1) + (k >> 1)
                    to_s = (s & ~1) | (k & 1)
                    pairs.append((d * self.shots + s, to_d * self.shots + to_s))
            assert len({pair[1] for pair in pairs}) == count
            yield r, pairs


def swapped(value, axis, bit):
    count = lax.axis_size(axis)
    return lax.ppermute(value, axis, [(i, i ^ bit) for i in range(count)])


def tied(value, *others):
    return lax.optimization_barrier((value, *others))[0]


def swapped_round(value, axis, r):
    count = lax.axis_size(axis)
    return lax.ppermute(value, axis, [(i, (i + r) % count) for i in range(count)])


def gather_rows(info_ref, lay, own_refs, other_refs, store):
    kc, c = info_ref[0], info_ref[1]
    window = pl.ds(pl.multiple_of(info_ref[2], TILE), lay.span)
    for core, refs in ((c, own_refs), (1 - c, other_refs)):
        k = 2 * kc + core
        for r, ref in enumerate(refs):
            source = lax.rem(k - r + lay.domain, lay.domain)
            for part in range(lay.part):
                store(source * lay.rows + core * lay.part + part, ref.at[:, part, window, :])


def make_coefs(raw_ref, coef_ref, lay):
    lane = lax.broadcasted_iota(jnp.int32, (lay.span, raw_ref.shape[-1]), 1)
    last = raw_ref.shape[-1] - 1

    def from_below(value):
        return jnp.where(lane == 0, 0.0, pltpu.roll(value, 1, 1))

    def from_above(value):
        return jnp.where(lane == last, 0.0, pltpu.roll(value, last, 1))

    def one_row(row, unused):
        velocity, eps, delta, tilt, azimuth = (raw_ref[i, row] for i in range(5))
        gain_eps = 1.0 + 2.0 * eps
        gain_delta = jnp.sqrt(1.0 + 2.0 * delta)
        sin_tilt = jnp.sin(tilt)
        n_x = sin_tilt * jnp.cos(azimuth)
        n_y = sin_tilt * jnp.sin(azimuth)
        n_z = jnp.cos(tilt)
        xx, yy, zz = n_x * n_x, n_y * n_y, n_z * n_z
        xz, yz = 0.5 * n_x * n_z, 0.5 * n_y * n_z
        values = (
            xx, 1.0 - xx, yy, 1.0 - yy, 0.5 * n_x * n_y,
            from_below(zz), from_below(1.0 - zz), from_below(xz), from_below(yz),
            from_above(zz), from_above(1.0 - zz), from_above(xz), from_above(yz),
            velocity * gain_eps, velocity * gain_delta, velocity,
        )
        for i, value in enumerate(values):
            coef_ref[i, row] = value
        return unused

    lax.fori_loop(0, lay.width, one_row, 0)


def run_steps(state, coef_ref, inject_refs, image_ref, lay):
    z_count = state.shape[-1]
    last = z_count - 1
    lane = lax.broadcasted_iota(jnp.int32, (TILE, z_count), 1)
    chunk = next(size for size in (8, 4, 2, 1) if lay.width % size == 0)

    def row_of(now, field, row, tile):
        base = TILE + TILE * tile
        middle = state[now, field, row, base : base + TILE, :]
        low = state[now, field, row, base - 1 : base - 1 + TILE, :]
        high = state[now, field, row, base + 1 : base + 1 + TILE, :]
        return middle, high - low, high + low

    def sweep(step, now, new, first, tile, wave):
        depth = (SRC_Z, REC_Z)[wave]
        turn = lax.rem(depth - step + z_count, z_count)
        lines = slice(TILE * tile, TILE * tile + TILE)
        inner = slice(TILE + TILE * tile, 2 * TILE + TILE * tile)
        pair = (2 * wave, 2 * wave + 1)
        before = [row_of(now, field, first, tile) for field in pair]
        here = [row_of(now, field, first + 1, tile) for field in pair]
        for i in range(chunk):
            row = first + i
            beyond = [row_of(now, field, row + 2, tile) for field in pair]
            coef = [coef_ref[n, row, lines, :] for n in range(COEFS)]
            xx, xx0, yy, yy0, xy = coef[:5]
            zz_b, zz0_b, xz_b, yz_b, zz_a, zz0_a, xz_a, yz_a = coef[5:13]
            axial_gain, cross_gain, velocity = coef[13:]

            def terms(field):
                f, diff_y, sum_y = here[field]
                sum_x = beyond[field][0] + before[field][0]
                diff_x = beyond[field][0] - before[field][0]
                mixed = beyond[field][1] - before[field][1]
                below = xz_b * diff_x + yz_b * diff_y
                above = xz_a * diff_x + yz_a * diff_y
                return f, sum_x, sum_y, xy * mixed, below, above

            p, sum_x, sum_y, mixed, below, above = terms(0)
            across = xx0 * sum_x + yy0 * sum_y - mixed
            across += pltpu.roll(zz0_b * p - below, last, 1) + pltpu.roll(zz0_a * p + above, 1, 1)
            across -= 4.0 * p
            q, sum_x, sum_y, mixed, below, above = terms(1)
            axial = xx * sum_x + yy * sum_y + mixed
            axial += pltpu.roll(zz_b * q + below, last, 1) + pltpu.roll(zz_a * q - above, 1, 1)
            axial -= 2.0 * q
            pulse = pltpu.roll(inject_refs[wave][row, lines, :], turn, 1)
            pulse = velocity * jnp.where(lane == depth, pulse, 0.0)
            old_p = state[new, pair[0], row + 1, inner, :]
            old_q = state[new, pair[1], row + 1, inner, :]
            new_p = (p + p - old_p) + (axial_gain * across + cross_gain * axial) + pulse
            new_q = (q + q - old_q) + (cross_gain * across + velocity * axial) + pulse
            state[new, pair[0], row + 1, inner, :] = new_p
            state[new, pair[1], row + 1, inner, :] = new_q
            if wave == 1:
                image_ref[row, lines, :] += state[new, 0, row + 1, inner, :] * new_p
            before, here = here, beyond

    def one_step(step, unused):
        now = lax.rem(step, 2)

        def one_chunk(first):
            for tile in range(lay.span // TILE):
                for wave in (0, 1):
                    sweep(step, now, 1 - now, first, tile, wave)

        if chunk == lay.width:
            one_chunk(0)
        else:
            lax.fori_loop(0, lay.width // chunk, lambda n, u: (one_chunk(n * chunk), u)[1], 0)
        return unused

    lax.fori_loop(0, lay.steps, one_step, 0)


def clear_edges(state, lay):
    rows, lines = state.shape[2], state.shape[3]
    edge = jnp.zeros((lines,) + state.shape[4:], jnp.float32)
    strip = jnp.zeros((rows, TILE) + state.shape[4:], jnp.float32)
    for time in range(state.shape[0]):
        for field in range(state.shape[1]):
            state[time, field, 0] = edge
            state[time, field, rows - 1] = edge
            state[time, field, :, :TILE] = strip
            state[time, field, :, lines - TILE :] = strip


def wave_kernel(lay, info_ref, source_ref, receiver_ref, *refs):
    waves_own, waves_other, model_own, model_other, pieces = (
        refs[i * lay.domain : (i + 1) * lay.domain] for i in range(5)
    )
    raw, coef_ref, image_ref, state = refs[5 * lay.domain :]
    clear_edges(state, lay)

    def store_wave(row, ref):
        for i in range(8):
            time, field = (i >> 1) & 1, 2 * (i >> 2) + (i & 1)
            state[time, field, row + 1, TILE : TILE + lay.span, :] = ref[i]

    def store_model(row, ref):
        for i in range(5):
            raw[i, row] = ref[i]

    gather_rows(info_ref, lay, waves_own, waves_other, store_wave)
    gather_rows(info_ref, lay, model_own, model_other, store_model)
    make_coefs(raw, coef_ref, lay)
    image_ref[...] = jnp.zeros_like(image_ref)
    run_steps(state, coef_ref, (source_ref, receiver_ref), image_ref, lay)
    d, skip = info_ref[3], info_ref[4]
    if lay.own % TILE == 0:
        skip = pl.multiple_of(skip, TILE)
    for r, piece in enumerate(pieces):
        first = lax.rem(d + r, lay.domain) * lay.rows
        for row in range(lay.rows):
            if lay.own % TILE == 0:
                piece[row] = image_ref[first + row, pl.ds(skip, lay.own), :]
            else:
                piece[row] = pltpu.roll(image_ref[first + row], lay.span - skip, 0)[: lay.own]


def stack_kernel(*refs):
    *arrays, out, sem = refs
    copies = [pltpu.make_async_copy(array, out.at[i], sem.at[i]) for i, array in enumerate(arrays)]
    for copy in copies:
        copy.start()
    for copy in copies:
        copy.wait()


def stacked(arrays):
    return pl.pallas_call(
        stack_kernel,
        out_shape=jax.ShapeDtypeStruct((len(arrays),) + arrays[0].shape, jnp.float32),
        in_specs=[pl.BlockSpec(memory_space=pl.ANY)] * len(arrays),
        out_specs=pl.BlockSpec(memory_space=pltpu.VMEM),
        scratch_shapes=[pltpu.SemaphoreType.DMA((len(arrays),))],
    )(*arrays)


def frame_kernel(lay, info_ref, *refs, slab):
    pieces, outs, frame = refs[: lay.domain], refs[lay.domain : -1], refs[-1]
    frame[...] = jnp.zeros_like(frame)
    room = -(-lay.own // TILE) * TILE + TILE
    filler = jnp.zeros((room - lay.own, frame.shape[-1]), jnp.float32)
    for r, piece in enumerate(pieces):
        place = info_ref[r]
        first = pl.multiple_of(place & ~(TILE - 1), TILE)
        for row in range(lay.rows):
            moved = pltpu.roll(jnp.concatenate([piece[row], filler]), place & (TILE - 1), 0)
            frame[row, pl.ds(first, room), :] += moved
    for r, out in enumerate(outs):
        first = pl.multiple_of(info_ref[lay.domain + r] * slab, TILE)
        for row in range(lay.rows):
            out[row] = frame[row, pl.ds(first, slab), :]


def call(kernel, cost, lay, outs, scratch, info, *operands):
    vmem = pl.BlockSpec(memory_space=pltpu.VMEM)
    held = sum(4 * math.prod(array.shape) for array in [*operands, *outs, *scratch])
    return pl.pallas_call(
        functools.partial(kernel, lay),
        out_shape=outs,
        in_specs=[pl.BlockSpec(memory_space=pltpu.SMEM)] + [vmem] * len(operands),
        out_specs=jax.tree.map(lambda unused: vmem, outs),
        scratch_shapes=scratch,
        compiler_params=pltpu.CompilerParams(vmem_limit_bytes=held + held // 8 + 2**21),
        cost_estimate=pl.CostEstimate(flops=0, bytes_accessed=cost, transcendentals=0),
    )(info, *operands)


def per_device(
    velocity,
    thomsen_eps,
    thomsen_delta,
    tilt_angle,
    azimuth,
    shot_anchor,
    source_x,
    source_y,
    wavelet,
    receiver_x,
    receiver_y,
    traces,
    source_now,
    source_before,
    receiver_now,
    receiver_before,
    slab_owner,
):
    rows, lines, z_count = source_now.shape[2:]
    steps = wavelet.shape[1]
    domain, shots = lax.axis_size("domain"), lax.axis_size("shot")
    lay = Layout(domain, shots, rows, lines, steps)
    d, s = lax.axis_index("domain"), lax.axis_index("shot")
    core = s & 1
    chip_id = lax.rem(d, lay.half)
    works_on = d // lay.half
    zero = jnp.int32(0)

    window = lay.start(chip_id) + lay.shift(core) - lay.pad[0]
    skip = (2 * chip_id + core) * lay.own - window
    info = jnp.stack([chip_id, core, lay.shift(core), d, skip]).astype(jnp.int32)
    tight = lay.pad == (0, 0)

    def wave_messages(fields):
        fields = [jnp.pad(field[0], ((0, 0), (0, 0), lay.pad, (0, 0))) for field in fields]
        messages = []
        for r in range(domain):
            k = lax.rem(d + r, domain)
            spot = (zero, (k & 1) * lay.part, lay.start(k >> 1), zero)
            size = (2, lay.part, lay.chip, z_count)
            messages.append(jnp.concatenate([lax.dynamic_slice(field, spot, size) for field in fields]))
        return messages

    def send(messages):
        return [lax.ppermute(messages[r], ("domain", "shot"), pairs) for r, pairs in lay.rounds()]

    def other_core(messages):
        return [swapped(message, "shot", 1) for message in messages]

    waves = send(wave_messages((source_now, source_before, receiver_now, receiver_before)))
    model = stacked((velocity, thomsen_eps, thomsen_delta, tilt_angle, azimuth))
    slab = model.shape[2]
    whole = jnp.zeros(model.shape[:2] + (shots * slab, z_count), jnp.float32)
    for r in range(shots):
        block = swapped(model, "shot", r) if r else model
        whole = lax.dynamic_update_slice(whole, block, (zero, zero, (s ^ r) * slab, zero))
    model = whole
    anchor = shot_anchor[0]
    if tight:
        first_line = anchor
    else:
        model = lax.dynamic_slice_in_dim(model, anchor, lines, 2)
        model = jnp.pad(model, ((0, 0), (0, 0), lay.pad, (0, 0)))
        first_line = zero
    messages = []
    for r in range(domain):
        k = lax.rem(d + r, domain)
        spot = (zero, (k & 1) * lay.part, first_line + lay.start(k >> 1), zero)
        messages.append(lax.dynamic_slice(model, spot, (5, lay.part, lay.chip, z_count)))
    *messages, waves[-1] = lax.optimization_barrier((*messages, waves[-1]))
    models = send(messages)
    *waves, models[0] = lax.optimization_barrier((*waves, models[0]))
    waves_other, models_other = other_core(waves), other_core(models)

    receivers = receiver_x.shape[1]
    traces, wavelet, receiver_x, receiver_y, source_x, source_y, shot_anchor, unused = lax.optimization_barrier(
        (traces, wavelet, receiver_x, receiver_y, source_x, source_y, shot_anchor, waves[0])
    )
    mine = jnp.concatenate(
        [
            traces[0].reshape(-1),
            wavelet[0],
            receiver_x[0].astype(jnp.float32),
            receiver_y[0].astype(jnp.float32),
            source_x.astype(jnp.float32),
            source_y.astype(jnp.float32),
            shot_anchor.astype(jnp.float32),
        ]
    )
    twin = swapped(mine, "shot", 1)
    table = jnp.where(works_on == core, mine, twin)
    trace_rows = table[: steps * receivers].reshape(steps, receivers)
    at = steps * receivers
    wave_row = table[at : at + steps]
    at += steps
    rec_x = table[at : at + receivers].astype(jnp.int32)
    rec_y = table[at + receivers : at + 2 * receivers].astype(jnp.int32)
    at += 2 * receivers
    src_x, src_y = table[at].astype(jnp.int32), table[at + 1].astype(jnp.int32)
    twin_anchor = twin[at + 2].astype(jnp.int32)
    anchors = (jnp.where(core == 0, anchor, twin_anchor), jnp.where(core == 0, twin_anchor, anchor))

    row_ids = jnp.arange(lay.width)
    line_ids = window + jnp.arange(lay.span)
    spread = ((0, 0), (0, 0), (0, z_count - steps))
    spot = (row_ids[:, None] == src_x) & (line_ids[None, :] == src_y)
    source_pulse = jnp.where(spot[:, :, None], wave_row[None, None, :], 0.0)
    receiver_pulse = jnp.einsum(
        "yr,xtr->xyt",
        (line_ids[:, None] == rec_y[None, :]).astype(jnp.float32),
        jnp.where((row_ids[:, None] == rec_x[None, :])[:, None, :], trace_rows[None], 0.0),
        precision=lax.Precision.HIGHEST,
        preferred_element_type=jnp.float32,
    )
    source_pulse = jnp.pad(source_pulse, spread)
    receiver_pulse = jnp.pad(receiver_pulse, spread)

    block = (lay.width, lay.span, z_count)
    pieces = call(
        wave_kernel,
        60_000_000,
        lay,
        [jax.ShapeDtypeStruct((rows, lay.own, z_count), jnp.float32)] * domain,
        [
            pltpu.VMEM((5,) + block, jnp.float32),
            pltpu.VMEM((COEFS,) + block, jnp.float32),
            pltpu.VMEM(block, jnp.float32),
            pltpu.VMEM((2, 4, lay.width + 2, lay.span + 2 * TILE, z_count), jnp.float32),
        ],
        info,
        source_pulse,
        receiver_pulse,
        *waves,
        *waves_other,
        *models,
        *models_other,
    )

    source = lax.rem(d - jnp.arange(domain) + domain, domain)
    places = jnp.where(source < lay.half, anchors[0], anchors[1])
    places = places + (2 * lax.rem(source, lay.half) + core) * lay.own
    owners = slab_owner[s ^ jnp.arange(shots)]
    pieces = [
        swapped_round(piece, "domain", r) if r else piece for r, piece in enumerate(pieces)
    ]
    room = -(-lay.own // TILE) * TILE + TILE
    parts = call(
        functools.partial(frame_kernel, slab=slab),
        2_000_000,
        lay,
        [jax.ShapeDtypeStruct((rows, slab, z_count), jnp.float32)] * shots,
        [pltpu.VMEM((rows, shots * slab + room, z_count), jnp.float32)],
        jnp.concatenate([places, owners]).astype(jnp.int32),
        *pieces,
    )
    total = parts[0]
    for r in range(1, shots):
        total = total + swapped(parts[r], "shot", r)
    return total / steps


def solution(mesh):
    in_specs = (
        P(("groups", "domain"), "shot", None),
        P(("groups", "domain"), "shot", None),
        P(("groups", "domain"), "shot", None),
        P(("groups", "domain"), "shot", None),
        P(("groups", "domain"), "shot", None),
        P(("groups", "shot")),
        P(("groups", "shot")),
        P(("groups", "shot")),
        P(("groups", "shot"), None),
        P(("groups", "shot"), None),
        P(("groups", "shot"), None),
        P(("groups", "shot"), None, None),
        P(("groups", "shot"), None, "domain", None, None),
        P(("groups", "shot"), None, "domain", None, None),
        P(("groups", "shot"), None, "domain", None, None),
        P(("groups", "shot"), None, "domain", None, None),
        P("groups"),
    )
    out_specs = P(("groups", "domain"), "shot", None)
    return jax.shard_map(
        per_device, mesh=mesh, in_specs=in_specs, out_specs=out_specs, check_vma=False
    )
```

time: 174 us -> 113 us (0.65)
  Pallas kernels: 91.5 us -> 20 us
  starting transfers between devices: 36.8 us -> 54.5 us
  waiting for transfers between devices: 27.8 us -> 21.5 us
    pallas_call x2 -> x1, Pallas kernels: 70.2 us -> 1.96 us  [stacked(): pl.pallas_call(stack_kernel, out_shape=jax.ShapeDtypeStruct((len(arrays),...]
    ppermute x12 -> x8, starting transfers between devices: 24.4 us -> 35.3 us  [send(): lax.ppermute(messages[r], ('domain', 'shot'), pairs)]
    ppermute x9 -> x15, starting transfers between devices: 7.63 us -> 14.5 us  [swapped(): return lax.ppermute(value, axis, [(i, i ^ bit) for i in range(count)])]
    ppermute x9 -> x15, waiting for transfers between devices: 15.9 us -> 12 us  [swapped(): return lax.ppermute(value, axis, [(i, i ^ bit) for i in range(count)])]
    pallas_call x3 -> x2, Pallas kernels: 21.3 us -> 18.1 us  [call(): pl.pallas_call(functools.partial(kernel, lay), out_shape=outs, in_specs=[...]
    concatenate x0 -> x4, other arithmetic: none -> 3.16 us  [wave_messages(): jnp.concatenate([lax.dynamic_slice(field, spot, size) for field in fields])]
    another operation x6 -> x0, other arithmetic: 2.48 us -> none  [the longest x3 1.46 us: per_device(): jnp.stack([jnp.where(upper, twin, model), jnp.where(upper, model, twin)],...]
    ppermute x12 -> x8, waiting for transfers between devices: 8.49 us -> 6.84 us  [send(): lax.ppermute(messages[r], ('domain', 'shot'), pairs)]
  transfers between devices with their start and end apart: 24 -> 26, of which waited for: 10 -> 9; matrix products, arithmetic and copies ran while one was open for 5% -> 8% of each run, Pallas kernels for 47% -> 0%
where the time goes in v3:
time: 113 us; the launch traced here: 112 us
  starting transfers between devices  54.5 us (48%)
  waiting for transfers between devices  21.5 us (19%)
  Pallas kernels  20 us (18%)
  local copies, waits for them, and re-layouts  7.52 us (7%)
  other arithmetic  4.25 us (4%)
  between operations  4.18 us (4%)
    ppermute x8, starting transfers between devices, send(): lax.ppermute(messages[r], ('domain', 'shot'), pairs)  35.3 us
    pallas_call x2, Pallas kernels, call(): pl.pallas_call(functools.partial(kernel, lay), out_shape=outs, in_specs=[...  18.1 us
    ppermute x15, starting transfers between devices, swapped(): return lax.ppermute(value, axis, [(i, i ^ bit) for i in range(count)])  14.5 us
    ppermute x15, waiting for transfers between devices, swapped(): return lax.ppermute(value, axis, [(i, i ^ bit) for i in range(count)])  12 us
    ppermute x8, waiting for transfers between devices, send(): lax.ppermute(messages[r], ('domain', 'shot'), pairs)  6.84 us
    ppermute x3, starting transfers between devices, swapped_round(): lax.ppermute(value, axis, [(i, (i + r) % count) for i in range(count)])  4.69 us
    concatenate x4, other arithmetic, wave_messages(): jnp.concatenate([lax.dynamic_slice(field, spot, size) for field in fields])  3.16 us
    ppermute x3, waiting for transfers between devices, swapped_round(): lax.ppermute(value, axis, [(i, (i + r) % count) for i in range(count)])  2.72 us
  transfers between devices with their start and end apart: 26, of which 9 were waited for; matrix products, arithmetic and copies ran while one was open for 8% of the time, Pallas kernels for 0%

profile of v3, /device:TPU:0, one launch (start us, length us, event | category | flops | bytes accessed | tf_op | source)
XLA Modules:
  0.0 112.4 jit_solution(13597402436519576530)
XLA Ops:
  0.0 2.0 %shard_map.163 = f32[5,2,96,128]{3,2,1,0:T(8,128)} custom-call(f32[2,96,128]{2,1,0:T(8,128)} %refs_0_.1, f32[2,96,128]{2,1,0:T(8,128)} %refs_1_.1, f32[2,96,128]{2,1,0:T(8,128)} %refs_2_.1, f32[2,96,128]{2,1,0:T(8,128)} %refs_3_.1, f32[2,96,128]{2,1,0:T(8,128)} %refs_4_.1), custom_call_target="tpu_custom_call" | custom-call | tf_op jit(solution)/shard_map/pallas_call | solution.py:244
  2.5 2.6 %collective-permute-start.4 = (f32[5,2,96,128]{3,2,1,0:T(8,128)}, f32[5,2,96,128]{3,2,1,0:T(8,128)S(1)}, u32[]{:S(2)}, u32[]{:S(2)}) collective-permute-start(f32[5,2,96,128]{3,2,1,0:T(8,128)} %shard_map.163), channel_id=1, source_target_pairs={{0,2},{1,3},{2,0},{3,1},{4,6},{5,7},{6,4},{7,5},{8,10},{9,11},{10,... | collective-permute-start | bytes 1474568 | tf_op jit(solution)/shard_map/ppermute | solution.py:58
  5.1 1.3 %dynamic-slice_bitcast_fusion.2 = (f32[2,1,104,128]{3,2,1,0:T(8,128)S(1)}, f32[2,1,104,128]{3,2,1,0:T(8,128)S(1)}, f32[2,1,104,128]{3,2,1,0:T(8,128)S(1)}, f32[2...) fusion(f32[1,2,2,192,128]{4,3,2,1,0:T(8,128)} %param.30, ...), kind=kLoop, calls=%fused_computation.9 | loop fusion | bytes 1703968 | tf_op jit(solution)/shard_map/dynamic_slice | solution.py:325
  6.5 0.8 pad_maximum_fusion.3
  7.3 3.7 %collective-permute-start.6 = (f32[8,1,104,128]{3,2,1,0:T(8,128)}, f32[8,1,104,128]{3,2,1,0:T(8,128)S(1)}, u32[]{:S(2)}, u32[]{:S(2)}) collective-permute-start(f32[8,1,104,128]{3,2,1,0:T(8,128)} %pad_maximum_fusion.3), channel_id=1, source_target_pairs={{0,5},{1,13},{2,7},{3,15},{4,0},{5,8},{6,2},{7,10},{8,1},{9,9},{10... | collective-permute-start | bytes 1277960 | tf_op jit(solution)/shard_map/ppermute | solution.py:329
  11.0 0.8 pad_maximum_fusion.2
  12.8 0.8 pad_maximum_fusion.1
  13.5 0.8 pad_maximum_fusion
  14.6 4.2 %collective-permute-start.1 = (f32[8,1,104,128]{3,2,1,0:T(8,128)}, f32[8,1,104,128]{3,2,1,0:T(8,128)S(1)}, u32[]{:S(2)}, u32[]{:S(2)}) collective-permute-start(f32[8,1,104,128]{3,2,1,0:T(8,128)} %pad_maximum_fusion.1), channel_id=1, source_target_pairs={{0,1},{1,9},{2,3},{3,11},{4,4},{5,12},{6,6},{7,14},{8,5},{9,13},{1... | collective-permute-start | bytes 1277960 | tf_op jit(solution)/shard_map/ppermute | solution.py:329
  18.7 1.1 constant_dynamic-update-slice_fusion.2
  19.9 1.7 %collective-permute-start = (f32[8,1,104,128]{3,2,1,0:T(8,128)}, f32[8,1,104,128]{3,2,1,0:T(8,128)S(1)}, u32[]{:S(2)}, u32[]{:S(2)}) collective-permute-start(f32[8,1,104,128]{3,2,1,0:T(8,128)} %pad_maximum_fusion), channel_id=1, source_target_pairs={{0,0},{1,8},{2,2},{3,10},{4,1},{5,9},{6,3},{7,11},{8,4},{9,12},{10... | collective-permute-start | bytes 1277960 | tf_op jit(solution)/shard_map/ppermute | solution.py:329
  21.6 5.8 %collective-permute-done.5 = f32[5,2,96,128]{3,2,1,0:T(8,128)S(1)} collective-permute-done((f32[5,2,96,128]{3,2,1,0:T(8,128)}, f32[5,2,96,128]{3,2,1,0:T(8,128)S(1)}, u32[]{:S(2)}, u32[]{:S(2)}) %collective-permute-start.5) | collective-permute-done | bytes 491552 | tf_op jit(solution)/shard_map/ppermute | solution.py:58
  27.5 0.7 collective-permute-start.7
  28.2 5.9 %collective-permute-start.13 = (f32[5,1,104,128]{3,2,1,0:T(8,128)S(1)}, f32[5,1,104,128]{3,2,1,0:T(8,128)}, u32[]{:S(2)}, u32[]{:S(2)}) collective-permute-start(f32[5,1,104,128]{3,2,1,0:T(8,128)S(1)} %get-tuple-element.44), channel_id=1, source_target_pairs={{0,1},{1,9},{2,3},{3,11},{4,4},{5,12},{6,6},{7,14},{8,5},{9,13},{1... | collective-permute-start | bytes 798728 | tf_op jit(solution)/shard_map/ppermute | solution.py:329
  35.6 3.4 %collective-permute-done.1.refs_1_ = f32[8,1,104,128]{3,2,1,0:T(8,128)S(1)} collective-permute-done((f32[8,1,104,128]{3,2,1,0:T(8,128)}, f32[8,1,104,128]{3,2,1,0:T(8,128)S(1)}, u32[]{:S(2)}, u32[]{:S(2)}) %collective-permute-start.1) | collective-permute-done | bytes 426016 | tf_op jit(solution)/shard_map/ppermute | solution.py:329
  39.2 6.5 %collective-permute-start.8 = (f32[2571]{0:T(1024)S(1)}, f32[2571]{0:T(1024)S(1)}, u32[]{:S(2)}, u32[]{:S(2)}) collective-permute-start(f32[2571]{0:T(1024)S(1)} %concatenate.22), channel_id=1, source_target_pairs={{0,1},{1,0},{2,3},{3,2},{4,5},{5,4},{6,7},{7,6},{8,9},{9,8},{10,11... | collective-permute-start | bytes 30860 | tf_op jit(solution)/shard_map/ppermute | solution.py:58
  46.4 18.9 %collective-permute-start.15 = (f32[5,1,104,128]{3,2,1,0:T(8,128)S(1)}, f32[5,1,104,128]{3,2,1,0:T(8,128)}, u32[]{:S(2)}, u32[]{:S(2)}) collective-permute-start(f32[5,1,104,128]{3,2,1,0:T(8,128)S(1)} %get-tuple-element.46), channel_id=1, source_target_pairs={{0,5},{1,13},{2,7},{3,15},{4,0},{5,8},{6,2},{7,10},{8,1},{9,9},{10... | collective-permute-start | bytes 798728 | tf_op jit(solution)/shard_map/ppermute | solution.py:329
  65.8 1.8 %collective-permute-done.14.refs_10_ = f32[5,1,104,128]{3,2,1,0:T(8,128)} collective-permute-done((f32[5,1,104,128]{3,2,1,0:T(8,128)S(1)}, f32[5,1,104,128]{3,2,1,0:T(8,128)}, u32[]{:S(2)}, u32[]{:S(2)}) %collective-permute-start.14) | collective-permute-done | bytes 266272 | tf_op jit(solution)/shard_map/ppermute | solution.py:329
  70.5 1.6 %collective-permute-done.15.refs_11_ = f32[5,1,104,128]{3,2,1,0:T(8,128)} collective-permute-done((f32[5,1,104,128]{3,2,1,0:T(8,128)S(1)}, f32[5,1,104,128]{3,2,1,0:T(8,128)}, u32[]{:S(2)}, u32[]{:S(2)}) %collective-permute-start.15) | collective-permute-done | bytes 266272 | tf_op jit(solution)/shard_map/ppermute | solution.py:329
  72.1 1.1 collective-permute-start.10
  73.2 0.7 copy-done.3
  75.9 1.0 collective-permute-done.19.refs_15_
  77.0 0.9 copy-done.2
  78.0 0.9 copy-done.4
  78.9 17.4 %shard_map.164 = (f32[2,48,128]{2,1,0:T(8,128)S(1)}, f32[2,48,128]{2,1,0:T(8,128)S(1)}, f32[2,48,128]{2,1,0:T(8,128)S(1)}, f32[2,48,128]{2,1,0:T(8,128)S(1)}) custom-call(s32[5]{0:T(128)S(1)} %stack.23.info_ref, f32[8,64,128]{2,1,0:T(8,128)S(1)} %pad.7.source_ref, f32[8,64,128]{2,1,0:T(8,128)S(1)} %pad.8.receiver_ref, ...), custom_call_target="tpu_custom_call" | custom-call | bytes 60000000 | tf_op jit(solution)/shard_map/pallas_call | solution.py:273
  96.4 2.9 %collective-permute-start.21 = (f32[2,48,128]{2,1,0:T(8,128)S(1)}, f32[2,48,128]{2,1,0:T(8,128)S(1)}, u32[]{:S(2)}, u32[]{:S(2)}) collective-permute-start(f32[2,48,128]{2,1,0:T(8,128)S(1)} %get-tuple-element.49), channel_id=1, source_target_pairs={{0,8},{4,12},{8,0},{12,4},{1,9},{5,13},{9,1},{13,5},{2,10},{6,14},... | collective-permute-start | bytes 147464 | tf_op jit(solution)/shard_map/ppermute | solution.py:67
  99.3 1.7 %collective-permute-start.22 = (f32[2,48,128]{2,1,0:T(8,128)S(1)}, f32[2,48,128]{2,1,0:T(8,128)S(1)}, u32[]{:S(2)}, u32[]{:S(2)}) collective-permute-start(f32[2,48,128]{2,1,0:T(8,128)S(1)} %get-tuple-element.50), channel_id=1, source_target_pairs={{0,12},{4,0},{8,4},{12,8},{1,13},{5,1},{9,5},{13,9},{2,14},{6,2},{... | collective-permute-start | bytes 147464 | tf_op jit(solution)/shard_map/ppermute | solution.py:67
  101.1 1.7 %collective-permute-done.20.refs_1_ = f32[2,48,128]{2,1,0:T(8,128)S(1)} collective-permute-done((f32[2,48,128]{2,1,0:T(8,128)S(1)}, f32[2,48,128]{2,1,0:T(8,128)S(1)}, u32[]{:S(2)}, u32[]{:S(2)}) %collective-permute-start.20) | collective-permute-done | bytes 49184 | tf_op jit(solution)/shard_map/ppermute | solution.py:67
  102.8 1.0 collective-permute-done.21.refs_2_
  104.6 2.0 %collective-permute-start.24 = (f32[2,96,128]{2,1,0:T(8,128)S(1)}, f32[2,96,128]{2,1,0:T(8,128)S(1)}, u32[]{:S(2)}, u32[]{:S(2)}) collective-permute-start(f32[2,96,128]{2,1,0:T(8,128)S(1)} %get-tuple-element.53), channel_id=1, source_target_pairs={{0,2},{1,3},{2,0},{3,1},{4,6},{5,7},{6,4},{7,5},{8,10},{9,11},{10,... | collective-permute-start | bytes 294920 | tf_op jit(solution)/shard_map/ppermute | solution.py:58
  106.6 3.6 %collective-permute-done.24 = f32[2,96,128]{2,1,0:T(8,128)S(1)} collective-permute-done((f32[2,96,128]{2,1,0:T(8,128)S(1)}, f32[2,96,128]{2,1,0:T(8,128)S(1)}, u32[]{:S(2)}, u32[]{:S(2)}) %collective-permute-start.24) | collective-permute-done | bytes 98336 | tf_op jit(solution)/shard_map/ppermute | solution.py:58
  110.2 1.5 %collective-permute-done.25 = f32[2,96,128]{2,1,0:T(8,128)S(1)} collective-permute-done((f32[2,96,128]{2,1,0:T(8,128)S(1)}, f32[2,96,128]{2,1,0:T(8,128)S(1)}, u32[]{:S(2)}, u32[]{:S(2)}) %collective-permute-start.25) | collective-permute-done | bytes 98336 | tf_op jit(solution)/shard_map/ppermute | solution.py:58
  (86 shorter events, 7.5 us)
Async XLA Ops:
  0.0 45.6 %copy-start = (s32[4]{0:T(128)S(1)}, s32[4]{0:T(128)}, u32[]{:S(2)}) copy-start(s32[4]{0:T(128)} %param.33) | copy-start | bytes 52
  2.0 12.6 %collective-permute-start.3 = (f32[5,2,96,128]{3,2,1,0:T(8,128)}, f32[5,2,96,128]{3,2,1,0:T(8,128)}, u32[]{:S(2)}, u32[]{:S(2)}) collective-permute-start(f32[5,2,96,128]{3,2,1,0:T(8,128)} %shard_map.163), channel_id=1, source_target_pairs={{0,1},{1,0},{2,3},{3,2},{4,5},{5,4},{6,7},{7,6},{8,9},{9,8},{10,11... | collective-permute-start | bytes 1474568 | tf_op jit(solution)/shard_map/ppermute | solution.py:58
  2.5 17.4 %collective-permute-start.4 = (f32[5,2,96,128]{3,2,1,0:T(8,128)}, f32[5,2,96,128]{3,2,1,0:T(8,128)S(1)}, u32[]{:S(2)}, u32[]{:S(2)}) collective-permute-start(f32[5,2,96,128]{3,2,1,0:T(8,128)} %shard_map.163), channel_id=1, source_target_pairs={{0,2},{1,3},{2,0},{3,1},{4,6},{5,7},{6,4},{7,5},{8,10},{9,11},{10,... | collective-permute-start | bytes 1474568 | tf_op jit(solution)/shard_map/ppermute | solution.py:58
  5.1 22.3 %collective-permute-start.5 = (f32[5,2,96,128]{3,2,1,0:T(8,128)}, f32[5,2,96,128]{3,2,1,0:T(8,128)S(1)}, u32[]{:S(2)}, u32[]{:S(2)}) collective-permute-start(f32[5,2,96,128]{3,2,1,0:T(8,128)} %shard_map.163), channel_id=1, source_target_pairs={{0,3},{1,2},{2,1},{3,0},{4,7},{5,6},{6,5},{7,4},{8,11},{9,10},{10,... | collective-permute-start | bytes 1474568 | tf_op jit(solution)/shard_map/ppermute | solution.py:58
  7.3 20.2 %collective-permute-start.6 = (f32[8,1,104,128]{3,2,1,0:T(8,128)}, f32[8,1,104,128]{3,2,1,0:T(8,128)S(1)}, u32[]{:S(2)}, u32[]{:S(2)}) collective-permute-start(f32[8,1,104,128]{3,2,1,0:T(8,128)} %pad_maximum_fusion.3), channel_id=1, source_target_pairs={{0,5},{1,13},{2,7},{3,15},{4,0},{5,8},{6,2},{7,10},{8,1},{9,9},{10... | collective-permute-start | bytes 1277960 | tf_op jit(solution)/shard_map/ppermute | solution.py:329
  11.8 22.3 %collective-permute-start.2 = (f32[8,1,104,128]{3,2,1,0:T(8,128)}, f32[8,1,104,128]{3,2,1,0:T(8,128)S(1)}, u32[]{:S(2)}, u32[]{:S(2)}) collective-permute-start(f32[8,1,104,128]{3,2,1,0:T(8,128)} %pad_maximum_fusion.2), channel_id=1, source_target_pairs={{0,4},{1,12},{2,6},{3,14},{4,5},{5,13},{6,7},{7,15},{8,0},{9,8},{1... | collective-permute-start | bytes 1277960 | tf_op jit(solution)/shard_map/ppermute | solution.py:329
  14.6 24.4 %collective-permute-start.1 = (f32[8,1,104,128]{3,2,1,0:T(8,128)}, f32[8,1,104,128]{3,2,1,0:T(8,128)S(1)}, u32[]{:S(2)}, u32[]{:S(2)}) collective-permute-start(f32[8,1,104,128]{3,2,1,0:T(8,128)} %pad_maximum_fusion.1), channel_id=1, source_target_pairs={{0,1},{1,9},{2,3},{3,11},{4,4},{5,12},{6,6},{7,14},{8,5},{9,13},{1... | collective-permute-start | bytes 1277960 | tf_op jit(solution)/shard_map/ppermute | solution.py:329
  19.8 19.2 %copy-start.8 = (f32[1,8,256]{2,1,0:T(8,128)S(1)}, f32[1,8,256]{2,1,0:T(8,128)}, u32[]{:S(2)}) copy-start(f32[1,8,256]{2,1,0:T(8,128)} %param.28) | copy-start | bytes 24580
  19.8 19.2 %copy-start.9 = (s32[1,256]{1,0:T(1,128)S(1)}, s32[1,256]{1,0:T(1,128)}, u32[]{:S(2)}) copy-start(s32[1,256]{1,0:T(1,128)} %param.26) | copy-start | bytes 3076
  19.8 19.2 %copy-start.10 = (s32[1,256]{1,0:T(1,128)S(1)}, s32[1,256]{1,0:T(1,128)}, u32[]{:S(2)}) copy-start(s32[1,256]{1,0:T(1,128)} %param.27) | copy-start | bytes 3076
  19.8 19.2 %copy-start.11 = (f32[1,8]{1,0:T(1,128)S(1)}, f32[1,8]{1,0:T(1,128)}, u32[]{:S(2)}) copy-start(f32[1,8]{1,0:T(1,128)} %param.25) | copy-start | bytes 100
  19.9 19.1 %collective-permute-start = (f32[8,1,104,128]{3,2,1,0:T(8,128)}, f32[8,1,104,128]{3,2,1,0:T(8,128)S(1)}, u32[]{:S(2)}, u32[]{:S(2)}) collective-permute-start(f32[8,1,104,128]{3,2,1,0:T(8,128)} %pad_maximum_fusion), channel_id=1, source_target_pairs={{0,0},{1,8},{2,2},{3,10},{4,1},{5,9},{6,3},{7,11},{8,4},{9,12},{10... | collective-permute-start | bytes 1277960 | tf_op jit(solution)/shard_map/ppermute | solution.py:329
  27.5 11.5 %collective-permute-start.7 = (f32[5,1,104,128]{3,2,1,0:T(8,128)S(1)}, f32[5,1,104,128]{3,2,1,0:T(8,128)S(1)}, u32[]{:S(2)}, u32[]{:S(2)}) collective-permute-start(f32[5,1,104,128]{3,2,1,0:T(8,128)S(1)} %get-tuple-element.31), channel_id=1, source_target_pairs={{0,0},{1,8},{2,2},{3,10},{4,1},{5,9},{6,3},{7,11},{8,4},{9,12},{10... | collective-permute-start | bytes 798728 | tf_op jit(solution)/shard_map/ppermute | solution.py:329
  28.2 37.1 %collective-permute-start.13 = (f32[5,1,104,128]{3,2,1,0:T(8,128)S(1)}, f32[5,1,104,128]{3,2,1,0:T(8,128)}, u32[]{:S(2)}, u32[]{:S(2)}) collective-permute-start(f32[5,1,104,128]{3,2,1,0:T(8,128)S(1)} %get-tuple-element.44), channel_id=1, source_target_pairs={{0,1},{1,9},{2,3},{3,11},{4,4},{5,12},{6,6},{7,14},{8,5},{9,13},{1... | collective-permute-start | bytes 798728 | tf_op jit(solution)/shard_map/ppermute | solution.py:329
  34.2 33.5 %collective-permute-start.14 = (f32[5,1,104,128]{3,2,1,0:T(8,128)S(1)}, f32[5,1,104,128]{3,2,1,0:T(8,128)}, u32[]{:S(2)}, u32[]{:S(2)}) collective-permute-start(f32[5,1,104,128]{3,2,1,0:T(8,128)S(1)} %get-tuple-element.45), channel_id=1, source_target_pairs={{0,4},{1,12},{2,6},{3,14},{4,5},{5,13},{6,7},{7,15},{8,0},{9,8},{1... | collective-permute-start | bytes 798728 | tf_op jit(solution)/shard_map/ppermute | solution.py:329
  39.0 35.5 %copy-start.1 = (f32[5,1,104,128]{3,2,1,0:T(8,128)}, f32[5,1,104,128]{3,2,1,0:T(8,128)S(1)}, u32[]{:S(2)}) copy-start(f32[5,1,104,128]{3,2,1,0:T(8,128)S(1)} %collective-permute-done.7.refs_8_) | copy-start | bytes 798724
  39.2 28.5 %collective-permute-start.8 = (f32[2571]{0:T(1024)S(1)}, f32[2571]{0:T(1024)S(1)}, u32[]{:S(2)}, u32[]{:S(2)}) collective-permute-start(f32[2571]{0:T(1024)S(1)} %concatenate.22), channel_id=1, source_target_pairs={{0,1},{1,0},{2,3},{3,2},{4,5},{5,4},{6,7},{7,6},{8,9},{9,8},{10,11... | collective-permute-start | bytes 30860 | tf_op jit(solution)/shard_map/ppermute | solution.py:58
  46.4 25.7 %collective-permute-start.15 = (f32[5,1,104,128]{3,2,1,0:T(8,128)S(1)}, f32[5,1,104,128]{3,2,1,0:T(8,128)}, u32[]{:S(2)}, u32[]{:S(2)}) collective-permute-start(f32[5,1,104,128]{3,2,1,0:T(8,128)S(1)} %get-tuple-element.46), channel_id=1, source_target_pairs={{0,5},{1,13},{2,7},{3,15},{4,0},{5,8},{6,2},{7,10},{8,1},{9,9},{10... | collective-permute-start | bytes 798728 | tf_op jit(solution)/shard_map/ppermute | solution.py:329
  65.3 11.8 %collective-permute-start.9 = (f32[8,1,104,128]{3,2,1,0:T(8,128)S(1)}, f32[8,1,104,128]{3,2,1,0:T(8,128)S(1)}, u32[]{:S(2)}, u32[]{:S(2)}) collective-permute-start(f32[8,1,104,128]{3,2,1,0:T(8,128)S(1)} %collective-permute-done.refs_0_), channel_id=1, source_target_pairs={{0,1},{1,0},{2,3},{3,2},{4,5},{5,4},{6,7},{7,6},{8,9},{9,8},{10,11... | collective-permute-start | bytes 1277960 | tf_op jit(solution)/shard_map/ppermute | solution.py:58
  65.3 7.8 %collective-permute-start.16 = (f32[5,1,104,128]{3,2,1,0:T(8,128)S(1)}, f32[5,1,104,128]{3,2,1,0:T(8,128)S(1)}, u32[]{:S(2)}, u32[]{:S(2)}) collective-permute-start(f32[5,1,104,128]{3,2,1,0:T(8,128)S(1)} %collective-permute-done.7.refs_8_), channel_id=1, source_target_pairs={{0,1},{1,0},{2,3},{3,2},{4,5},{5,4},{6,7},{7,6},{8,9},{9,8},{10,11... | collective-permute-start | bytes 798728 | tf_op jit(solution)/shard_map/ppermute | solution.py:58
  67.7 6.2 %collective-permute-start.17 = (f32[5,1,104,128]{3,2,1,0:T(8,128)}, f32[5,1,104,128]{3,2,1,0:T(8,128)}, u32[]{:S(2)}, u32[]{:S(2)}) collective-permute-start(f32[5,1,104,128]{3,2,1,0:T(8,128)} %collective-permute-done.13.refs_9_), channel_id=1, source_target_pairs={{0,1},{1,0},{2,3},{3,2},{4,5},{5,4},{6,7},{7,6},{8,9},{9,8},{10,11... | collective-permute-start | bytes 798728 | tf_op jit(solution)/shard_map/ppermute | solution.py:58
  67.7 6.8 %collective-permute-start.18 = (f32[5,1,104,128]{3,2,1,0:T(8,128)}, f32[5,1,104,128]{3,2,1,0:T(8,128)}, u32[]{:S(2)}, u32[]{:S(2)}) collective-permute-start(f32[5,1,104,128]{3,2,1,0:T(8,128)} %collective-permute-done.14.refs_10_), channel_id=1, source_target_pairs={{0,1},{1,0},{2,3},{3,2},{4,5},{5,4},{6,7},{7,6},{8,9},{9,8},{10,11... | collective-permute-start | bytes 798728 | tf_op jit(solution)/shard_map/ppermute | solution.py:58
  72.1 4.9 %collective-permute-start.10 = (f32[8,1,104,128]{3,2,1,0:T(8,128)S(1)}, f32[8,1,104,128]{3,2,1,0:T(8,128)S(1)}, u32[]{:S(2)}, u32[]{:S(2)}) collective-permute-start(f32[8,1,104,128]{3,2,1,0:T(8,128)S(1)} %collective-permute-done.1.refs_1_), channel_id=1, source_target_pairs={{0,1},{1,0},{2,3},{3,2},{4,5},{5,4},{6,7},{7,6},{8,9},{9,8},{10,11... | collective-permute-start | bytes 1277960 | tf_op jit(solution)/shard_map/ppermute | solution.py:58
  73.9 3.1 %collective-permute-start.11 = (f32[8,1,104,128]{3,2,1,0:T(8,128)S(1)}, f32[8,1,104,128]{3,2,1,0:T(8,128)S(1)}, u32[]{:S(2)}, u32[]{:S(2)}) collective-permute-start(f32[8,1,104,128]{3,2,1,0:T(8,128)S(1)} %collective-permute-done.2.refs_2_), channel_id=1, source_target_pairs={{0,1},{1,0},{2,3},{3,2},{4,5},{5,4},{6,7},{7,6},{8,9},{9,8},{10,11... | collective-permute-start | bytes 1277960 | tf_op jit(solution)/shard_map/ppermute | solution.py:58
  73.9 3.1 %collective-permute-start.12 = (f32[8,1,104,128]{3,2,1,0:T(8,128)S(1)}, f32[8,1,104,128]{3,2,1,0:T(8,128)}, u32[]{:S(2)}, u32[]{:S(2)}) collective-permute-start(f32[8,1,104,128]{3,2,1,0:T(8,128)S(1)} %collective-permute-done.6.refs_3_), channel_id=1, source_target_pairs={{0,1},{1,0},{2,3},{3,2},{4,5},{5,4},{6,7},{7,6},{8,9},{9,8},{10,11... | collective-permute-start | bytes 1277960 | tf_op jit(solution)/shard_map/ppermute | solution.py:58
  74.5 2.5 %collective-permute-start.19 = (f32[5,1,104,128]{3,2,1,0:T(8,128)}, f32[5,1,104,128]{3,2,1,0:T(8,128)}, u32[]{:S(2)}, u32[]{:S(2)}) collective-permute-start(f32[5,1,104,128]{3,2,1,0:T(8,128)} %collective-permute-done.15.refs_11_), channel_id=1, source_target_pairs={{0,1},{1,0},{2,3},{3,2},{4,5},{5,4},{6,7},{7,6},{8,9},{9,8},{10,11... | collective-permute-start | bytes 798728 | tf_op jit(solution)/shard_map/ppermute | solution.py:58
  96.4 6.5 %collective-permute-start.20 = (f32[2,48,128]{2,1,0:T(8,128)S(1)}, f32[2,48,128]{2,1,0:T(8,128)S(1)}, u32[]{:S(2)}, u32[]{:S(2)}) collective-permute-start(f32[2,48,128]{2,1,0:T(8,128)S(1)} %get-tuple-element.48), channel_id=1, source_target_pairs={{0,4},{4,8},{8,12},{12,0},{1,5},{5,9},{9,13},{13,1},{2,6},{6,10},{... | collective-permute-start | bytes 147464 | tf_op jit(solution)/shard_map/ppermute | solution.py:67
  96.4 7.4 %collective-permute-start.21 = (f32[2,48,128]{2,1,0:T(8,128)S(1)}, f32[2,48,128]{2,1,0:T(8,128)S(1)}, u32[]{:S(2)}, u32[]{:S(2)}) collective-permute-start(f32[2,48,128]{2,1,0:T(8,128)S(1)} %get-tuple-element.49), channel_id=1, source_target_pairs={{0,8},{4,12},{8,0},{12,4},{1,9},{5,13},{9,1},{13,5},{2,10},{6,14},... | collective-permute-start | bytes 147464 | tf_op jit(solution)/shard_map/ppermute | solution.py:67
  99.3 4.5 %collective-permute-start.22 = (f32[2,48,128]{2,1,0:T(8,128)S(1)}, f32[2,48,128]{2,1,0:T(8,128)S(1)}, u32[]{:S(2)}, u32[]{:S(2)}) collective-permute-start(f32[2,48,128]{2,1,0:T(8,128)S(1)} %get-tuple-element.50), channel_id=1, source_target_pairs={{0,12},{4,0},{8,4},{12,8},{1,13},{5,1},{9,5},{13,9},{2,14},{6,2},{... | collective-permute-start | bytes 147464 | tf_op jit(solution)/shard_map/ppermute | solution.py:67
  104.5 2.1 %collective-permute-start.23 = (f32[2,96,128]{2,1,0:T(8,128)S(1)}, f32[2,96,128]{2,1,0:T(8,128)S(1)}, u32[]{:S(2)}, u32[]{:S(2)}) collective-permute-start(f32[2,96,128]{2,1,0:T(8,128)S(1)} %get-tuple-element.52), channel_id=1, source_target_pairs={{0,1},{1,0},{2,3},{3,2},{4,5},{5,4},{6,7},{7,6},{8,9},{9,8},{10,11... | collective-permute-start | bytes 294920 | tf_op jit(solution)/shard_map/ppermute | solution.py:58
  104.6 5.6 %collective-permute-start.24 = (f32[2,96,128]{2,1,0:T(8,128)S(1)}, f32[2,96,128]{2,1,0:T(8,128)S(1)}, u32[]{:S(2)}, u32[]{:S(2)}) collective-permute-start(f32[2,96,128]{2,1,0:T(8,128)S(1)} %get-tuple-element.53), channel_id=1, source_target_pairs={{0,2},{1,3},{2,0},{3,1},{4,6},{5,7},{6,4},{7,5},{8,10},{9,11},{10,... | collective-permute-start | bytes 294920 | tf_op jit(solution)/shard_map/ppermute | solution.py:58
  106.6 5.2 %collective-permute-start.25 = (f32[2,96,128]{2,1,0:T(8,128)S(1)}, f32[2,96,128]{2,1,0:T(8,128)S(1)}, u32[]{:S(2)}, u32[]{:S(2)}) collective-permute-start(f32[2,96,128]{2,1,0:T(8,128)S(1)} %get-tuple-element.54), channel_id=1, source_target_pairs={{0,3},{1,2},{2,1},{3,0},{4,7},{5,6},{6,5},{7,4},{8,11},{9,10},{10,... | collective-permute-start | bytes 294920 | tf_op jit(solution)/shard_map/ppermute | solution.py:58
  (6 other events, 18.2 us)

commit v4 on v3

v4 whole, which is shorter than its diff:
```python
import functools
import math

import jax
import jax.numpy as jnp
from jax import lax
from jax.experimental import pallas as pl
from jax.experimental.pallas import tpu as pltpu
from jax.sharding import PartitionSpec as P

SRC_Z = 3
REC_Z = 1
TILE = 8
COEFS = 16


class Layout:
    def __init__(self, domain, shots, rows, lines, steps):
        self.domain, self.shots, self.rows, self.lines, self.steps = domain, shots, rows, lines, steps
        self.half = domain // 2
        self.part = rows // 2
        self.width = rows * domain
        self.own = lines // domain
        halo = -(-steps // TILE) * TILE
        if self.half == 2 and self.own % TILE == 0:
            self.pad = (0, 0)
            self.chip = 2 * self.own + halo
            self.stride = lines - self.chip
            self.span = self.own + 2 * halo
        else:
            self.chip = -(-(2 * self.own + 2 * halo) // TILE) * TILE
            self.pad = (halo, max(0, (self.half - 1) * 2 * self.own + self.chip - halo - lines))
            self.stride = 2 * self.own
            self.span = self.chip

    def start(self, kc):
        return kc * self.stride

    def shift(self, c):
        return c * (self.chip - self.span)

    def position(self):
        d, s = lax.axis_index("domain"), lax.axis_index("shot")
        return lax.rem(d, self.half), s & 1, d, d // self.half

    def rounds(self):
        count = self.domain * self.shots
        for r in range(self.domain):
            pairs = []
            for d in range(self.domain):
                for s in range(self.shots):
                    k = (d + r) % self.domain
                    to_d = self.half * (s & 1) + (k >> 1)
                    to_s = (s & ~1) | (k & 1)
                    pairs.append((d * self.shots + s, to_d * self.shots + to_s))
            assert len({pair[1] for pair in pairs}) == count
            yield r, pairs


def swapped(value, axis, bit):
    count = lax.axis_size(axis)
    return lax.ppermute(value, axis, [(i, i ^ bit) for i in range(count)])


def tied(value, *others):
    return lax.optimization_barrier((value, *others))[0]


def swapped_round(value, axis, r):
    count = lax.axis_size(axis)
    return lax.ppermute(value, axis, [(i, (i + r) % count) for i in range(count)])


def gather_rows(lay, own_refs, other_refs, store):
    kc, c, unused, unused = lay.position()
    window = pl.ds(pl.multiple_of(lay.shift(c), TILE), lay.span)
    for core, refs in ((c, own_refs), (1 - c, other_refs)):
        k = 2 * kc + core
        for r, ref in enumerate(refs):
            source = lax.rem(k - r + lay.domain, lay.domain)
            for part in range(lay.part):
                store(source * lay.rows + core * lay.part + part, ref.at[:, part, window, :])


def table_kernel(traces, wavelet, rec_x, rec_y, src_x, src_y, anchor, table):
    steps = traces.shape[1]
    table[...] = jnp.zeros_like(table)
    table[:steps] = traces[0]
    table[steps : steps + 1, :steps] = wavelet[...]
    row = (1, table.shape[1])
    table[steps + 1 : steps + 2] = rec_x[...].astype(jnp.float32)
    table[steps + 2 : steps + 3] = rec_y[...].astype(jnp.float32)
    for i, scalar in enumerate((src_x, src_y, anchor)):
        table[steps + 3 + i : steps + 4 + i] = jnp.full(row, scalar[0], jnp.int32).astype(jnp.float32)


def table_of(*arrays):
    steps, receivers = arrays[0].shape[1:]
    smem, vmem = (pl.BlockSpec(memory_space=space) for space in (pltpu.SMEM, pltpu.VMEM))
    return pl.pallas_call(
        table_kernel,
        out_shape=jax.ShapeDtypeStruct((-(-(steps + 6) // TILE) * TILE, receivers), jnp.float32),
        in_specs=[vmem] * 4 + [smem] * 3,
        out_specs=vmem,
        compiler_params=pltpu.CompilerParams(vmem_limit_bytes=2**21),
    )(*arrays)


def pulse_kernel(lay, mine, twin, receiver_out, source_out, scalars, padded):
    kc, c, d, works_on = lay.position()
    steps, lanes = lay.steps, receiver_out.shape[-1]
    window = lay.start(kc) + lay.shift(c) - lay.pad[0]
    table = jnp.where(works_on == c, mine[...], twin[...])

    def scalar(values, row):
        return jnp.max(values[row : row + 1]).astype(jnp.int32)

    src_x, src_y = scalar(table, steps + 3), scalar(table, steps + 4) - window
    first = jnp.clip(src_y, 0, lay.span - 1) & ~(TILE - 1)
    anchors = scalar(mine[...], steps + 5), scalar(twin[...], steps + 5)
    scalars[0], scalars[1] = src_x, first
    scalars[2] = jnp.where(c == 0, anchors[0], anchors[1])
    scalars[3] = jnp.where(c == 0, anchors[1], anchors[0])

    lane = lax.broadcasted_iota(jnp.int32, (TILE, lanes), 1)
    line = lax.broadcasted_iota(jnp.int32, (TILE, lanes), 0)
    spot = (lane == SRC_Z) & (line + first == src_y)
    at_step = lax.broadcasted_iota(jnp.int32, (1, table.shape[1]), 1)
    for step in range(steps):
        amount = jnp.sum(jnp.where(at_step == step, table[steps : steps + 1], 0.0))
        source_out[step] = jnp.where(spot, amount, 0.0)

    lines = lax.broadcasted_iota(jnp.int32, (lay.span, table.shape[1]), 0) + window
    there = (lines == table[steps + 2 : steps + 3].astype(jnp.int32)).astype(jnp.float32)
    padded[...] = jnp.zeros_like(padded)

    def one_row(row, unused):
        here = table[steps + 1 : steps + 2].astype(jnp.int32) == row
        padded[:steps] = jnp.where(here, table[:steps], 0.0)
        receiver_out[row] = lax.dot_general(
            there,
            padded[...],
            (((1,), (1,)), ((), ())),
            precision=lax.Precision.HIGHEST,
            preferred_element_type=jnp.float32,
        )
        return unused

    lax.fori_loop(0, lay.width, one_row, 0)


def pulses(lay, mine, twin, z_count):
    shapes = [(lay.width, lay.span, z_count), (lay.steps, TILE, z_count)]
    held = 4 * (2 * math.prod(shapes[0]) + z_count * mine.shape[1])
    smem, vmem = (pl.BlockSpec(memory_space=space) for space in (pltpu.SMEM, pltpu.VMEM))
    return pl.pallas_call(
        functools.partial(pulse_kernel, lay),
        out_shape=[jax.ShapeDtypeStruct(shape, jnp.float32) for shape in shapes]
        + [jax.ShapeDtypeStruct((4,), jnp.int32)],
        in_specs=[vmem] * 2,
        out_specs=[vmem, vmem, smem],
        scratch_shapes=[pltpu.VMEM((z_count, mine.shape[1]), jnp.float32)],
        compiler_params=pltpu.CompilerParams(vmem_limit_bytes=held + 2**21),
    )(mine, twin)


def sin_cos(angle):
    square = angle * angle
    sine, cosine = 1.0 / 6227020800.0, -1.0 / 87178291200.0
    for n in (11, 9, 7, 5, 3, 1):
        sine = sine * square + (-1.0) ** (n // 2) / math.factorial(n)
    for n in (12, 10, 8, 6, 4, 2, 0):
        cosine = cosine * square + (-1.0) ** (n // 2) / math.factorial(n)
    return sine * angle, cosine


def medium_kernel(velocity, eps, delta, tilt, azimuth, out):
    speed = velocity[...]
    out[0] = speed
    out[1] = speed * (1.0 + 2.0 * eps[...])
    out[2] = speed * jnp.sqrt(1.0 + 2.0 * delta[...])
    sin_tilt, unused = sin_cos(tilt[...])
    sine, cosine = sin_cos(0.5 * azimuth[...])
    out[3] = sin_tilt * (1.0 - 2.0 * sine * sine)
    out[4] = sin_tilt * (2.0 * sine * cosine)


def medium(*arrays):
    vmem = pl.BlockSpec(memory_space=pltpu.VMEM)
    return pl.pallas_call(
        medium_kernel,
        out_shape=jax.ShapeDtypeStruct((len(arrays),) + arrays[0].shape, jnp.float32),
        in_specs=[vmem] * len(arrays),
        out_specs=vmem,
    )(*arrays)


def make_coefs(raw_ref, coef_ref, lay):
    lane = lax.broadcasted_iota(jnp.int32, (TILE, raw_ref.shape[-1]), 1)
    last = raw_ref.shape[-1] - 1

    def from_below(value):
        return jnp.where(lane == 0, 0.0, pltpu.roll(value, 1, 1))

    def from_above(value):
        return jnp.where(lane == last, 0.0, pltpu.roll(value, last, 1))

    def one_row(row, unused):
        for tile in range(lay.span // TILE):
            lines = slice(TILE * tile, TILE * tile + TILE)
            n_x, n_y = raw_ref[0, row, lines, :], raw_ref[1, row, lines, :]
            xx, yy = n_x * n_x, n_y * n_y
            flat = xx + yy
            zz = 1.0 - flat
            half = 0.5 * jnp.sqrt(zz)
            xz, yz = half * n_x, half * n_y
            values = (
                xx, 1.0 - xx, yy, 1.0 - yy, 0.5 * n_x * n_y,
                from_below(zz), from_below(flat), from_below(xz), from_below(yz),
                from_above(zz), from_above(flat), from_above(xz), from_above(yz),
            )
            for i, value in enumerate(values):
                coef_ref[i, row, lines, :] = value
        return unused

    lax.fori_loop(0, lay.width, one_row, 0)


def run_steps(state, coef_ref, source, inject_ref, image_ref, lay):
    z_count = state.shape[-1]
    last = z_count - 1
    lane = lax.broadcasted_iota(jnp.int32, (TILE, z_count), 1)
    chunk = next(size for size in (8, 4, 2, 1) if lay.width % size == 0)

    def row_of(now, field, row, tile):
        base = TILE + TILE * tile
        middle = state[now, field, row, base : base + TILE, :]
        low = state[now, field, row, base - 1 : base - 1 + TILE, :]
        high = state[now, field, row, base + 1 : base + 1 + TILE, :]
        return middle, high - low, high + low

    def sweep(step, now, new, first, tile, wave):
        turn = lax.rem(REC_Z - step + z_count, z_count)
        lines = slice(TILE * tile, TILE * tile + TILE)
        inner = slice(TILE + TILE * tile, 2 * TILE + TILE * tile)
        pair = (2 * wave, 2 * wave + 1)
        before = [row_of(now, field, first, tile) for field in pair]
        here = [row_of(now, field, first + 1, tile) for field in pair]
        for i in range(chunk):
            row = first + i
            beyond = [row_of(now, field, row + 2, tile) for field in pair]
            coef = [coef_ref[n, row, lines, :] for n in range(COEFS)]
            xx, xx0, yy, yy0, xy = coef[:5]
            zz_b, zz0_b, xz_b, yz_b, zz_a, zz0_a, xz_a, yz_a = coef[5:13]
            velocity, axial_gain, cross_gain = coef[13:]

            def terms(field):
                f, diff_y, sum_y = here[field]
                sum_x = beyond[field][0] + before[field][0]
                diff_x = beyond[field][0] - before[field][0]
                mixed = beyond[field][1] - before[field][1]
                below = xz_b * diff_x + yz_b * diff_y
                above = xz_a * diff_x + yz_a * diff_y
                return f, sum_x, sum_y, xy * mixed, below, above

            p, sum_x, sum_y, mixed, below, above = terms(0)
            across = xx0 * sum_x + yy0 * sum_y - mixed
            across += pltpu.roll(zz0_b * p - below, last, 1) + pltpu.roll(zz0_a * p + above, 1, 1)
            twice_p = p + p
            across -= twice_p + twice_p
            q, sum_x, sum_y, mixed, below, above = terms(1)
            axial = xx * sum_x + yy * sum_y + mixed
            axial += pltpu.roll(zz_b * q + below, last, 1) + pltpu.roll(zz_a * q - above, 1, 1)
            twice_q = q + q
            axial -= twice_q
            old_p = state[new, pair[0], row + 1, inner, :]
            old_q = state[new, pair[1], row + 1, inner, :]
            new_p = (twice_p - old_p) + (axial_gain * across + cross_gain * axial)
            new_q = (twice_q - old_q) + (cross_gain * across + velocity * axial)
            if wave == 1:
                pulse = pltpu.roll(inject_ref[row, lines, :], turn, 1)
                pulse = velocity * jnp.where(lane == REC_Z, pulse, 0.0)
                new_p, new_q = new_p + pulse, new_q + pulse
            state[new, pair[0], row + 1, inner, :] = new_p
            state[new, pair[1], row + 1, inner, :] = new_q
            if wave == 1:
                image_ref[row, lines, :] += state[new, 0, row + 1, inner, :] * new_p
            before, here = here, beyond

    def one_step(step, now):
        def sweeps(wave):
            def one_chunk(first):
                for tile in range(lay.span // TILE):
                    sweep(step, now, 1 - now, first, tile, wave)

            if chunk == lay.width:
                one_chunk(0)
            else:
                lax.fori_loop(0, lay.width // chunk, lambda n, u: (one_chunk(n * chunk), u)[1], 0)

        sweeps(0)
        source_x, first, source_ref = source
        first = pl.multiple_of(first, TILE)
        pulse = coef_ref[COEFS - 3, source_x, pl.ds(first, TILE), :] * source_ref[step]
        for field in (0, 1):
            state[1 - now, field, source_x + 1, pl.ds(TILE + first, TILE), :] += pulse
        sweeps(1)

    def two_steps(i, unused):
        one_step(2 * i, 0)
        one_step(2 * i + 1, 1)
        return unused

    lax.fori_loop(0, lay.steps // 2, two_steps, 0)
    if lay.steps % 2:
        one_step(lay.steps - 1, 0)


def clear_edges(state, lay):
    rows, lines = state.shape[2], state.shape[3]
    edge = jnp.zeros((lines,) + state.shape[4:], jnp.float32)
    strip = jnp.zeros((rows, TILE) + state.shape[4:], jnp.float32)
    for time in range(state.shape[0]):
        for field in range(state.shape[1]):
            state[time, field, 0] = edge
            state[time, field, rows - 1] = edge
            state[time, field, :, :TILE] = strip
            state[time, field, :, lines - TILE :] = strip


def wave_kernel(lay, scalars, source_ref, receiver_ref, *refs):
    waves_own, waves_other, model_own, model_other, pieces = (
        refs[i * lay.domain : (i + 1) * lay.domain] for i in range(5)
    )
    raw, coef_ref, image_ref, state = refs[5 * lay.domain :]
    clear_edges(state, lay)

    def store_wave(row, ref):
        for i in range(8):
            time, field = (i >> 1) & 1, 2 * (i >> 2) + (i & 1)
            state[time, field, row + 1, TILE : TILE + lay.span, :] = ref[i]

    def store_model(row, ref):
        for i in range(5):
            target = coef_ref.at[COEFS - 3 + i, row] if i < 3 else raw.at[i - 3, row]
            target[...] = ref[i]

    gather_rows(lay, waves_own, waves_other, store_wave)
    gather_rows(lay, model_own, model_other, store_model)
    make_coefs(raw, coef_ref, lay)
    image_ref[...] = jnp.zeros_like(image_ref)
    run_steps(state, coef_ref, (scalars[0], scalars[1], source_ref), receiver_ref, image_ref, lay)
    kc, c, d, unused = lay.position()
    skip = (2 * kc + c) * lay.own - (lay.start(kc) + lay.shift(c) - lay.pad[0])
    if lay.own % TILE == 0:
        skip = pl.multiple_of(skip, TILE)
    for r, piece in enumerate(pieces):
        first = lax.rem(d + r, lay.domain) * lay.rows
        for row in range(lay.rows):
            if lay.own % TILE == 0:
                piece[row] = image_ref[first + row, pl.ds(skip, lay.own), :]
            else:
                piece[row] = pltpu.roll(image_ref[first + row], lay.span - skip, 0)[: lay.own]


def frame_kernel(lay, scalars, owners, *refs, slab):
    pieces, outs, frame = refs[: lay.domain], refs[lay.domain : -1], refs[-1]
    unused, c, d, unused = lay.position()
    frame[...] = jnp.zeros_like(frame)
    room = -(-lay.own // TILE) * TILE + TILE
    filler = jnp.zeros((room - lay.own, frame.shape[-1]), jnp.float32)
    for r, piece in enumerate(pieces):
        source = lax.rem(d - r + lay.domain, lay.domain)
        place = scalars[2 + source // lay.half] + (2 * lax.rem(source, lay.half) + c) * lay.own
        first = pl.multiple_of(place & ~(TILE - 1), TILE)
        for row in range(lay.rows):
            moved = pltpu.roll(jnp.concatenate([piece[row], filler]), place & (TILE - 1), 0)
            frame[row, pl.ds(first, room), :] += moved
    for r, out in enumerate(outs):
        first = pl.multiple_of(owners[lax.axis_index("shot") ^ r] * slab, TILE)
        for row in range(lay.rows):
            out[row] = frame[row, pl.ds(first, slab), :]


def call(kernel, cost, lay, outs, scratch, scalars, *operands):
    smem = pl.BlockSpec(memory_space=pltpu.SMEM)
    vmem = pl.BlockSpec(memory_space=pltpu.VMEM)
    held = sum(4 * math.prod(array.shape) for array in [*operands, *outs, *scratch])
    return pl.pallas_call(
        functools.partial(kernel, lay),
        out_shape=outs,
        in_specs=[smem] * len(scalars) + [vmem] * len(operands),
        out_specs=[vmem] * len(outs),
        scratch_shapes=scratch,
        compiler_params=pltpu.CompilerParams(vmem_limit_bytes=held + held // 8 + 2**21),
        cost_estimate=pl.CostEstimate(flops=0, bytes_accessed=cost, transcendentals=0),
    )(*scalars, *operands)


def per_device(
    velocity,
    thomsen_eps,
    thomsen_delta,
    tilt_angle,
    azimuth,
    shot_anchor,
    source_x,
    source_y,
    wavelet,
    receiver_x,
    receiver_y,
    traces,
    source_now,
    source_before,
    receiver_now,
    receiver_before,
    slab_owner,
):
    rows, lines, z_count = source_now.shape[2:]
    steps = wavelet.shape[1]
    domain, shots = lax.axis_size("domain"), lax.axis_size("shot")
    lay = Layout(domain, shots, rows, lines, steps)
    d, s = lax.axis_index("domain"), lax.axis_index("shot")
    zero = jnp.int32(0)

    tight = lay.pad == (0, 0)

    def wave_messages(fields):
        fields = [jnp.pad(field[0], ((0, 0), (0, 0), lay.pad, (0, 0))) for field in fields]
        messages = []
        for r in range(domain):
            k = lax.rem(d + r, domain)
            spot = (zero, (k & 1) * lay.part, lay.start(k >> 1), zero)
            size = (2, lay.part, lay.chip, z_count)
            messages.append(jnp.concatenate([lax.dynamic_slice(field, spot, size) for field in fields]))
        return messages

    def send(messages):
        return [lax.ppermute(messages[r], ("domain", "shot"), pairs) for r, pairs in lay.rounds()]

    def other_core(messages):
        return [swapped(message, "shot", 1) for message in messages]

    messages = wave_messages((source_now, source_before, receiver_now, receiver_before))
    velocity, messages[0] = lax.optimization_barrier((velocity, messages[0]))
    waves = send(messages)
    model = medium(velocity, thomsen_eps, thomsen_delta, tilt_angle, azimuth)
    slab = model.shape[2]
    whole = jnp.zeros(model.shape[:2] + (shots * slab, z_count), jnp.float32)
    for r in range(shots):
        block = swapped(model, "shot", r) if r else model
        whole = lax.dynamic_update_slice(whole, block, (zero, zero, (s ^ r) * slab, zero))
    model = whole
    anchor = shot_anchor[0]
    if tight:
        first_line = anchor
    else:
        model = lax.dynamic_slice_in_dim(model, anchor, lines, 2)
        model = jnp.pad(model, ((0, 0), (0, 0), lay.pad, (0, 0)))
        first_line = zero
    messages = []
    for r in range(domain):
        k = lax.rem(d + r, domain)
        spot = (zero, (k & 1) * lay.part, first_line + lay.start(k >> 1), zero)
        messages.append(lax.dynamic_slice(model, spot, (5, lay.part, lay.chip, z_count)))
    *messages, waves[-1] = lax.optimization_barrier((*messages, waves[-1]))
    models = send(messages)
    *waves, models[0] = lax.optimization_barrier((*waves, models[0]))
    waves_other, models_other = other_core(waves), other_core(models)

    traces, waves[0] = lax.optimization_barrier((traces, waves[0]))
    table = table_of(traces, wavelet, receiver_x, receiver_y, source_x, source_y, shot_anchor)
    receiver_pulse, source_pulse, scalars = pulses(lay, table, swapped(table, "shot", 1), z_count)
    block = (lay.width, lay.span, z_count)
    pieces = call(
        wave_kernel,
        60_000_000,
        lay,
        [jax.ShapeDtypeStruct((rows, lay.own, z_count), jnp.float32)] * domain,
        [
            pltpu.VMEM((2,) + block, jnp.float32),
            pltpu.VMEM((COEFS,) + block, jnp.float32),
            pltpu.VMEM(block, jnp.float32),
            pltpu.VMEM((2, 4, lay.width + 2, lay.span + 2 * TILE, z_count), jnp.float32),
        ],
        (scalars,),
        source_pulse,
        receiver_pulse,
        *waves,
        *waves_other,
        *models,
        *models_other,
    )

    pieces = [
        swapped_round(piece, "domain", r) if r else piece for r, piece in enumerate(pieces)
    ]
    room = -(-lay.own // TILE) * TILE + TILE
    parts = call(
        functools.partial(frame_kernel, slab=slab),
        2_000_000,
        lay,
        [jax.ShapeDtypeStruct((rows, slab, z_count), jnp.float32)] * shots,
        [pltpu.VMEM((rows, shots * slab + room, z_count), jnp.float32)],
        (scalars, slab_owner),
        *pieces,
    )
    total = parts[0]
    for r in range(1, shots):
        total = total + swapped(parts[r], "shot", r)
    return total / steps


def solution(mesh):
    in_specs = (
        P(("groups", "domain"), "shot", None),
        P(("groups", "domain"), "shot", None),
        P(("groups", "domain"), "shot", None),
        P(("groups", "domain"), "shot", None),
        P(("groups", "domain"), "shot", None),
        P(("groups", "shot")),
        P(("groups", "shot")),
        P(("groups", "shot")),
        P(("groups", "shot"), None),
        P(("groups", "shot"), None),
        P(("groups", "shot"), None),
        P(("groups", "shot"), None, None),
        P(("groups", "shot"), None, "domain", None, None),
        P(("groups", "shot"), None, "domain", None, None),
        P(("groups", "shot"), None, "domain", None, None),
        P(("groups", "shot"), None, "domain", None, None),
        P("groups"),
    )
    out_specs = P(("groups", "domain"), "shot", None)
    return jax.shard_map(
        per_device, mesh=mesh, in_specs=in_specs, out_specs=out_specs, check_vma=False
    )
```

time: 113 us -> 106 us (0.938)
  waiting for transfers between devices: 21.5 us -> 34 us
  starting transfers between devices: 54.5 us -> 45.2 us
  local copies, waits for them, and re-layouts: 7.52 us -> 3.31 us
  Pallas kernels: 20 us -> 16.9 us
  between operations: 4.18 us -> 2.35 us
    ppermute x8, waiting for transfers between devices: 6.84 us -> 17.9 us  [send(): lax.ppermute(messages[r], ('domain', 'shot'), pairs)]
    ppermute x15, starting transfers between devices: 14.5 us -> 7.43 us  [swapped(): return lax.ppermute(value, axis, [(i, i ^ bit) for i in range(count)])]
    pallas_call x2, Pallas kernels: 18.1 us -> 12.2 us  [call(): pl.pallas_call(functools.partial(kernel, lay), out_shape=outs, in_specs=[...]
    pallas_call x1 -> x3, Pallas kernels: 1.96 us -> 4.71 us  [the longest x1 2.62 us: pulses(): pl.pallas_call(functools.partial(pulse_kernel, lay), out_shape=[jax.Shape...]
    unnamed x25 -> x16, local copies, waits for them, and re-layouts: 2.67 us -> 0.04 us
    ppermute x8, starting transfers between devices: 35.3 us -> 33.5 us  [send(): lax.ppermute(messages[r], ('domain', 'shot'), pairs)]
    dynamic_slice x2, local copies, waits for them, and re-layouts: 1.37 us -> 2.86 us  [wave_messages(): lax.dynamic_slice(field, spot, size)]
    slice x4 -> x0, local copies, waits for them, and re-layouts: 1.18 us -> none  [the longest x1 0.59 us: per_device(): table[at].astype(jnp.int32)]
  transfers between devices with their start and end apart: 26 -> 26, of which waited for: 9 -> 9; matrix products, arithmetic and copies ran while one was open for 8% -> 3% of each run, Pallas kernels for 0% -> 2%
where the time goes in v4:
time: 106 us; the launch traced here: 105 us
  starting transfers between devices  45.2 us (43%)
  waiting for transfers between devices  34 us (32%)
  Pallas kernels  16.9 us (16%)
  other arithmetic  3.56 us (3%)
  local copies, waits for them, and re-layouts  3.31 us (3%)
  between operations  2.35 us (2%)
    ppermute x8, starting transfers between devices, send(): lax.ppermute(messages[r], ('domain', 'shot'), pairs)  33.5 us
    ppermute x8, waiting for transfers between devices, send(): lax.ppermute(messages[r], ('domain', 'shot'), pairs)  17.9 us
    ppermute x15, waiting for transfers between devices, swapped(): return lax.ppermute(value, axis, [(i, i ^ bit) for i in range(count)])  12.9 us
    pallas_call x2, Pallas kernels, call(): pl.pallas_call(functools.partial(kernel, lay), out_shape=outs, in_specs=[...  12.2 us
    ppermute x15, starting transfers between devices, swapped(): return lax.ppermute(value, axis, [(i, i ^ bit) for i in range(count)])  7.43 us
    ppermute x3, starting transfers between devices, swapped_round(): lax.ppermute(value, axis, [(i, (i + r) % count) for i in range(count)])  4.27 us
    ppermute x3, waiting for transfers between devices, swapped_round(): lax.ppermute(value, axis, [(i, (i + r) % count) for i in range(count)])  3.12 us
    concatenate x4, other arithmetic, wave_messages(): jnp.concatenate([lax.dynamic_slice(field, spot, size) for field in fields])  2.9 us
  transfers between devices with their start and end apart: 26, of which 9 were waited for; matrix products, arithmetic and copies ran while one was open for 3% of the time, Pallas kernels for 2%

profile of v4, /device:TPU:0, one launch (start us, length us, event | category | flops | bytes accessed | tf_op | source)
XLA Modules:
  0.0 105.2 jit_solution(1715057316707044416)
XLA Ops:
  0.0 2.0 %dynamic-slice_bitcast_fusion = (f32[2,1,104,128]{3,2,1,0:T(8,128)S(1)}, f32[2,1,104,128]{3,2,1,0:T(8,128)S(1)}, f32[2,1,104,128]{3,2,1,0:T(8,128)S(1)}, f32[2,1...) fusion(f32[1,2,2,192,128]{4,3,2,1,0:T(8,128)} %param.32, ...), kind=kLoop, calls=%fused_computation.4 | loop fusion | bytes 1703968 | tf_op jit(solution)/shard_map/dynamic_slice | solution.py:435
  2.0 0.8 dynamic-slice_bitcast_fusion.2
  2.9 2.1 %shard_map.163 = f32[5,2,96,128]{3,2,1,0:T(8,128)} custom-call(f32[2,96,128]{2,1,0:T(8,128)} %velocity, f32[2,96,128]{2,1,0:T(8,128)} %eps.1, f32[2,96,128]{2,1,0:T(8,128)} %delta.1, f32[2,96,128]{2,1,0:T(8,128)} %tilt.1, f32[2,96,128]{2,1,0:T(8,128)} %azimuth.1), custom_call_target="tpu_custom_call" | custom-call | tf_op jit(solution)/shard_map/pallas_call | solution.py:190
  5.4 2.5 %collective-permute-start.4 = (f32[5,2,96,128]{3,2,1,0:T(8,128)}, f32[5,2,96,128]{3,2,1,0:T(8,128)S(1)}, u32[]{:S(2)}, u32[]{:S(2)}) collective-permute-start(f32[5,2,96,128]{3,2,1,0:T(8,128)} %shard_map.163), channel_id=1, source_target_pairs={{0,2},{1,3},{2,0},{3,1},{4,6},{5,7},{6,4},{7,5},{8,10},{9,11},{10,... | collective-permute-start | bytes 1474568 | tf_op jit(solution)/shard_map/ppermute | solution.py:62
  8.1 0.7 collective-permute-start
  8.8 0.8 pad_maximum_fusion.1
  9.6 6.2 %collective-permute-start.1 = (f32[8,1,104,128]{3,2,1,0:T(8,128)}, f32[8,1,104,128]{3,2,1,0:T(8,128)S(1)}, u32[]{:S(2)}, u32[]{:S(2)}) collective-permute-start(f32[8,1,104,128]{3,2,1,0:T(8,128)} %pad_maximum_fusion.1), channel_id=1, source_target_pairs={{0,1},{1,9},{2,3},{3,11},{4,4},{5,12},{6,6},{7,14},{8,5},{9,13},{1... | collective-permute-start | bytes 1277960 | tf_op jit(solution)/shard_map/ppermute | solution.py:439
  16.5 1.1 %pad_maximum_fusion.2 = f32[8,1,104,128]{3,2,1,0:T(8,128)S(1)} fusion(f32[2,1,104,128]{3,2,1,0:T(8,128)} %get-tuple-element.74, f32[2,1,104,128]{3,2,1,0:T(8,128)} %get-tuple-element.75, f32[2,1,104,128]{3,2,1,0:T(8,128)} %get-tuple-element.66, f32[2,1,104,128]{3,2,1,0:T(8,128)} %get-tuple-element.79), kind=kLoop, calls=%fused_computation.2 | loop fusion | flops 319488 | bytes 851968 | tf_op jit(solution)/shard_map/concatenate | solution.py:435
  17.5 1.0 pad_maximum_fusion.3
  18.8 3.3 %collective-permute-start.6 = (f32[8,1,104,128]{3,2,1,0:T(8,128)S(1)}, f32[8,1,104,128]{3,2,1,0:T(8,128)S(1)}, u32[]{:S(2)}, u32[]{:S(2)}) collective-permute-start(f32[8,1,104,128]{3,2,1,0:T(8,128)S(1)} %pad_maximum_fusion.3), channel_id=1, source_target_pairs={{0,5},{1,13},{2,7},{3,15},{4,0},{5,8},{6,2},{7,10},{8,1},{9,9},{10... | collective-permute-start | bytes 1277960 | tf_op jit(solution)/shard_map/ppermute | solution.py:439
  22.2 0.7 collective-permute-start.2
  22.9 7.5 %collective-permute-done.5 = f32[5,2,96,128]{3,2,1,0:T(8,128)S(1)} collective-permute-done((f32[5,2,96,128]{3,2,1,0:T(8,128)}, f32[5,2,96,128]{3,2,1,0:T(8,128)S(1)}, u32[]{:S(2)}, u32[]{:S(2)}) %collective-permute-start.5) | collective-permute-done | bytes 491552 | tf_op jit(solution)/shard_map/ppermute | solution.py:62
  30.5 1.6 %collective-permute-done.6.refs_3_ = f32[8,1,104,128]{3,2,1,0:T(8,128)S(1)} collective-permute-done((f32[8,1,104,128]{3,2,1,0:T(8,128)S(1)}, f32[8,1,104,128]{3,2,1,0:T(8,128)S(1)}, u32[]{:S(2)}, u32[]{:S(2)}) %collective-permute-start.6) | collective-permute-done | bytes 426016 | tf_op jit(solution)/shard_map/ppermute | solution.py:439
  32.2 0.7 collective-permute-start.7
  32.9 18.7 %collective-permute-start.13 = (f32[5,1,104,128]{3,2,1,0:T(8,128)S(1)}, f32[5,1,104,128]{3,2,1,0:T(8,128)S(1)}, u32[]{:S(2)}, u32[]{:S(2)}) collective-permute-start(f32[5,1,104,128]{3,2,1,0:T(8,128)S(1)} %get-tuple-element.44), channel_id=1, source_target_pairs={{0,1},{1,9},{2,3},{3,11},{4,4},{5,12},{6,6},{7,14},{8,5},{9,13},{1... | collective-permute-start | bytes 798728 | tf_op jit(solution)/shard_map/ppermute | solution.py:439
  51.6 3.2 %collective-permute-start.15 = (f32[5,1,104,128]{3,2,1,0:T(8,128)S(1)}, f32[5,1,104,128]{3,2,1,0:T(8,128)S(1)}, u32[]{:S(2)}, u32[]{:S(2)}) collective-permute-start(f32[5,1,104,128]{3,2,1,0:T(8,128)S(1)} %get-tuple-element.46), channel_id=1, source_target_pairs={{0,5},{1,13},{2,7},{3,15},{4,0},{5,8},{6,2},{7,10},{8,1},{9,9},{10... | collective-permute-start | bytes 798728 | tf_op jit(solution)/shard_map/ppermute | solution.py:439
  55.0 5.0 %collective-permute-done.13.refs_9_ = f32[5,1,104,128]{3,2,1,0:T(8,128)S(1)} collective-permute-done((f32[5,1,104,128]{3,2,1,0:T(8,128)S(1)}, f32[5,1,104,128]{3,2,1,0:T(8,128)S(1)}, u32[]{:S(2)}, u32[]{:S(2)}) %collective-permute-start.13) | collective-permute-done | bytes 266272 | tf_op jit(solution)/shard_map/ppermute | solution.py:439
  60.0 11.3 %collective-permute-done.14.refs_10_ = f32[5,1,104,128]{3,2,1,0:T(8,128)S(1)} collective-permute-done((f32[5,1,104,128]{3,2,1,0:T(8,128)S(1)}, f32[5,1,104,128]{3,2,1,0:T(8,128)S(1)}, u32[]{:S(2)}, u32[]{:S(2)}) %collective-permute-start.14) | collective-permute-done | bytes 266272 | tf_op jit(solution)/shard_map/ppermute | solution.py:439
  72.6 0.6 collective-permute-start.8
  73.2 0.7 collective-permute-start.9
  75.0 2.6 %shard_map.165 = (f32[8,64,128]{2,1,0:T(8,128)S(1)}, f32[8,8,128]{2,1,0:T(8,128)S(1)}, s32[4]{0:T(128)S(1)}) custom-call(f32[16,256]{1,0:T(8,128)S(1)} %shard_map.164.mine, f32[16,256]{1,0:T(8,128)S(1)} %collective-permute-done.8.twin), custom_call_target="tpu_custom_call" | custom-call | tf_op jit(solution)/shard_map/pallas_call | solution.py:156
  77.7 11.5 %shard_map.166 = (f32[2,48,128]{2,1,0:T(8,128)S(1)}, f32[2,48,128]{2,1,0:T(8,128)S(1)}, f32[2,48,128]{2,1,0:T(8,128)S(1)}, f32[2,48,128]{2,1,0:T(8,128)S(1)}) custom-call(s32[4]{0:T(128)S(1)} %get-tuple-element.36.scalars, f32[8,8,128]{2,1,0:T(8,128)S(1)} %get-tuple-element.37.source_ref, f32[8,64,128]{2,1,0:T(8,128)S(1)} %get-tuple-element.38.receiver_ref, ...), custom_call_target="tpu_custom_call" | custom-call | bytes 60000000 | tf_op jit(solution)/shard_map/pallas_call | solution.py:389
  89.3 2.0 %collective-permute-start.21 = (f32[2,48,128]{2,1,0:T(8,128)S(1)}, f32[2,48,128]{2,1,0:T(8,128)S(1)}, u32[]{:S(2)}, u32[]{:S(2)}) collective-permute-start(f32[2,48,128]{2,1,0:T(8,128)S(1)} %get-tuple-element.49), channel_id=1, source_target_pairs={{0,8},{4,12},{8,0},{12,4},{1,9},{5,13},{9,1},{13,5},{2,10},{6,14},... | collective-permute-start | bytes 147464 | tf_op jit(solution)/shard_map/ppermute | solution.py:71
  91.3 2.2 %collective-permute-start.22 = (f32[2,48,128]{2,1,0:T(8,128)S(1)}, f32[2,48,128]{2,1,0:T(8,128)S(1)}, u32[]{:S(2)}, u32[]{:S(2)}) collective-permute-start(f32[2,48,128]{2,1,0:T(8,128)S(1)} %get-tuple-element.50), channel_id=1, source_target_pairs={{0,12},{4,0},{8,4},{12,8},{1,13},{5,1},{9,5},{13,9},{2,14},{6,2},{... | collective-permute-start | bytes 147464 | tf_op jit(solution)/shard_map/ppermute | solution.py:71
  93.5 2.2 %collective-permute-done.20.refs_1_ = f32[2,48,128]{2,1,0:T(8,128)S(1)} collective-permute-done((f32[2,48,128]{2,1,0:T(8,128)S(1)}, f32[2,48,128]{2,1,0:T(8,128)S(1)}, u32[]{:S(2)}, u32[]{:S(2)}) %collective-permute-start.20) | collective-permute-done | bytes 49184 | tf_op jit(solution)/shard_map/ppermute | solution.py:71
  95.7 0.9 collective-permute-done.21.refs_2_
  96.6 0.7 shard_map.167
  97.3 0.6 collective-permute-start.25
  97.9 1.1 %collective-permute-start.24 = (f32[2,96,128]{2,1,0:T(8,128)S(1)}, f32[2,96,128]{2,1,0:T(8,128)S(1)}, u32[]{:S(2)}, u32[]{:S(2)}) collective-permute-start(f32[2,96,128]{2,1,0:T(8,128)S(1)} %get-tuple-element.53), channel_id=1, source_target_pairs={{0,2},{1,3},{2,0},{3,1},{4,6},{5,7},{6,4},{7,5},{8,10},{9,11},{10,... | collective-permute-start | bytes 294920 | tf_op jit(solution)/shard_map/ppermute | solution.py:62
  99.2 3.1 %collective-permute-done.25 = f32[2,96,128]{2,1,0:T(8,128)S(1)} collective-permute-done((f32[2,96,128]{2,1,0:T(8,128)S(1)}, f32[2,96,128]{2,1,0:T(8,128)S(1)}, u32[]{:S(2)}, u32[]{:S(2)}) %collective-permute-start.25) | collective-permute-done | bytes 98336 | tf_op jit(solution)/shard_map/ppermute | solution.py:62
  102.3 2.3 %collective-permute-done.24 = f32[2,96,128]{2,1,0:T(8,128)S(1)} collective-permute-done((f32[2,96,128]{2,1,0:T(8,128)S(1)}, f32[2,96,128]{2,1,0:T(8,128)S(1)}, u32[]{:S(2)}, u32[]{:S(2)}) %collective-permute-start.24) | collective-permute-done | bytes 98336 | tf_op jit(solution)/shard_map/ppermute | solution.py:62
  104.6 0.7 add_multiply_fusion
  (54 shorter events, 2.6 us)
Async XLA Ops:
  5.0 13.8 %collective-permute-start.3 = (f32[5,2,96,128]{3,2,1,0:T(8,128)}, f32[5,2,96,128]{3,2,1,0:T(8,128)S(1)}, u32[]{:S(2)}, u32[]{:S(2)}) collective-permute-start(f32[5,2,96,128]{3,2,1,0:T(8,128)} %shard_map.163), channel_id=1, source_target_pairs={{0,1},{1,0},{2,3},{3,2},{4,5},{5,4},{6,7},{7,6},{8,9},{9,8},{10,11... | collective-permute-start | bytes 1474568 | tf_op jit(solution)/shard_map/ppermute | solution.py:62
  5.4 16.7 %collective-permute-start.4 = (f32[5,2,96,128]{3,2,1,0:T(8,128)}, f32[5,2,96,128]{3,2,1,0:T(8,128)S(1)}, u32[]{:S(2)}, u32[]{:S(2)}) collective-permute-start(f32[5,2,96,128]{3,2,1,0:T(8,128)} %shard_map.163), channel_id=1, source_target_pairs={{0,2},{1,3},{2,0},{3,1},{4,6},{5,7},{6,4},{7,5},{8,10},{9,11},{10,... | collective-permute-start | bytes 1474568 | tf_op jit(solution)/shard_map/ppermute | solution.py:62
  7.9 22.4 %collective-permute-start.5 = (f32[5,2,96,128]{3,2,1,0:T(8,128)}, f32[5,2,96,128]{3,2,1,0:T(8,128)S(1)}, u32[]{:S(2)}, u32[]{:S(2)}) collective-permute-start(f32[5,2,96,128]{3,2,1,0:T(8,128)} %shard_map.163), channel_id=1, source_target_pairs={{0,3},{1,2},{2,1},{3,0},{4,7},{5,6},{6,5},{7,4},{8,11},{9,10},{10,... | collective-permute-start | bytes 1474568 | tf_op jit(solution)/shard_map/ppermute | solution.py:62
  8.1 43.5 %collective-permute-start = (f32[8,1,104,128]{3,2,1,0:T(8,128)S(1)}, f32[8,1,104,128]{3,2,1,0:T(8,128)S(1)}, u32[]{:S(2)}, u32[]{:S(2)}) collective-permute-start(f32[8,1,104,128]{3,2,1,0:T(8,128)S(1)} %pad_maximum_fusion), channel_id=1, source_target_pairs={{0,0},{1,8},{2,2},{3,10},{4,1},{5,9},{6,3},{7,11},{8,4},{9,12},{10... | collective-permute-start | bytes 1277960 | tf_op jit(solution)/shard_map/ppermute | solution.py:439
  9.6 9.1 %copy-start.5 = (f32[5,2,96,128]{3,2,1,0:T(8,128)S(1)}, f32[5,2,96,128]{3,2,1,0:T(8,128)}, u32[]{:S(2)}) copy-start(f32[5,2,96,128]{3,2,1,0:T(8,128)} %shard_map.163) | copy-start | bytes 1474564
  9.6 42.0 %collective-permute-start.1 = (f32[8,1,104,128]{3,2,1,0:T(8,128)}, f32[8,1,104,128]{3,2,1,0:T(8,128)S(1)}, u32[]{:S(2)}, u32[]{:S(2)}) collective-permute-start(f32[8,1,104,128]{3,2,1,0:T(8,128)} %pad_maximum_fusion.1), channel_id=1, source_target_pairs={{0,1},{1,9},{2,3},{3,11},{4,4},{5,12},{6,6},{7,14},{8,5},{9,13},{1... | collective-permute-start | bytes 1277960 | tf_op jit(solution)/shard_map/ppermute | solution.py:439
  18.8 13.4 %collective-permute-start.6 = (f32[8,1,104,128]{3,2,1,0:T(8,128)S(1)}, f32[8,1,104,128]{3,2,1,0:T(8,128)S(1)}, u32[]{:S(2)}, u32[]{:S(2)}) collective-permute-start(f32[8,1,104,128]{3,2,1,0:T(8,128)S(1)} %pad_maximum_fusion.3), channel_id=1, source_target_pairs={{0,5},{1,13},{2,7},{3,15},{4,0},{5,8},{6,2},{7,10},{8,1},{9,9},{10... | collective-permute-start | bytes 1277960 | tf_op jit(solution)/shard_map/ppermute | solution.py:439
  22.1 50.4 %copy-start = (f32[1,8,256]{2,1,0:T(8,128)S(1)}, f32[1,8,256]{2,1,0:T(8,128)}, u32[]{:S(2)}) copy-start(f32[1,8,256]{2,1,0:T(8,128)} %traces) | copy-start | bytes 24580
  22.1 50.4 %copy-start.1 = (s32[1,256]{1,0:T(1,128)S(1)}, s32[1,256]{1,0:T(1,128)}, u32[]{:S(2)}) copy-start(s32[1,256]{1,0:T(1,128)} %rec_x.1) | copy-start | bytes 3076
  22.2 50.4 %copy-start.2 = (s32[1,256]{1,0:T(1,128)S(1)}, s32[1,256]{1,0:T(1,128)}, u32[]{:S(2)}) copy-start(s32[1,256]{1,0:T(1,128)} %rec_y.1) | copy-start | bytes 3076
  22.2 50.4 %copy-start.3 = (f32[1,8]{1,0:T(1,128)S(1)}, f32[1,8]{1,0:T(1,128)}, u32[]{:S(2)}) copy-start(f32[1,8]{1,0:T(1,128)} %wavelet.1) | copy-start | bytes 100
  22.2 32.7 %collective-permute-start.2 = (f32[8,1,104,128]{3,2,1,0:T(8,128)S(1)}, f32[8,1,104,128]{3,2,1,0:T(8,128)S(1)}, u32[]{:S(2)}, u32[]{:S(2)}) collective-permute-start(f32[8,1,104,128]{3,2,1,0:T(8,128)S(1)} %pad_maximum_fusion.2), channel_id=1, source_target_pairs={{0,4},{1,12},{2,6},{3,14},{4,5},{5,13},{6,7},{7,15},{8,0},{9,8},{1... | collective-permute-start | bytes 1277960 | tf_op jit(solution)/shard_map/ppermute | solution.py:439
  32.2 22.7 %collective-permute-start.7 = (f32[5,1,104,128]{3,2,1,0:T(8,128)S(1)}, f32[5,1,104,128]{3,2,1,0:T(8,128)S(1)}, u32[]{:S(2)}, u32[]{:S(2)}) collective-permute-start(f32[5,1,104,128]{3,2,1,0:T(8,128)S(1)} %get-tuple-element.33), channel_id=1, source_target_pairs={{0,0},{1,8},{2,2},{3,10},{4,1},{5,9},{6,3},{7,11},{8,4},{9,12},{10... | collective-permute-start | bytes 798728 | tf_op jit(solution)/shard_map/ppermute | solution.py:439
  32.9 27.1 %collective-permute-start.13 = (f32[5,1,104,128]{3,2,1,0:T(8,128)S(1)}, f32[5,1,104,128]{3,2,1,0:T(8,128)S(1)}, u32[]{:S(2)}, u32[]{:S(2)}) collective-permute-start(f32[5,1,104,128]{3,2,1,0:T(8,128)S(1)} %get-tuple-element.44), channel_id=1, source_target_pairs={{0,1},{1,9},{2,3},{3,11},{4,4},{5,12},{6,6},{7,14},{8,5},{9,13},{1... | collective-permute-start | bytes 798728 | tf_op jit(solution)/shard_map/ppermute | solution.py:439
  51.5 19.7 %collective-permute-start.14 = (f32[5,1,104,128]{3,2,1,0:T(8,128)S(1)}, f32[5,1,104,128]{3,2,1,0:T(8,128)S(1)}, u32[]{:S(2)}, u32[]{:S(2)}) collective-permute-start(f32[5,1,104,128]{3,2,1,0:T(8,128)S(1)} %get-tuple-element.45), channel_id=1, source_target_pairs={{0,4},{1,12},{2,6},{3,14},{4,5},{5,13},{6,7},{7,15},{8,0},{9,8},{1... | collective-permute-start | bytes 798728 | tf_op jit(solution)/shard_map/ppermute | solution.py:439
  51.6 21.6 %collective-permute-start.15 = (f32[5,1,104,128]{3,2,1,0:T(8,128)S(1)}, f32[5,1,104,128]{3,2,1,0:T(8,128)S(1)}, u32[]{:S(2)}, u32[]{:S(2)}) collective-permute-start(f32[5,1,104,128]{3,2,1,0:T(8,128)S(1)} %get-tuple-element.46), channel_id=1, source_target_pairs={{0,5},{1,13},{2,7},{3,15},{4,0},{5,8},{6,2},{7,10},{8,1},{9,9},{10... | collective-permute-start | bytes 798728 | tf_op jit(solution)/shard_map/ppermute | solution.py:439
  54.9 19.5 %collective-permute-start.16 = (f32[5,1,104,128]{3,2,1,0:T(8,128)S(1)}, f32[5,1,104,128]{3,2,1,0:T(8,128)S(1)}, u32[]{:S(2)}, u32[]{:S(2)}) collective-permute-start(f32[5,1,104,128]{3,2,1,0:T(8,128)S(1)} %collective-permute-done.7.refs_8_), channel_id=1, source_target_pairs={{0,1},{1,0},{2,3},{3,2},{4,5},{5,4},{6,7},{7,6},{8,9},{9,8},{10,11... | collective-permute-start | bytes 798728 | tf_op jit(solution)/shard_map/ppermute | solution.py:62
  60.0 14.6 %collective-permute-start.17 = (f32[5,1,104,128]{3,2,1,0:T(8,128)S(1)}, f32[5,1,104,128]{3,2,1,0:T(8,128)S(1)}, u32[]{:S(2)}, u32[]{:S(2)}) collective-permute-start(f32[5,1,104,128]{3,2,1,0:T(8,128)S(1)} %collective-permute-done.13.refs_9_), channel_id=1, source_target_pairs={{0,1},{1,0},{2,3},{3,2},{4,5},{5,4},{6,7},{7,6},{8,9},{9,8},{10,11... | collective-permute-start | bytes 798728 | tf_op jit(solution)/shard_map/ppermute | solution.py:62
  71.2 3.6 %collective-permute-start.18 = (f32[5,1,104,128]{3,2,1,0:T(8,128)S(1)}, f32[5,1,104,128]{3,2,1,0:T(8,128)S(1)}, u32[]{:S(2)}, u32[]{:S(2)}) collective-permute-start(f32[5,1,104,128]{3,2,1,0:T(8,128)S(1)} %collective-permute-done.14.refs_10_), channel_id=1, source_target_pairs={{0,1},{1,0},{2,3},{3,2},{4,5},{5,4},{6,7},{7,6},{8,9},{9,8},{10,11... | collective-permute-start | bytes 798728 | tf_op jit(solution)/shard_map/ppermute | solution.py:62
  72.6 1.4 %collective-permute-start.8 = (f32[16,256]{1,0:T(8,128)S(1)}, f32[16,256]{1,0:T(8,128)S(1)}, u32[]{:S(2)}, u32[]{:S(2)}) collective-permute-start(f32[16,256]{1,0:T(8,128)S(1)} %shard_map.164.mine), channel_id=1, source_target_pairs={{0,1},{1,0},{2,3},{3,2},{4,5},{5,4},{6,7},{7,6},{8,9},{9,8},{10,11... | collective-permute-start | bytes 49160 | tf_op jit(solution)/shard_map/ppermute | solution.py:62
  73.2 4.5 %collective-permute-start.9 = (f32[8,1,104,128]{3,2,1,0:T(8,128)S(1)}, f32[8,1,104,128]{3,2,1,0:T(8,128)S(1)}, u32[]{:S(2)}, u32[]{:S(2)}) collective-permute-start(f32[8,1,104,128]{3,2,1,0:T(8,128)S(1)} %collective-permute-done.refs_0_), channel_id=1, source_target_pairs={{0,1},{1,0},{2,3},{3,2},{4,5},{5,4},{6,7},{7,6},{8,9},{9,8},{10,11... | collective-permute-start | bytes 1277960 | tf_op jit(solution)/shard_map/ppermute | solution.py:62
  74.0 3.7 %collective-permute-start.10 = (f32[8,1,104,128]{3,2,1,0:T(8,128)S(1)}, f32[8,1,104,128]{3,2,1,0:T(8,128)S(1)}, u32[]{:S(2)}, u32[]{:S(2)}) collective-permute-start(f32[8,1,104,128]{3,2,1,0:T(8,128)S(1)} %collective-permute-done.1.refs_1_), channel_id=1, source_target_pairs={{0,1},{1,0},{2,3},{3,2},{4,5},{5,4},{6,7},{7,6},{8,9},{9,8},{10,11... | collective-permute-start | bytes 1277960 | tf_op jit(solution)/shard_map/ppermute | solution.py:62
  74.4 3.3 %collective-permute-start.11 = (f32[8,1,104,128]{3,2,1,0:T(8,128)S(1)}, f32[8,1,104,128]{3,2,1,0:T(8,128)S(1)}, u32[]{:S(2)}, u32[]{:S(2)}) collective-permute-start(f32[8,1,104,128]{3,2,1,0:T(8,128)S(1)} %collective-permute-done.2.refs_2_), channel_id=1, source_target_pairs={{0,1},{1,0},{2,3},{3,2},{4,5},{5,4},{6,7},{7,6},{8,9},{9,8},{10,11... | collective-permute-start | bytes 1277960 | tf_op jit(solution)/shard_map/ppermute | solution.py:62
  74.5 3.2 %collective-permute-start.12 = (f32[8,1,104,128]{3,2,1,0:T(8,128)S(1)}, f32[8,1,104,128]{3,2,1,0:T(8,128)S(1)}, u32[]{:S(2)}, u32[]{:S(2)}) collective-permute-start(f32[8,1,104,128]{3,2,1,0:T(8,128)S(1)} %collective-permute-done.6.refs_3_), channel_id=1, source_target_pairs={{0,1},{1,0},{2,3},{3,2},{4,5},{5,4},{6,7},{7,6},{8,9},{9,8},{10,11... | collective-permute-start | bytes 1277960 | tf_op jit(solution)/shard_map/ppermute | solution.py:62
  74.9 2.8 %collective-permute-start.19 = (f32[5,1,104,128]{3,2,1,0:T(8,128)S(1)}, f32[5,1,104,128]{3,2,1,0:T(8,128)S(1)}, u32[]{:S(2)}, u32[]{:S(2)}) collective-permute-start(f32[5,1,104,128]{3,2,1,0:T(8,128)S(1)} %collective-permute-done.15.refs_11_), channel_id=1, source_target_pairs={{0,1},{1,0},{2,3},{3,2},{4,5},{5,4},{6,7},{7,6},{8,9},{9,8},{10,11... | collective-permute-start | bytes 798728 | tf_op jit(solution)/shard_map/ppermute | solution.py:62
  77.7 18.9 %copy-start.4 = (s32[4]{0:T(128)S(1)}, s32[4]{0:T(128)}, u32[]{:S(2)}) copy-start(s32[4]{0:T(128)} %owners.1) | copy-start | bytes 52
  89.2 6.5 %collective-permute-start.20 = (f32[2,48,128]{2,1,0:T(8,128)S(1)}, f32[2,48,128]{2,1,0:T(8,128)S(1)}, u32[]{:S(2)}, u32[]{:S(2)}) collective-permute-start(f32[2,48,128]{2,1,0:T(8,128)S(1)} %get-tuple-element.48), channel_id=1, source_target_pairs={{0,4},{4,8},{8,12},{12,0},{1,5},{5,9},{9,13},{13,1},{2,6},{6,10},{... | collective-permute-start | bytes 147464 | tf_op jit(solution)/shard_map/ppermute | solution.py:71
  89.3 7.3 %collective-permute-start.21 = (f32[2,48,128]{2,1,0:T(8,128)S(1)}, f32[2,48,128]{2,1,0:T(8,128)S(1)}, u32[]{:S(2)}, u32[]{:S(2)}) collective-permute-start(f32[2,48,128]{2,1,0:T(8,128)S(1)} %get-tuple-element.49), channel_id=1, source_target_pairs={{0,8},{4,12},{8,0},{12,4},{1,9},{5,13},{9,1},{13,5},{2,10},{6,14},... | collective-permute-start | bytes 147464 | tf_op jit(solution)/shard_map/ppermute | solution.py:71
  91.3 5.3 %collective-permute-start.22 = (f32[2,48,128]{2,1,0:T(8,128)S(1)}, f32[2,48,128]{2,1,0:T(8,128)S(1)}, u32[]{:S(2)}, u32[]{:S(2)}) collective-permute-start(f32[2,48,128]{2,1,0:T(8,128)S(1)} %get-tuple-element.50), channel_id=1, source_target_pairs={{0,12},{4,0},{8,4},{12,8},{1,13},{5,1},{9,5},{13,9},{2,14},{6,2},{... | collective-permute-start | bytes 147464 | tf_op jit(solution)/shard_map/ppermute | solution.py:71
  97.3 5.0 %collective-permute-start.25 = (f32[2,96,128]{2,1,0:T(8,128)S(1)}, f32[2,96,128]{2,1,0:T(8,128)S(1)}, u32[]{:S(2)}, u32[]{:S(2)}) collective-permute-start(f32[2,96,128]{2,1,0:T(8,128)S(1)} %get-tuple-element.54), channel_id=1, source_target_pairs={{0,3},{1,2},{2,1},{3,0},{4,7},{5,6},{6,5},{7,4},{8,11},{9,10},{10,... | collective-permute-start | bytes 294920 | tf_op jit(solution)/shard_map/ppermute | solution.py:62
  97.9 6.6 %collective-permute-start.24 = (f32[2,96,128]{2,1,0:T(8,128)S(1)}, f32[2,96,128]{2,1,0:T(8,128)S(1)}, u32[]{:S(2)}, u32[]{:S(2)}) collective-permute-start(f32[2,96,128]{2,1,0:T(8,128)S(1)} %get-tuple-element.53), channel_id=1, source_target_pairs={{0,2},{1,3},{2,0},{3,1},{4,6},{5,7},{6,4},{7,5},{8,10},{9,11},{10,... | collective-permute-start | bytes 294920 | tf_op jit(solution)/shard_map/ppermute | solution.py:62
  99.0 5.5 %collective-permute-start.23 = (f32[2,96,128]{2,1,0:T(8,128)S(1)}, f32[2,96,128]{2,1,0:T(8,128)S(1)}, u32[]{:S(2)}, u32[]{:S(2)}) collective-permute-start(f32[2,96,128]{2,1,0:T(8,128)S(1)} %get-tuple-element.52), channel_id=1, source_target_pairs={{0,1},{1,0},{2,3},{3,2},{4,5},{5,4},{6,7},{7,6},{8,9},{9,8},{10,11... | collective-permute-start | bytes 294920 | tf_op jit(solution)/shard_map/ppermute | solution.py:62
  (2 other events, 4.1 us)

commit v5 on v4

--- a/solution.py
+++ b/solution.py
@@ -18,7 +18,6 @@
     def __init__(self, domain, shots, rows, lines, steps):
         self.domain, self.shots, self.rows, self.lines, self.steps = domain, shots, rows, lines, steps
         self.half = domain // 2
-        self.part = rows // 2
         self.width = rows * domain
         self.own = lines // domain
         halo = -(-steps // TILE) * TILE
@@ -43,15 +42,17 @@
         d, s = lax.axis_index("domain"), lax.axis_index("shot")
         return lax.rem(d, self.half), s & 1, d, d // self.half
 
+    def chip_of(self, d, r):
+        return lax.rem((d >> 1) + r, self.half) if not isinstance(d, int) else ((d >> 1) + r) % self.half
+
     def rounds(self):
         count = self.domain * self.shots
-        for r in range(self.domain):
+        for r in range(self.half):
             pairs = []
             for d in range(self.domain):
                 for s in range(self.shots):
-                    k = (d + r) % self.domain
-                    to_d = self.half * (s & 1) + (k >> 1)
-                    to_s = (s & ~1) | (k & 1)
+                    to_d = self.half * (s & 1) + self.chip_of(d, r)
+                    to_s = (s & ~1) | (d & 1)
                     pairs.append((d * self.shots + s, to_d * self.shots + to_s))
             assert len({pair[1] for pair in pairs}) == count
             yield r, pairs
@@ -75,11 +76,10 @@
     kc, c, unused, unused = lay.position()
     window = pl.ds(pl.multiple_of(lay.shift(c), TILE), lay.span)
     for core, refs in ((c, own_refs), (1 - c, other_refs)):
-        k = 2 * kc + core
         for r, ref in enumerate(refs):
-            source = lax.rem(k - r + lay.domain, lay.domain)
-            for part in range(lay.part):
-                store(source * lay.rows + core * lay.part + part, ref.at[:, part, window, :])
+            source = 2 * lax.rem(kc - r + lay.half, lay.half) + core
+            for part in range(lay.rows):
+                store(source * lay.rows + part, ref.at[:, part, window, :])
 
 
 def table_kernel(traces, wavelet, rec_x, rec_y, src_x, src_y, anchor, table):
@@ -329,10 +329,8 @@
 
 
 def wave_kernel(lay, scalars, source_ref, receiver_ref, *refs):
-    waves_own, waves_other, model_own, model_other, pieces = (
-        refs[i * lay.domain : (i + 1) * lay.domain] for i in range(5)
-    )
-    raw, coef_ref, image_ref, state = refs[5 * lay.domain :]
+    waves_own, waves_other, model_own, model_other = (refs[i * lay.half : (i + 1) * lay.half] for i in range(4))
+    pieces, (raw, coef_ref, image_ref, state) = refs[4 * lay.half : -4], refs[-4:]
     clear_edges(state, lay)
 
     def store_wave(row, ref):
@@ -428,11 +426,11 @@
     def wave_messages(fields):
         fields = [jnp.pad(field[0], ((0, 0), (0, 0), lay.pad, (0, 0))) for field in fields]
         messages = []
-        for r in range(domain):
-            k = lax.rem(d + r, domain)
-            spot = (zero, (k & 1) * lay.part, lay.start(k >> 1), zero)
-            size = (2, lay.part, lay.chip, z_count)
-            messages.append(jnp.concatenate([lax.dynamic_slice(field, spot, size) for field in fields]))
+        for r in range(lay.half):
+            first = lay.start(lay.chip_of(d, r))
+            messages.append(
+                jnp.concatenate([lax.dynamic_slice_in_dim(field, first, lay.chip, 2) for field in fields])
+            )
         return messages
 
     def send(messages):
@@ -442,7 +440,6 @@
         return [swapped(message, "shot", 1) for message in messages]
 
     messages = wave_messages((source_now, source_before, receiver_now, receiver_before))
-    velocity, messages[0] = lax.optimization_barrier((velocity, messages[0]))
     waves = send(messages)
     model = medium(velocity, thomsen_eps, thomsen_delta, tilt_angle, azimuth)
     slab = model.shape[2]
@@ -459,18 +456,18 @@
         model = jnp.pad(model, ((0, 0), (0, 0), lay.pad, (0, 0)))
         first_line = zero
     messages = []
-    for r in range(domain):
-        k = lax.rem(d + r, domain)
-        spot = (zero, (k & 1) * lay.part, first_line + lay.start(k >> 1), zero)
-        messages.append(lax.dynamic_slice(model, spot, (5, lay.part, lay.chip, z_count)))
-    *messages, waves[-1] = lax.optimization_barrier((*messages, waves[-1]))
+    for r in range(lay.half):
+        first = first_line + lay.start(lay.chip_of(d, r))
+        messages.append(lax.dynamic_slice_in_dim(model, first, lay.chip, 2))
     models = send(messages)
     *waves, models[0] = lax.optimization_barrier((*waves, models[0]))
-    waves_other, models_other = other_core(waves), other_core(models)
+    waves_other = other_core(waves)
 
     traces, waves[0] = lax.optimization_barrier((traces, waves[0]))
     table = table_of(traces, wavelet, receiver_x, receiver_y, source_x, source_y, shot_anchor)
     receiver_pulse, source_pulse, scalars = pulses(lay, table, swapped(table, "shot", 1), z_count)
+    *models, receiver_pulse = lax.optimization_barrier((*models, receiver_pulse))
+    models_other = other_core(models)
     block = (lay.width, lay.span, z_count)
     pieces = call(
         wave_kernel,

time: 106 us -> 102 us (0.962)
  starting transfers between devices: 45.2 us -> 35.9 us
  waiting for transfers between devices: 34 us -> 40.5 us
  other arithmetic: 3.56 us -> 1.69 us
    ppermute x8 -> x4, starting transfers between devices: 33.5 us -> 7.55 us  [send(): lax.ppermute(messages[r], ('domain', 'shot'), pairs)]
    ppermute x15 -> x11, starting transfers between devices: 7.43 us -> 23.1 us  [swapped(): return lax.ppermute(value, axis, [(i, i ^ bit) for i in range(count)])]
    ppermute x15 -> x11, waiting for transfers between devices: 12.9 us -> 21.6 us  [swapped(): return lax.ppermute(value, axis, [(i, i ^ bit) for i in range(count)])]
    dynamic_update_slice x4, local copies, waits for them, and re-layouts: 0.15 us -> 2.21 us  [per_device(): lax.dynamic_update_slice(whole, block, (zero, zero, (s ^ r) * slab, zero))]
    concatenate x4 -> x2, other arithmetic: 2.9 us -> 1.03 us  [wave_messages(): jnp.concatenate([lax.dynamic_slice_in_dim(field, first, lay.chip, 2) for...]
    ppermute x8 -> x4, waiting for transfers between devices: 17.9 us -> 16.2 us  [send(): lax.ppermute(messages[r], ('domain', 'shot'), pairs)]
    dynamic_slice x3, local copies, waits for them, and re-layouts: 2.97 us -> 1.5 us  [the longest x2 1.39 us: wave_messages(): lax.dynamic_slice_in_dim(field, first, lay.chip, 2)]
  transfers between devices with their start and end apart: 26 -> 18, of which waited for: 9 -> 10; matrix products, arithmetic and copies ran while one was open for 3% -> 5% of each run, Pallas kernels for 2% -> 3%
where the time goes in v5:
time: 102 us; the launch traced here: 101 us
  waiting for transfers between devices  40.5 us (40%)
  starting transfers between devices  35.9 us (35%)
  Pallas kernels  16.9 us (17%)
  local copies, waits for them, and re-layouts  3.9 us (4%)
  between operations  2.22 us (2%)
  other arithmetic  1.69 us (2%)
    ppermute x11, starting transfers between devices, swapped(): return lax.ppermute(value, axis, [(i, i ^ bit) for i in range(count)])  23.1 us
    ppermute x11, waiting for transfers between devices, swapped(): return lax.ppermute(value, axis, [(i, i ^ bit) for i in range(count)])  21.6 us
    ppermute x4, waiting for transfers between devices, send(): lax.ppermute(messages[r], ('domain', 'shot'), pairs)  16.2 us
    pallas_call x2, Pallas kernels, call(): pl.pallas_call(functools.partial(kernel, lay), out_shape=outs, in_specs=[...  12.1 us
    ppermute x4, starting transfers between devices, send(): lax.ppermute(messages[r], ('domain', 'shot'), pairs)  7.55 us
    ppermute x3, starting transfers between devices, swapped_round(): lax.ppermute(value, axis, [(i, (i + r) % count) for i in range(count)])  5.29 us
    ppermute x3, waiting for transfers between devices, swapped_round(): lax.ppermute(value, axis, [(i, (i + r) % count) for i in range(count)])  2.76 us
    pallas_call x1, Pallas kernels, pulses(): pl.pallas_call(functools.partial(pulse_kernel, lay), out_shape=[jax.Shape...  2.62 us
  transfers between devices with their start and end apart: 18, of which 10 were waited for; matrix products, arithmetic and copies ran while one was open for 5% of the time, Pallas kernels for 3%

profile of v5, /device:TPU:0, one launch (start us, length us, event | category | flops | bytes accessed | tf_op | source)
XLA Modules:
  0.0 101.2 jit_solution(4497916418781431114)
XLA Ops:
  0.0 2.2 %shard_map.163 = f32[5,2,96,128]{3,2,1,0:T(8,128)} custom-call(f32[2,96,128]{2,1,0:T(8,128)} %velocity.1, f32[2,96,128]{2,1,0:T(8,128)} %eps.1, f32[2,96,128]{2,1,0:T(8,128)} %delta.1, f32[2,96,128]{2,1,0:T(8,128)} %tilt.1, f32[2,96,128]{2,1,0:T(8,128)} %azimuth.1), custom_call_target="tpu_custom_call" | custom-call | tf_op jit(solution)/shard_map/pallas_call | solution.py:190
  2.2 0.5 collective-permute-start.2
  2.6 2.5 %collective-permute-start.3 = (f32[5,2,96,128]{3,2,1,0:T(8,128)}, f32[5,2,96,128]{3,2,1,0:T(8,128)}, u32[]{:S(2)}, u32[]{:S(2)}) collective-permute-start(f32[5,2,96,128]{3,2,1,0:T(8,128)} %shard_map.163), channel_id=1, source_target_pairs={{0,2},{1,3},{2,0},{3,1},{4,6},{5,7},{6,4},{7,5},{8,10},{9,11},{10,... | collective-permute-start | bytes 1474568 | tf_op jit(solution)/shard_map/ppermute | solution.py:63
  5.3 1.3 %dynamic-slice_bitcast_fusion.2 = (f32[2,2,104,128]{3,2,1,0:T(8,128)S(1)}, f32[2,2,104,128]{3,2,1,0:T(8,128)S(1)}, f32[2,2,104,128]{3,2,1,0:T(8,128)S(1)}, f32[2,2,104,128]{3,2,1,0:T(8,128)S(1)}) fusion(f32[1,2,2,192,128]{4,3,2,1,0:T(8,128)} %param.30, s32[]{:T(128)S(6)} %select_n.31, s32[]{:T(128)S(6)} %select_n.30, f32[1,2,2,192,128]{4,3,2,1,0:T(8,128)} %param.29), kind=kLoop, calls=%fused_computation.4 | loop fusion | bytes 1703944 | tf_op jit(solution)/shard_map/dynamic_slice | solution.py:432
  6.8 1.9 %collective-permute-start.1 = (f32[8,2,104,128]{3,2,1,0:T(8,128)S(1)}, f32[8,2,104,128]{3,2,1,0:T(8,128)S(1)}, u32[]{:S(2)}, u32[]{:S(2)}) collective-permute-start(f32[8,2,104,128]{3,2,1,0:T(8,128)S(1)} %pad_maximum_fusion.1), channel_id=1, source_target_pairs={{0,4},{1,12},{2,6},{3,14},{4,5},{5,13},{6,7},{7,15},{8,0},{9,8},{1... | collective-permute-start | bytes 2555912 | tf_op jit(solution)/shard_map/ppermute | solution.py:437
  8.6 1.0 pad_maximum_fusion
  9.6 1.8 %collective-permute-start = (f32[8,2,104,128]{3,2,1,0:T(8,128)}, f32[8,2,104,128]{3,2,1,0:T(8,128)S(1)}, u32[]{:S(2)}, u32[]{:S(2)}) collective-permute-start(f32[8,2,104,128]{3,2,1,0:T(8,128)} %pad_maximum_fusion), channel_id=1, source_target_pairs={{0,0},{1,8},{2,2},{3,10},{4,1},{5,9},{6,3},{7,11},{8,4},{9,12},{10... | collective-permute-start | bytes 2555912 | tf_op jit(solution)/shard_map/ppermute | solution.py:437
  12.3 1.1 %constant_dynamic-update-slice_fusion.2 = f32[5,2,384,128]{3,2,1,0:T(8,128)S(1)} fusion(f32[5,2,384,128]{3,2,1,0:T(8,128)S(1)} %constant_dynamic-update-slice_fusion.3, f32[5,2,96,128]{3,2,1,0:T(8,128)} %collective-permute-done.2, s32[]{:T(128)S(6)} %select_n.33), kind=kLoop, calls=%fused_computation.15 | loop fusion | bytes 983044 | tf_op jit(solution)/shard_map/dynamic_update_slice | solution.py:449
  13.4 4.1 %collective-permute-done.3 = f32[5,2,96,128]{3,2,1,0:T(8,128)} collective-permute-done((f32[5,2,96,128]{3,2,1,0:T(8,128)}, f32[5,2,96,128]{3,2,1,0:T(8,128)}, u32[]{:S(2)}, u32[]{:S(2)}) %collective-permute-start.3) | collective-permute-done | bytes 491552 | tf_op jit(solution)/shard_map/ppermute | solution.py:63
  17.5 1.1 %constant_dynamic-update-slice_fusion.1 = f32[5,2,384,128]{3,2,1,0:T(8,128)S(1)} fusion(f32[5,2,384,128]{3,2,1,0:T(8,128)S(1)} %constant_dynamic-update-slice_fusion.2, f32[5,2,96,128]{3,2,1,0:T(8,128)} %collective-permute-done.3, s32[]{:T(128)S(6)} %select_n.34), kind=kLoop, calls=%fused_computation.14 | loop fusion | bytes 983044 | tf_op jit(solution)/shard_map/dynamic_update_slice | solution.py:449
  18.6 9.0 %collective-permute-done.4 = f32[5,2,96,128]{3,2,1,0:T(8,128)S(1)} collective-permute-done((f32[5,2,96,128]{3,2,1,0:T(8,128)}, f32[5,2,96,128]{3,2,1,0:T(8,128)S(1)}, u32[]{:S(2)}, u32[]{:S(2)}) %collective-permute-start.4) | collective-permute-done | bytes 491552 | tf_op jit(solution)/shard_map/ppermute | solution.py:63
  27.7 0.7 collective-permute-start.5
  28.4 3.2 %collective-permute-start.7 = (f32[5,2,104,128]{3,2,1,0:T(8,128)S(1)}, f32[5,2,104,128]{3,2,1,0:T(8,128)S(1)}, u32[]{:S(2)}, u32[]{:S(2)}) collective-permute-start(f32[5,2,104,128]{3,2,1,0:T(8,128)S(1)} %get-tuple-element.43), channel_id=1, source_target_pairs={{0,4},{1,12},{2,6},{3,14},{4,5},{5,13},{6,7},{7,15},{8,0},{9,8},{1... | collective-permute-start | bytes 1597448 | tf_op jit(solution)/shard_map/ppermute | solution.py:437
  31.6 17.0 %collective-permute-start.8 = (f32[8,2,104,128]{3,2,1,0:T(8,128)S(1)}, f32[8,2,104,128]{3,2,1,0:T(8,128)S(1)}, u32[]{:S(2)}, u32[]{:S(2)}) collective-permute-start(f32[8,2,104,128]{3,2,1,0:T(8,128)S(1)} %collective-permute-done.refs_0_), channel_id=1, source_target_pairs={{0,1},{1,0},{2,3},{3,2},{4,5},{5,4},{6,7},{7,6},{8,9},{9,8},{10,11... | collective-permute-start | bytes 2555912 | tf_op jit(solution)/shard_map/ppermute | solution.py:63
  50.0 0.6 collective-permute-start.6
  50.6 1.3 %collective-permute-done.6.twin = f32[16,256]{1,0:T(8,128)S(1)} collective-permute-done((f32[16,256]{1,0:T(8,128)S(1)}, f32[16,256]{1,0:T(8,128)S(1)}, u32[]{:S(2)}, u32[]{:S(2)}) %collective-permute-start.6) | collective-permute-done | bytes 16416 | tf_op jit(solution)/shard_map/ppermute | solution.py:63
  51.9 2.6 %shard_map.165 = (f32[8,64,128]{2,1,0:T(8,128)S(1)}, f32[8,8,128]{2,1,0:T(8,128)S(1)}, s32[4]{0:T(128)S(1)}) custom-call(f32[16,256]{1,0:T(8,128)S(1)} %shard_map.164.mine, f32[16,256]{1,0:T(8,128)S(1)} %collective-permute-done.6.twin), custom_call_target="tpu_custom_call" | custom-call | tf_op jit(solution)/shard_map/pallas_call | solution.py:156
  54.5 16.2 %collective-permute-done.7.refs_5_ = f32[5,2,104,128]{3,2,1,0:T(8,128)S(1)} collective-permute-done((f32[5,2,104,128]{3,2,1,0:T(8,128)S(1)}, f32[5,2,104,128]{3,2,1,0:T(8,128)S(1)}, u32[]{:S(2)}, u32[]{:S(2)}) %collective-permute-start.7) | collective-permute-done | bytes 532512 | tf_op jit(solution)/shard_map/ppermute | solution.py:437
  70.7 0.5 collective-permute-start.11
  71.2 1.4 %collective-permute-done.10.refs_6_ = f32[5,2,104,128]{3,2,1,0:T(8,128)S(1)} collective-permute-done((f32[5,2,104,128]{3,2,1,0:T(8,128)S(1)}, f32[5,2,104,128]{3,2,1,0:T(8,128)S(1)}, u32[]{:S(2)}, u32[]{:S(2)}) %collective-permute-start.10) | collective-permute-done | bytes 532512 | tf_op jit(solution)/shard_map/ppermute | solution.py:63
  72.6 0.8 collective-permute-done.11.refs_7_
  73.4 11.5 %shard_map.166 = (f32[2,48,128]{2,1,0:T(8,128)S(1)}, f32[2,48,128]{2,1,0:T(8,128)S(1)}, f32[2,48,128]{2,1,0:T(8,128)S(1)}, f32[2,48,128]{2,1,0:T(8,128)S(1)}) custom-call(s32[4]{0:T(128)S(1)} %get-tuple-element.26.scalars, f32[8,8,128]{2,1,0:T(8,128)S(1)} %get-tuple-element.27.source_ref, f32[8,64,128]{2,1,0:T(8,128)S(1)} %get-tuple-element.30.receiver_ref, ...), custom_call_target="tpu_custom_call" | custom-call | bytes 60000000 | tf_op jit(solution)/shard_map/pallas_call | solution.py:387
  84.9 1.2 %collective-permute-start.12 = (f32[2,48,128]{2,1,0:T(8,128)S(1)}, f32[2,48,128]{2,1,0:T(8,128)S(1)}, u32[]{:S(2)}, u32[]{:S(2)}) collective-permute-start(f32[2,48,128]{2,1,0:T(8,128)S(1)} %get-tuple-element.36), channel_id=1, source_target_pairs={{0,4},{4,8},{8,12},{12,0},{1,5},{5,9},{9,13},{13,1},{2,6},{6,10},{... | collective-permute-start | bytes 147464 | tf_op jit(solution)/shard_map/ppermute | solution.py:72
  86.1 2.0 %collective-permute-start.13 = (f32[2,48,128]{2,1,0:T(8,128)S(1)}, f32[2,48,128]{2,1,0:T(8,128)S(1)}, u32[]{:S(2)}, u32[]{:S(2)}) collective-permute-start(f32[2,48,128]{2,1,0:T(8,128)S(1)} %get-tuple-element.37), channel_id=1, source_target_pairs={{0,8},{4,12},{8,0},{12,4},{1,9},{5,13},{9,1},{13,5},{2,10},{6,14},... | collective-permute-start | bytes 147464 | tf_op jit(solution)/shard_map/ppermute | solution.py:72
  88.1 2.1 %collective-permute-start.14 = (f32[2,48,128]{2,1,0:T(8,128)S(1)}, f32[2,48,128]{2,1,0:T(8,128)S(1)}, u32[]{:S(2)}, u32[]{:S(2)}) collective-permute-start(f32[2,48,128]{2,1,0:T(8,128)S(1)} %get-tuple-element.38), channel_id=1, source_target_pairs={{0,12},{4,0},{8,4},{12,8},{1,13},{5,1},{9,5},{13,9},{2,14},{6,2},{... | collective-permute-start | bytes 147464 | tf_op jit(solution)/shard_map/ppermute | solution.py:72
  90.1 0.7 collective-permute-done.12.refs_1_
  90.8 2.1 %collective-permute-done.13.refs_2_ = f32[2,48,128]{2,1,0:T(8,128)S(1)} collective-permute-done((f32[2,48,128]{2,1,0:T(8,128)S(1)}, f32[2,48,128]{2,1,0:T(8,128)S(1)}, u32[]{:S(2)}, u32[]{:S(2)}) %collective-permute-start.13) | collective-permute-done | bytes 49184 | tf_op jit(solution)/shard_map/ppermute | solution.py:72
  92.9 0.7 shard_map.167
  93.6 1.8 %collective-permute-start.16 = (f32[2,96,128]{2,1,0:T(8,128)S(1)}, f32[2,96,128]{2,1,0:T(8,128)S(1)}, u32[]{:S(2)}, u32[]{:S(2)}) collective-permute-start(f32[2,96,128]{2,1,0:T(8,128)S(1)} %get-tuple-element.41), channel_id=1, source_target_pairs={{0,2},{1,3},{2,0},{3,1},{4,6},{5,7},{6,4},{7,5},{8,10},{9,11},{10,... | collective-permute-start | bytes 294920 | tf_op jit(solution)/shard_map/ppermute | solution.py:63
  95.5 3.8 %collective-permute-done.16 = f32[2,96,128]{2,1,0:T(8,128)S(1)} collective-permute-done((f32[2,96,128]{2,1,0:T(8,128)S(1)}, f32[2,96,128]{2,1,0:T(8,128)S(1)}, u32[]{:S(2)}, u32[]{:S(2)}) %collective-permute-start.16) | collective-permute-done | bytes 98336 | tf_op jit(solution)/shard_map/ppermute | solution.py:63
  99.3 1.3 %collective-permute-done.17 = f32[2,96,128]{2,1,0:T(8,128)S(1)} collective-permute-done((f32[2,96,128]{2,1,0:T(8,128)S(1)}, f32[2,96,128]{2,1,0:T(8,128)S(1)}, u32[]{:S(2)}, u32[]{:S(2)}) %collective-permute-start.17) | collective-permute-done | bytes 98336 | tf_op jit(solution)/shard_map/ppermute | solution.py:63
  100.5 0.7 add_multiply_fusion
  (36 shorter events, 0.8 us)
Async XLA Ops:
  0.0 6.6 %copy-start.7 = (f32[1,2,2,192,128]{4,3,2,1,0:T(8,128)S(1)}, f32[1,2,2,192,128]{4,3,2,1,0:T(8,128)}, u32[]{:S(2)}) copy-start(f32[1,2,2,192,128]{4,3,2,1,0:T(8,128)} %param.31) | copy-start | bytes 1179652
  0.0 6.6 %copy-start.6 = (f32[1,2,2,192,128]{4,3,2,1,0:T(8,128)S(1)}, f32[1,2,2,192,128]{4,3,2,1,0:T(8,128)}, u32[]{:S(2)}) copy-start(f32[1,2,2,192,128]{4,3,2,1,0:T(8,128)} %param.32) | copy-start | bytes 1179652
  2.2 10.1 %collective-permute-start.2 = (f32[5,2,96,128]{3,2,1,0:T(8,128)}, f32[5,2,96,128]{3,2,1,0:T(8,128)}, u32[]{:S(2)}, u32[]{:S(2)}) collective-permute-start(f32[5,2,96,128]{3,2,1,0:T(8,128)} %shard_map.163), channel_id=1, source_target_pairs={{0,1},{1,0},{2,3},{3,2},{4,5},{5,4},{6,7},{7,6},{8,9},{9,8},{10,11... | collective-permute-start | bytes 1474568 | tf_op jit(solution)/shard_map/ppermute | solution.py:63
  2.6 14.9 %collective-permute-start.3 = (f32[5,2,96,128]{3,2,1,0:T(8,128)}, f32[5,2,96,128]{3,2,1,0:T(8,128)}, u32[]{:S(2)}, u32[]{:S(2)}) collective-permute-start(f32[5,2,96,128]{3,2,1,0:T(8,128)} %shard_map.163), channel_id=1, source_target_pairs={{0,2},{1,3},{2,0},{3,1},{4,6},{5,7},{6,4},{7,5},{8,10},{9,11},{10,... | collective-permute-start | bytes 1474568 | tf_op jit(solution)/shard_map/ppermute | solution.py:63
  5.1 22.4 %collective-permute-start.4 = (f32[5,2,96,128]{3,2,1,0:T(8,128)}, f32[5,2,96,128]{3,2,1,0:T(8,128)S(1)}, u32[]{:S(2)}, u32[]{:S(2)}) collective-permute-start(f32[5,2,96,128]{3,2,1,0:T(8,128)} %shard_map.163), channel_id=1, source_target_pairs={{0,3},{1,2},{2,1},{3,0},{4,7},{5,6},{6,5},{7,4},{8,11},{9,10},{10,... | collective-permute-start | bytes 1474568 | tf_op jit(solution)/shard_map/ppermute | solution.py:63
  6.8 5.5 %copy-start.5 = (f32[5,2,96,128]{3,2,1,0:T(8,128)S(1)}, f32[5,2,96,128]{3,2,1,0:T(8,128)}, u32[]{:S(2)}) copy-start(f32[5,2,96,128]{3,2,1,0:T(8,128)} %shard_map.163) | copy-start | bytes 1474564
  6.8 24.9 %collective-permute-start.1 = (f32[8,2,104,128]{3,2,1,0:T(8,128)S(1)}, f32[8,2,104,128]{3,2,1,0:T(8,128)S(1)}, u32[]{:S(2)}, u32[]{:S(2)}) collective-permute-start(f32[8,2,104,128]{3,2,1,0:T(8,128)S(1)} %pad_maximum_fusion.1), channel_id=1, source_target_pairs={{0,4},{1,12},{2,6},{3,14},{4,5},{5,13},{6,7},{7,15},{8,0},{9,8},{1... | collective-permute-start | bytes 2555912 | tf_op jit(solution)/shard_map/ppermute | solution.py:437
  9.6 22.0 %collective-permute-start = (f32[8,2,104,128]{3,2,1,0:T(8,128)}, f32[8,2,104,128]{3,2,1,0:T(8,128)S(1)}, u32[]{:S(2)}, u32[]{:S(2)}) collective-permute-start(f32[8,2,104,128]{3,2,1,0:T(8,128)} %pad_maximum_fusion), channel_id=1, source_target_pairs={{0,0},{1,8},{2,2},{3,10},{4,1},{5,9},{6,3},{7,11},{8,4},{9,12},{10... | collective-permute-start | bytes 2555912 | tf_op jit(solution)/shard_map/ppermute | solution.py:437
  13.4 36.5 %copy-start = (f32[1,8,256]{2,1,0:T(8,128)S(1)}, f32[1,8,256]{2,1,0:T(8,128)}, u32[]{:S(2)}) copy-start(f32[1,8,256]{2,1,0:T(8,128)} %traces) | copy-start | bytes 24580
  13.4 36.5 %copy-start.1 = (s32[1,256]{1,0:T(1,128)S(1)}, s32[1,256]{1,0:T(1,128)}, u32[]{:S(2)}) copy-start(s32[1,256]{1,0:T(1,128)} %rec_x.1) | copy-start | bytes 3076
  13.4 36.5 %copy-start.2 = (s32[1,256]{1,0:T(1,128)S(1)}, s32[1,256]{1,0:T(1,128)}, u32[]{:S(2)}) copy-start(s32[1,256]{1,0:T(1,128)} %rec_y.1) | copy-start | bytes 3076
  13.4 36.5 %copy-start.3 = (f32[1,8]{1,0:T(1,128)S(1)}, f32[1,8]{1,0:T(1,128)}, u32[]{:S(2)}) copy-start(f32[1,8]{1,0:T(1,128)} %wavelet.1) | copy-start | bytes 100
  27.7 3.9 %collective-permute-start.5 = (f32[5,2,104,128]{3,2,1,0:T(8,128)S(1)}, f32[5,2,104,128]{3,2,1,0:T(8,128)S(1)}, u32[]{:S(2)}, u32[]{:S(2)}) collective-permute-start(f32[5,2,104,128]{3,2,1,0:T(8,128)S(1)} %get-tuple-element.44), channel_id=1, source_target_pairs={{0,0},{1,8},{2,2},{3,10},{4,1},{5,9},{6,3},{7,11},{8,4},{9,12},{10... | collective-permute-start | bytes 1597448 | tf_op jit(solution)/shard_map/ppermute | solution.py:437
  28.4 42.2 %collective-permute-start.7 = (f32[5,2,104,128]{3,2,1,0:T(8,128)S(1)}, f32[5,2,104,128]{3,2,1,0:T(8,128)S(1)}, u32[]{:S(2)}, u32[]{:S(2)}) collective-permute-start(f32[5,2,104,128]{3,2,1,0:T(8,128)S(1)} %get-tuple-element.43), channel_id=1, source_target_pairs={{0,4},{1,12},{2,6},{3,14},{4,5},{5,13},{6,7},{7,15},{8,0},{9,8},{1... | collective-permute-start | bytes 1597448 | tf_op jit(solution)/shard_map/ppermute | solution.py:437
  31.6 41.7 %collective-permute-start.8 = (f32[8,2,104,128]{3,2,1,0:T(8,128)S(1)}, f32[8,2,104,128]{3,2,1,0:T(8,128)S(1)}, u32[]{:S(2)}, u32[]{:S(2)}) collective-permute-start(f32[8,2,104,128]{3,2,1,0:T(8,128)S(1)} %collective-permute-done.refs_0_), channel_id=1, source_target_pairs={{0,1},{1,0},{2,3},{3,2},{4,5},{5,4},{6,7},{7,6},{8,9},{9,8},{10,11... | collective-permute-start | bytes 2555912 | tf_op jit(solution)/shard_map/ppermute | solution.py:63
  48.6 24.7 %collective-permute-start.9 = (f32[8,2,104,128]{3,2,1,0:T(8,128)S(1)}, f32[8,2,104,128]{3,2,1,0:T(8,128)S(1)}, u32[]{:S(2)}, u32[]{:S(2)}) collective-permute-start(f32[8,2,104,128]{3,2,1,0:T(8,128)S(1)} %collective-permute-done.1.refs_1_), channel_id=1, source_target_pairs={{0,1},{1,0},{2,3},{3,2},{4,5},{5,4},{6,7},{7,6},{8,9},{9,8},{10,11... | collective-permute-start | bytes 2555912 | tf_op jit(solution)/shard_map/ppermute | solution.py:63
  50.0 1.9 %collective-permute-start.6 = (f32[16,256]{1,0:T(8,128)S(1)}, f32[16,256]{1,0:T(8,128)S(1)}, u32[]{:S(2)}, u32[]{:S(2)}) collective-permute-start(f32[16,256]{1,0:T(8,128)S(1)} %shard_map.164.mine), channel_id=1, source_target_pairs={{0,1},{1,0},{2,3},{3,2},{4,5},{5,4},{6,7},{7,6},{8,9},{9,8},{10,11... | collective-permute-start | bytes 49160 | tf_op jit(solution)/shard_map/ppermute | solution.py:63
  70.7 1.9 %collective-permute-start.10 = (f32[5,2,104,128]{3,2,1,0:T(8,128)S(1)}, f32[5,2,104,128]{3,2,1,0:T(8,128)S(1)}, u32[]{:S(2)}, u32[]{:S(2)}) collective-permute-start(f32[5,2,104,128]{3,2,1,0:T(8,128)S(1)} %collective-permute-done.5.refs_4_), channel_id=1, source_target_pairs={{0,1},{1,0},{2,3},{3,2},{4,5},{5,4},{6,7},{7,6},{8,9},{9,8},{10,11... | collective-permute-start | bytes 1597448 | tf_op jit(solution)/shard_map/ppermute | solution.py:63
  70.7 2.7 %collective-permute-start.11 = (f32[5,2,104,128]{3,2,1,0:T(8,128)S(1)}, f32[5,2,104,128]{3,2,1,0:T(8,128)S(1)}, u32[]{:S(2)}, u32[]{:S(2)}) collective-permute-start(f32[5,2,104,128]{3,2,1,0:T(8,128)S(1)} %collective-permute-done.7.refs_5_), channel_id=1, source_target_pairs={{0,1},{1,0},{2,3},{3,2},{4,5},{5,4},{6,7},{7,6},{8,9},{9,8},{10,11... | collective-permute-start | bytes 1597448 | tf_op jit(solution)/shard_map/ppermute | solution.py:63
  73.4 19.5 %copy-start.4 = (s32[4]{0:T(128)S(1)}, s32[4]{0:T(128)}, u32[]{:S(2)}) copy-start(s32[4]{0:T(128)} %owners.1) | copy-start | bytes 52
  84.9 6.0 %collective-permute-start.12 = (f32[2,48,128]{2,1,0:T(8,128)S(1)}, f32[2,48,128]{2,1,0:T(8,128)S(1)}, u32[]{:S(2)}, u32[]{:S(2)}) collective-permute-start(f32[2,48,128]{2,1,0:T(8,128)S(1)} %get-tuple-element.36), channel_id=1, source_target_pairs={{0,4},{4,8},{8,12},{12,0},{1,5},{5,9},{9,13},{13,1},{2,6},{6,10},{... | collective-permute-start | bytes 147464 | tf_op jit(solution)/shard_map/ppermute | solution.py:72
  86.1 6.8 %collective-permute-start.13 = (f32[2,48,128]{2,1,0:T(8,128)S(1)}, f32[2,48,128]{2,1,0:T(8,128)S(1)}, u32[]{:S(2)}, u32[]{:S(2)}) collective-permute-start(f32[2,48,128]{2,1,0:T(8,128)S(1)} %get-tuple-element.37), channel_id=1, source_target_pairs={{0,8},{4,12},{8,0},{12,4},{1,9},{5,13},{9,1},{13,5},{2,10},{6,14},... | collective-permute-start | bytes 147464 | tf_op jit(solution)/shard_map/ppermute | solution.py:72
  88.1 4.8 %collective-permute-start.14 = (f32[2,48,128]{2,1,0:T(8,128)S(1)}, f32[2,48,128]{2,1,0:T(8,128)S(1)}, u32[]{:S(2)}, u32[]{:S(2)}) collective-permute-start(f32[2,48,128]{2,1,0:T(8,128)S(1)} %get-tuple-element.38), channel_id=1, source_target_pairs={{0,12},{4,0},{8,4},{12,8},{1,13},{5,1},{9,5},{13,9},{2,14},{6,2},{... | collective-permute-start | bytes 147464 | tf_op jit(solution)/shard_map/ppermute | solution.py:72
  93.6 1.9 %collective-permute-start.15 = (f32[2,96,128]{2,1,0:T(8,128)S(1)}, f32[2,96,128]{2,1,0:T(8,128)S(1)}, u32[]{:S(2)}, u32[]{:S(2)}) collective-permute-start(f32[2,96,128]{2,1,0:T(8,128)S(1)} %get-tuple-element.40), channel_id=1, source_target_pairs={{0,1},{1,0},{2,3},{3,2},{4,5},{5,4},{6,7},{7,6},{8,9},{9,8},{10,11... | collective-permute-start | bytes 294920 | tf_op jit(solution)/shard_map/ppermute | solution.py:63
  93.6 5.6 %collective-permute-start.16 = (f32[2,96,128]{2,1,0:T(8,128)S(1)}, f32[2,96,128]{2,1,0:T(8,128)S(1)}, u32[]{:S(2)}, u32[]{:S(2)}) collective-permute-start(f32[2,96,128]{2,1,0:T(8,128)S(1)} %get-tuple-element.41), channel_id=1, source_target_pairs={{0,2},{1,3},{2,0},{3,1},{4,6},{5,7},{6,4},{7,5},{8,10},{9,11},{10,... | collective-permute-start | bytes 294920 | tf_op jit(solution)/shard_map/ppermute | solution.py:63
  95.4 5.1 %collective-permute-start.17 = (f32[2,96,128]{2,1,0:T(8,128)S(1)}, f32[2,96,128]{2,1,0:T(8,128)S(1)}, u32[]{:S(2)}, u32[]{:S(2)}) collective-permute-start(f32[2,96,128]{2,1,0:T(8,128)S(1)} %get-tuple-element.42), channel_id=1, source_target_pairs={{0,3},{1,2},{2,1},{3,0},{4,7},{5,6},{6,5},{7,4},{8,11},{9,10},{10,... | collective-permute-start | bytes 294920 | tf_op jit(solution)/shard_map/ppermute | solution.py:63

commit v6 on v5

--- a/solution.py
+++ b/solution.py
@@ -502,9 +502,12 @@
         (scalars, slab_owner),
         *pieces,
     )
+    parts, bit = list(parts), 1
+    while bit < shots:
+        for r in range(0, shots, 2 * bit):
+            parts[r] = parts[r] + swapped(parts[r + bit], "shot", bit)
+        bit *= 2
     total = parts[0]
-    for r in range(1, shots):
-        total = total + swapped(parts[r], "shot", r)
     return total / steps
 
 

time: 102 us -> 101 us (level)
  waiting for transfers between devices: 40.5 us -> 39.4 us
    ppermute x11, waiting for transfers between devices: 21.6 us -> 20.5 us  [swapped(): return lax.ppermute(value, axis, [(i, i ^ bit) for i in range(count)])]
where the time goes in v6:
time: 101 us
  waiting for transfers between devices  39.4 us (39%)
  starting transfers between devices  36.4 us (36%)
  Pallas kernels  16.9 us (17%)
  local copies, waits for them, and re-layouts  3.9 us (4%)
  between operations  2.23 us (2%)
  other arithmetic  1.7 us (2%)
    ppermute x11, starting transfers between devices, swapped(): return lax.ppermute(value, axis, [(i, i ^ bit) for i in range(count)])  23.5 us
    ppermute x11, waiting for transfers between devices, swapped(): return lax.ppermute(value, axis, [(i, i ^ bit) for i in range(count)])  20.5 us
    ppermute x4, waiting for transfers between devices, send(): lax.ppermute(messages[r], ('domain', 'shot'), pairs)  16.2 us
    pallas_call x2, Pallas kernels, call(): pl.pallas_call(functools.partial(kernel, lay), out_shape=outs, in_specs=[...  12.1 us
    ppermute x4, starting transfers between devices, send(): lax.ppermute(messages[r], ('domain', 'shot'), pairs)  7.55 us
    ppermute x3, starting transfers between devices, swapped_round(): lax.ppermute(value, axis, [(i, (i + r) % count) for i in range(count)])  5.32 us
    ppermute x3, waiting for transfers between devices, swapped_round(): lax.ppermute(value, axis, [(i, (i + r) % count) for i in range(count)])  2.72 us
    pallas_call x1, Pallas kernels, pulses(): pl.pallas_call(functools.partial(pulse_kernel, lay), out_shape=[jax.Shape...  2.62 us
  transfers between devices with their start and end apart: 18, of which 10 were waited for; matrix products, arithmetic and copies ran while one was open for 5% of the time, Pallas kernels for 3%

profile of v6, /device:TPU:0, one launch (start us, length us, event | category | flops | bytes accessed | tf_op | source)
XLA Modules:
  0.0 100.5 jit_solution(4914053150380352643)
XLA Ops:
  0.0 2.2 %shard_map.163 = f32[5,2,96,128]{3,2,1,0:T(8,128)} custom-call(f32[2,96,128]{2,1,0:T(8,128)} %velocity.1, f32[2,96,128]{2,1,0:T(8,128)} %eps.1, f32[2,96,128]{2,1,0:T(8,128)} %delta.1, f32[2,96,128]{2,1,0:T(8,128)} %tilt.1, f32[2,96,128]{2,1,0:T(8,128)} %azimuth.1), custom_call_target="tpu_custom_call" | custom-call | tf_op jit(solution)/shard_map/pallas_call | solution.py:190
  2.6 2.5 %collective-permute-start.3 = (f32[5,2,96,128]{3,2,1,0:T(8,128)}, f32[5,2,96,128]{3,2,1,0:T(8,128)}, u32[]{:S(2)}, u32[]{:S(2)}) collective-permute-start(f32[5,2,96,128]{3,2,1,0:T(8,128)} %shard_map.163), channel_id=1, source_target_pairs={{0,2},{1,3},{2,0},{3,1},{4,6},{5,7},{6,4},{7,5},{8,10},{9,11},{10,... | collective-permute-start | bytes 1474568 | tf_op jit(solution)/shard_map/ppermute | solution.py:63
  5.3 1.3 %dynamic-slice_bitcast_fusion.2 = (f32[2,2,104,128]{3,2,1,0:T(8,128)S(1)}, f32[2,2,104,128]{3,2,1,0:T(8,128)S(1)}, f32[2,2,104,128]{3,2,1,0:T(8,128)S(1)}, f32[2,2,104,128]{3,2,1,0:T(8,128)S(1)}) fusion(f32[1,2,2,192,128]{4,3,2,1,0:T(8,128)} %param.30, s32[]{:T(128)S(6)} %select_n.31, s32[]{:T(128)S(6)} %select_n.30, f32[1,2,2,192,128]{4,3,2,1,0:T(8,128)} %param.29), kind=kLoop, calls=%fused_computation.4 | loop fusion | bytes 1703944 | tf_op jit(solution)/shard_map/dynamic_slice | solution.py:432
  6.8 1.9 %collective-permute-start.1 = (f32[8,2,104,128]{3,2,1,0:T(8,128)S(1)}, f32[8,2,104,128]{3,2,1,0:T(8,128)S(1)}, u32[]{:S(2)}, u32[]{:S(2)}) collective-permute-start(f32[8,2,104,128]{3,2,1,0:T(8,128)S(1)} %pad_maximum_fusion.1), channel_id=1, source_target_pairs={{0,4},{1,12},{2,6},{3,14},{4,5},{5,13},{6,7},{7,15},{8,0},{9,8},{1... | collective-permute-start | bytes 2555912 | tf_op jit(solution)/shard_map/ppermute | solution.py:437
  8.6 1.0 pad_maximum_fusion
  9.6 1.8 %collective-permute-start = (f32[8,2,104,128]{3,2,1,0:T(8,128)}, f32[8,2,104,128]{3,2,1,0:T(8,128)S(1)}, u32[]{:S(2)}, u32[]{:S(2)}) collective-permute-start(f32[8,2,104,128]{3,2,1,0:T(8,128)} %pad_maximum_fusion), channel_id=1, source_target_pairs={{0,0},{1,8},{2,2},{3,10},{4,1},{5,9},{6,3},{7,11},{8,4},{9,12},{10... | collective-permute-start | bytes 2555912 | tf_op jit(solution)/shard_map/ppermute | solution.py:437
  12.3 1.1 %constant_dynamic-update-slice_fusion.2 = f32[5,2,384,128]{3,2,1,0:T(8,128)S(1)} fusion(f32[5,2,384,128]{3,2,1,0:T(8,128)S(1)} %constant_dynamic-update-slice_fusion.3, f32[5,2,96,128]{3,2,1,0:T(8,128)} %collective-permute-done.2, s32[]{:T(128)S(6)} %select_n.33), kind=kLoop, calls=%fused_computation.15 | loop fusion | bytes 983044 | tf_op jit(solution)/shard_map/dynamic_update_slice | solution.py:449
  13.4 4.1 %collective-permute-done.3 = f32[5,2,96,128]{3,2,1,0:T(8,128)} collective-permute-done((f32[5,2,96,128]{3,2,1,0:T(8,128)}, f32[5,2,96,128]{3,2,1,0:T(8,128)}, u32[]{:S(2)}, u32[]{:S(2)}) %collective-permute-start.3) | collective-permute-done | bytes 491552 | tf_op jit(solution)/shard_map/ppermute | solution.py:63
  17.5 1.1 %constant_dynamic-update-slice_fusion.1 = f32[5,2,384,128]{3,2,1,0:T(8,128)S(1)} fusion(f32[5,2,384,128]{3,2,1,0:T(8,128)S(1)} %constant_dynamic-update-slice_fusion.2, f32[5,2,96,128]{3,2,1,0:T(8,128)} %collective-permute-done.3, s32[]{:T(128)S(6)} %select_n.34), kind=kLoop, calls=%fused_computation.14 | loop fusion | bytes 983044 | tf_op jit(solution)/shard_map/dynamic_update_slice | solution.py:449
  18.6 9.0 %collective-permute-done.4 = f32[5,2,96,128]{3,2,1,0:T(8,128)S(1)} collective-permute-done((f32[5,2,96,128]{3,2,1,0:T(8,128)}, f32[5,2,96,128]{3,2,1,0:T(8,128)S(1)}, u32[]{:S(2)}, u32[]{:S(2)}) %collective-permute-start.4) | collective-permute-done | bytes 491552 | tf_op jit(solution)/shard_map/ppermute | solution.py:63
  27.7 0.7 collective-permute-start.5
  28.4 3.2 %collective-permute-start.7 = (f32[5,2,104,128]{3,2,1,0:T(8,128)S(1)}, f32[5,2,104,128]{3,2,1,0:T(8,128)S(1)}, u32[]{:S(2)}, u32[]{:S(2)}) collective-permute-start(f32[5,2,104,128]{3,2,1,0:T(8,128)S(1)} %get-tuple-element.43), channel_id=1, source_target_pairs={{0,4},{1,12},{2,6},{3,14},{4,5},{5,13},{6,7},{7,15},{8,0},{9,8},{1... | collective-permute-start | bytes 1597448 | tf_op jit(solution)/shard_map/ppermute | solution.py:437
  31.6 17.0 %collective-permute-start.8 = (f32[8,2,104,128]{3,2,1,0:T(8,128)S(1)}, f32[8,2,104,128]{3,2,1,0:T(8,128)S(1)}, u32[]{:S(2)}, u32[]{:S(2)}) collective-permute-start(f32[8,2,104,128]{3,2,1,0:T(8,128)S(1)} %collective-permute-done.refs_0_), channel_id=1, source_target_pairs={{0,1},{1,0},{2,3},{3,2},{4,5},{5,4},{6,7},{7,6},{8,9},{9,8},{10,11... | collective-permute-start | bytes 2555912 | tf_op jit(solution)/shard_map/ppermute | solution.py:63
  50.0 0.6 collective-permute-start.6
  50.6 1.3 %collective-permute-done.6.twin = f32[16,256]{1,0:T(8,128)S(1)} collective-permute-done((f32[16,256]{1,0:T(8,128)S(1)}, f32[16,256]{1,0:T(8,128)S(1)}, u32[]{:S(2)}, u32[]{:S(2)}) %collective-permute-start.6) | collective-permute-done | bytes 16416 | tf_op jit(solution)/shard_map/ppermute | solution.py:63
  51.9 2.6 %shard_map.165 = (f32[8,64,128]{2,1,0:T(8,128)S(1)}, f32[8,8,128]{2,1,0:T(8,128)S(1)}, s32[4]{0:T(128)S(1)}) custom-call(f32[16,256]{1,0:T(8,128)S(1)} %shard_map.164.mine, f32[16,256]{1,0:T(8,128)S(1)} %collective-permute-done.6.twin), custom_call_target="tpu_custom_call" | custom-call | tf_op jit(solution)/shard_map/pallas_call | solution.py:156
  54.5 16.2 %collective-permute-done.7.refs_5_ = f32[5,2,104,128]{3,2,1,0:T(8,128)S(1)} collective-permute-done((f32[5,2,104,128]{3,2,1,0:T(8,128)S(1)}, f32[5,2,104,128]{3,2,1,0:T(8,128)S(1)}, u32[]{:S(2)}, u32[]{:S(2)}) %collective-permute-start.7) | collective-permute-done | bytes 532512 | tf_op jit(solution)/shard_map/ppermute | solution.py:437
  70.7 0.5 collective-permute-start.11
  71.2 1.4 %collective-permute-done.10.refs_6_ = f32[5,2,104,128]{3,2,1,0:T(8,128)S(1)} collective-permute-done((f32[5,2,104,128]{3,2,1,0:T(8,128)S(1)}, f32[5,2,104,128]{3,2,1,0:T(8,128)S(1)}, u32[]{:S(2)}, u32[]{:S(2)}) %collective-permute-start.10) | collective-permute-done | bytes 532512 | tf_op jit(solution)/shard_map/ppermute | solution.py:63
  72.6 0.8 collective-permute-done.11.refs_7_
  73.4 11.5 %shard_map.166 = (f32[2,48,128]{2,1,0:T(8,128)S(1)}, f32[2,48,128]{2,1,0:T(8,128)S(1)}, f32[2,48,128]{2,1,0:T(8,128)S(1)}, f32[2,48,128]{2,1,0:T(8,128)S(1)}) custom-call(s32[4]{0:T(128)S(1)} %get-tuple-element.26.scalars, f32[8,8,128]{2,1,0:T(8,128)S(1)} %get-tuple-element.27.source_ref, f32[8,64,128]{2,1,0:T(8,128)S(1)} %get-tuple-element.30.receiver_ref, ...), custom_call_target="tpu_custom_call" | custom-call | bytes 60000000 | tf_op jit(solution)/shard_map/pallas_call | solution.py:387
  84.9 1.2 %collective-permute-start.12 = (f32[2,48,128]{2,1,0:T(8,128)S(1)}, f32[2,48,128]{2,1,0:T(8,128)S(1)}, u32[]{:S(2)}, u32[]{:S(2)}) collective-permute-start(f32[2,48,128]{2,1,0:T(8,128)S(1)} %get-tuple-element.36), channel_id=1, source_target_pairs={{0,4},{4,8},{8,12},{12,0},{1,5},{5,9},{9,13},{13,1},{2,6},{6,10},{... | collective-permute-start | bytes 147464 | tf_op jit(solution)/shard_map/ppermute | solution.py:72
  86.1 2.0 %collective-permute-start.13 = (f32[2,48,128]{2,1,0:T(8,128)S(1)}, f32[2,48,128]{2,1,0:T(8,128)S(1)}, u32[]{:S(2)}, u32[]{:S(2)}) collective-permute-start(f32[2,48,128]{2,1,0:T(8,128)S(1)} %get-tuple-element.37), channel_id=1, source_target_pairs={{0,8},{4,12},{8,0},{12,4},{1,9},{5,13},{9,1},{13,5},{2,10},{6,14},... | collective-permute-start | bytes 147464 | tf_op jit(solution)/shard_map/ppermute | solution.py:72
  88.1 2.1 %collective-permute-start.14 = (f32[2,48,128]{2,1,0:T(8,128)S(1)}, f32[2,48,128]{2,1,0:T(8,128)S(1)}, u32[]{:S(2)}, u32[]{:S(2)}) collective-permute-start(f32[2,48,128]{2,1,0:T(8,128)S(1)} %get-tuple-element.38), channel_id=1, source_target_pairs={{0,12},{4,0},{8,4},{12,8},{1,13},{5,1},{9,5},{13,9},{2,14},{6,2},{... | collective-permute-start | bytes 147464 | tf_op jit(solution)/shard_map/ppermute | solution.py:72
  90.2 0.6 collective-permute-done.12.refs_1_
  90.8 2.1 %collective-permute-done.13.refs_2_ = f32[2,48,128]{2,1,0:T(8,128)S(1)} collective-permute-done((f32[2,48,128]{2,1,0:T(8,128)S(1)}, f32[2,48,128]{2,1,0:T(8,128)S(1)}, u32[]{:S(2)}, u32[]{:S(2)}) %collective-permute-start.13) | collective-permute-done | bytes 49184 | tf_op jit(solution)/shard_map/ppermute | solution.py:72
  92.9 0.7 shard_map.167
  93.6 0.5 collective-permute-start.15
  94.1 0.8 collective-permute-done.16
  94.9 1.8 %collective-permute-start.17 = (f32[2,96,128]{2,1,0:T(8,128)S(1)}, f32[2,96,128]{2,1,0:T(8,128)S(1)}, u32[]{:S(2)}, u32[]{:S(2)}) collective-permute-start(f32[2,96,128]{2,1,0:T(8,128)S(1)} %add.61), channel_id=1, source_target_pairs={{0,2},{1,3},{2,0},{3,1},{4,6},{5,7},{6,4},{7,5},{8,10},{9,11},{10,... | collective-permute-start | bytes 294920 | tf_op jit(solution)/shard_map/ppermute | solution.py:63
  96.7 3.1 %collective-permute-done.17 = f32[2,96,128]{2,1,0:T(8,128)S(1)} collective-permute-done((f32[2,96,128]{2,1,0:T(8,128)S(1)}, f32[2,96,128]{2,1,0:T(8,128)S(1)}, u32[]{:S(2)}, u32[]{:S(2)}) %collective-permute-start.17) | collective-permute-done | bytes 98336 | tf_op jit(solution)/shard_map/ppermute | solution.py:63
  99.9 0.7 add_multiply_fusion
  (37 shorter events, 1.2 us)
Async XLA Ops:
  0.0 6.6 %copy-start.7 = (f32[1,2,2,192,128]{4,3,2,1,0:T(8,128)S(1)}, f32[1,2,2,192,128]{4,3,2,1,0:T(8,128)}, u32[]{:S(2)}) copy-start(f32[1,2,2,192,128]{4,3,2,1,0:T(8,128)} %param.31) | copy-start | bytes 1179652
  0.0 6.6 %copy-start.6 = (f32[1,2,2,192,128]{4,3,2,1,0:T(8,128)S(1)}, f32[1,2,2,192,128]{4,3,2,1,0:T(8,128)}, u32[]{:S(2)}) copy-start(f32[1,2,2,192,128]{4,3,2,1,0:T(8,128)} %param.32) | copy-start | bytes 1179652
  2.2 10.1 %collective-permute-start.2 = (f32[5,2,96,128]{3,2,1,0:T(8,128)}, f32[5,2,96,128]{3,2,1,0:T(8,128)}, u32[]{:S(2)}, u32[]{:S(2)}) collective-permute-start(f32[5,2,96,128]{3,2,1,0:T(8,128)} %shard_map.163), channel_id=1, source_target_pairs={{0,1},{1,0},{2,3},{3,2},{4,5},{5,4},{6,7},{7,6},{8,9},{9,8},{10,11... | collective-permute-start | bytes 1474568 | tf_op jit(solution)/shard_map/ppermute | solution.py:63
  2.6 14.9 %collective-permute-start.3 = (f32[5,2,96,128]{3,2,1,0:T(8,128)}, f32[5,2,96,128]{3,2,1,0:T(8,128)}, u32[]{:S(2)}, u32[]{:S(2)}) collective-permute-start(f32[5,2,96,128]{3,2,1,0:T(8,128)} %shard_map.163), channel_id=1, source_target_pairs={{0,2},{1,3},{2,0},{3,1},{4,6},{5,7},{6,4},{7,5},{8,10},{9,11},{10,... | collective-permute-start | bytes 1474568 | tf_op jit(solution)/shard_map/ppermute | solution.py:63
  5.1 22.4 %collective-permute-start.4 = (f32[5,2,96,128]{3,2,1,0:T(8,128)}, f32[5,2,96,128]{3,2,1,0:T(8,128)S(1)}, u32[]{:S(2)}, u32[]{:S(2)}) collective-permute-start(f32[5,2,96,128]{3,2,1,0:T(8,128)} %shard_map.163), channel_id=1, source_target_pairs={{0,3},{1,2},{2,1},{3,0},{4,7},{5,6},{6,5},{7,4},{8,11},{9,10},{10,... | collective-permute-start | bytes 1474568 | tf_op jit(solution)/shard_map/ppermute | solution.py:63
  6.8 5.5 %copy-start.5 = (f32[5,2,96,128]{3,2,1,0:T(8,128)S(1)}, f32[5,2,96,128]{3,2,1,0:T(8,128)}, u32[]{:S(2)}) copy-start(f32[5,2,96,128]{3,2,1,0:T(8,128)} %shard_map.163) | copy-start | bytes 1474564
  6.8 24.9 %collective-permute-start.1 = (f32[8,2,104,128]{3,2,1,0:T(8,128)S(1)}, f32[8,2,104,128]{3,2,1,0:T(8,128)S(1)}, u32[]{:S(2)}, u32[]{:S(2)}) collective-permute-start(f32[8,2,104,128]{3,2,1,0:T(8,128)S(1)} %pad_maximum_fusion.1), channel_id=1, source_target_pairs={{0,4},{1,12},{2,6},{3,14},{4,5},{5,13},{6,7},{7,15},{8,0},{9,8},{1... | collective-permute-start | bytes 2555912 | tf_op jit(solution)/shard_map/ppermute | solution.py:437
  9.6 22.0 %collective-permute-start = (f32[8,2,104,128]{3,2,1,0:T(8,128)}, f32[8,2,104,128]{3,2,1,0:T(8,128)S(1)}, u32[]{:S(2)}, u32[]{:S(2)}) collective-permute-start(f32[8,2,104,128]{3,2,1,0:T(8,128)} %pad_maximum_fusion), channel_id=1, source_target_pairs={{0,0},{1,8},{2,2},{3,10},{4,1},{5,9},{6,3},{7,11},{8,4},{9,12},{10... | collective-permute-start | bytes 2555912 | tf_op jit(solution)/shard_map/ppermute | solution.py:437
  13.4 36.5 %copy-start = (f32[1,8,256]{2,1,0:T(8,128)S(1)}, f32[1,8,256]{2,1,0:T(8,128)}, u32[]{:S(2)}) copy-start(f32[1,8,256]{2,1,0:T(8,128)} %traces) | copy-start | bytes 24580
  13.4 36.5 %copy-start.1 = (s32[1,256]{1,0:T(1,128)S(1)}, s32[1,256]{1,0:T(1,128)}, u32[]{:S(2)}) copy-start(s32[1,256]{1,0:T(1,128)} %rec_x.1) | copy-start | bytes 3076
  13.4 36.5 %copy-start.2 = (s32[1,256]{1,0:T(1,128)S(1)}, s32[1,256]{1,0:T(1,128)}, u32[]{:S(2)}) copy-start(s32[1,256]{1,0:T(1,128)} %rec_y.1) | copy-start | bytes 3076
  13.4 36.5 %copy-start.3 = (f32[1,8]{1,0:T(1,128)S(1)}, f32[1,8]{1,0:T(1,128)}, u32[]{:S(2)}) copy-start(f32[1,8]{1,0:T(1,128)} %wavelet.1) | copy-start | bytes 100
  27.7 3.9 %collective-permute-start.5 = (f32[5,2,104,128]{3,2,1,0:T(8,128)S(1)}, f32[5,2,104,128]{3,2,1,0:T(8,128)S(1)}, u32[]{:S(2)}, u32[]{:S(2)}) collective-permute-start(f32[5,2,104,128]{3,2,1,0:T(8,128)S(1)} %get-tuple-element.44), channel_id=1, source_target_pairs={{0,0},{1,8},{2,2},{3,10},{4,1},{5,9},{6,3},{7,11},{8,4},{9,12},{10... | collective-permute-start | bytes 1597448 | tf_op jit(solution)/shard_map/ppermute | solution.py:437
  28.4 42.2 %collective-permute-start.7 = (f32[5,2,104,128]{3,2,1,0:T(8,128)S(1)}, f32[5,2,104,128]{3,2,1,0:T(8,128)S(1)}, u32[]{:S(2)}, u32[]{:S(2)}) collective-permute-start(f32[5,2,104,128]{3,2,1,0:T(8,128)S(1)} %get-tuple-element.43), channel_id=1, source_target_pairs={{0,4},{1,12},{2,6},{3,14},{4,5},{5,13},{6,7},{7,15},{8,0},{9,8},{1... | collective-permute-start | bytes 1597448 | tf_op jit(solution)/shard_map/ppermute | solution.py:437
  31.6 41.7 %collective-permute-start.8 = (f32[8,2,104,128]{3,2,1,0:T(8,128)S(1)}, f32[8,2,104,128]{3,2,1,0:T(8,128)S(1)}, u32[]{:S(2)}, u32[]{:S(2)}) collective-permute-start(f32[8,2,104,128]{3,2,1,0:T(8,128)S(1)} %collective-permute-done.refs_0_), channel_id=1, source_target_pairs={{0,1},{1,0},{2,3},{3,2},{4,5},{5,4},{6,7},{7,6},{8,9},{9,8},{10,11... | collective-permute-start | bytes 2555912 | tf_op jit(solution)/shard_map/ppermute | solution.py:63
  48.6 24.7 %collective-permute-start.9 = (f32[8,2,104,128]{3,2,1,0:T(8,128)S(1)}, f32[8,2,104,128]{3,2,1,0:T(8,128)S(1)}, u32[]{:S(2)}, u32[]{:S(2)}) collective-permute-start(f32[8,2,104,128]{3,2,1,0:T(8,128)S(1)} %collective-permute-done.1.refs_1_), channel_id=1, source_target_pairs={{0,1},{1,0},{2,3},{3,2},{4,5},{5,4},{6,7},{7,6},{8,9},{9,8},{10,11... | collective-permute-start | bytes 2555912 | tf_op jit(solution)/shard_map/ppermute | solution.py:63
  50.0 1.9 %collective-permute-start.6 = (f32[16,256]{1,0:T(8,128)S(1)}, f32[16,256]{1,0:T(8,128)S(1)}, u32[]{:S(2)}, u32[]{:S(2)}) collective-permute-start(f32[16,256]{1,0:T(8,128)S(1)} %shard_map.164.mine), channel_id=1, source_target_pairs={{0,1},{1,0},{2,3},{3,2},{4,5},{5,4},{6,7},{7,6},{8,9},{9,8},{10,11... | collective-permute-start | bytes 49160 | tf_op jit(solution)/shard_map/ppermute | solution.py:63
  70.7 1.9 %collective-permute-start.10 = (f32[5,2,104,128]{3,2,1,0:T(8,128)S(1)}, f32[5,2,104,128]{3,2,1,0:T(8,128)S(1)}, u32[]{:S(2)}, u32[]{:S(2)}) collective-permute-start(f32[5,2,104,128]{3,2,1,0:T(8,128)S(1)} %collective-permute-done.5.refs_4_), channel_id=1, source_target_pairs={{0,1},{1,0},{2,3},{3,2},{4,5},{5,4},{6,7},{7,6},{8,9},{9,8},{10,11... | collective-permute-start | bytes 1597448 | tf_op jit(solution)/shard_map/ppermute | solution.py:63
  70.7 2.7 %collective-permute-start.11 = (f32[5,2,104,128]{3,2,1,0:T(8,128)S(1)}, f32[5,2,104,128]{3,2,1,0:T(8,128)S(1)}, u32[]{:S(2)}, u32[]{:S(2)}) collective-permute-start(f32[5,2,104,128]{3,2,1,0:T(8,128)S(1)} %collective-permute-done.7.refs_5_), channel_id=1, source_target_pairs={{0,1},{1,0},{2,3},{3,2},{4,5},{5,4},{6,7},{7,6},{8,9},{9,8},{10,11... | collective-permute-start | bytes 1597448 | tf_op jit(solution)/shard_map/ppermute | solution.py:63
  73.4 19.5 %copy-start.4 = (s32[4]{0:T(128)S(1)}, s32[4]{0:T(128)}, u32[]{:S(2)}) copy-start(s32[4]{0:T(128)} %owners.1) | copy-start | bytes 52
  84.9 6.0 %collective-permute-start.12 = (f32[2,48,128]{2,1,0:T(8,128)S(1)}, f32[2,48,128]{2,1,0:T(8,128)S(1)}, u32[]{:S(2)}, u32[]{:S(2)}) collective-permute-start(f32[2,48,128]{2,1,0:T(8,128)S(1)} %get-tuple-element.36), channel_id=1, source_target_pairs={{0,4},{4,8},{8,12},{12,0},{1,5},{5,9},{9,13},{13,1},{2,6},{6,10},{... | collective-permute-start | bytes 147464 | tf_op jit(solution)/shard_map/ppermute | solution.py:72
  86.1 6.8 %collective-permute-start.13 = (f32[2,48,128]{2,1,0:T(8,128)S(1)}, f32[2,48,128]{2,1,0:T(8,128)S(1)}, u32[]{:S(2)}, u32[]{:S(2)}) collective-permute-start(f32[2,48,128]{2,1,0:T(8,128)S(1)} %get-tuple-element.37), channel_id=1, source_target_pairs={{0,8},{4,12},{8,0},{12,4},{1,9},{5,13},{9,1},{13,5},{2,10},{6,14},... | collective-permute-start | bytes 147464 | tf_op jit(solution)/shard_map/ppermute | solution.py:72
  88.1 4.8 %collective-permute-start.14 = (f32[2,48,128]{2,1,0:T(8,128)S(1)}, f32[2,48,128]{2,1,0:T(8,128)S(1)}, u32[]{:S(2)}, u32[]{:S(2)}) collective-permute-start(f32[2,48,128]{2,1,0:T(8,128)S(1)} %get-tuple-element.38), channel_id=1, source_target_pairs={{0,12},{4,0},{8,4},{12,8},{1,13},{5,1},{9,5},{13,9},{2,14},{6,2},{... | collective-permute-start | bytes 147464 | tf_op jit(solution)/shard_map/ppermute | solution.py:72
  93.6 1.4 %collective-permute-start.16 = (f32[2,96,128]{2,1,0:T(8,128)S(1)}, f32[2,96,128]{2,1,0:T(8,128)S(1)}, u32[]{:S(2)}, u32[]{:S(2)}) collective-permute-start(f32[2,96,128]{2,1,0:T(8,128)S(1)} %get-tuple-element.42), channel_id=1, source_target_pairs={{0,1},{1,0},{2,3},{3,2},{4,5},{5,4},{6,7},{7,6},{8,9},{9,8},{10,11... | collective-permute-start | bytes 294920 | tf_op jit(solution)/shard_map/ppermute | solution.py:63
  93.6 3.1 %collective-permute-start.15 = (f32[2,96,128]{2,1,0:T(8,128)S(1)}, f32[2,96,128]{2,1,0:T(8,128)S(1)}, u32[]{:S(2)}, u32[]{:S(2)}) collective-permute-start(f32[2,96,128]{2,1,0:T(8,128)S(1)} %get-tuple-element.40), channel_id=1, source_target_pairs={{0,1},{1,0},{2,3},{3,2},{4,5},{5,4},{6,7},{7,6},{8,9},{9,8},{10,11... | collective-permute-start | bytes 294920 | tf_op jit(solution)/shard_map/ppermute | solution.py:63
  94.9 4.9 %collective-permute-start.17 = (f32[2,96,128]{2,1,0:T(8,128)S(1)}, f32[2,96,128]{2,1,0:T(8,128)S(1)}, u32[]{:S(2)}, u32[]{:S(2)}) collective-permute-start(f32[2,96,128]{2,1,0:T(8,128)S(1)} %add.61), channel_id=1, source_target_pairs={{0,2},{1,3},{2,0},{3,1},{4,6},{5,7},{6,4},{7,5},{8,10},{9,11},{10,... | collective-permute-start | bytes 294920 | tf_op jit(solution)/shard_map/ppermute | solution.py:63
